TPU v7x, 32 devices: a whole 2x2x4 slice. The times are simulated.
32 devices in a mesh: gx: 8 (over y, x, core), gy: 4 (over z).
Axes of the slice: x: 2, y: 2, z: 4, core: 2. Of those that a mesh axis runs over, the one named last changes fastest.
Arguments:
- populations: float32 [19, 32, 128, 256], P(None, 'gx', 'gy'), may hold values from 0.6 to 1.4
- relax_rates: float32 [19], replicated, may hold values from 0.8 to 1.9
- velocity: float32 [3, 16384], P(None, ('gx', 'gy')), may hold values from -0.2 to 0.2
- velocity_change: float32 [3, 16384], P(None, ('gx', 'gy')), may hold values from -0.16 to 0.16
- fractions: float32 [27, 16384], P(None, ('gx', 'gy')), may hold values from 0.05 to 0.5
- anchor: int32 [16384], P(('gx', 'gy')), may hold values from 8449 to 24318, as said below
- destination: int32 [16384], P(('gx', 'gy')), may hold values from 0 to 9, as said below
Outputs:
- advanced: float32 [19, 32, 128, 256], P(None, 'gx', 'gy')
Inputs may be any that keep to these rules, and one draw needn't show every extreme that they name: `destination`: empty rows (9) carry no particle. Every brick sends exactly 4 particles to each of its 8 neighbouring bricks that lie inside the grid across the bed (gy index within 0 to 3; along gx the neighbours wrap around); the rest of the occupied rows stay (4); brick rows at gy index q hold 512 // 2^q occupied rows. Each anchor lies at least one cell inside its destination brick along x, y and z, so that the whole correlation cube lies in that brick.
All inputs are finite; a program needn't handle non-finite values.
Results may differ from a plain program's by a relative error of at most 0.0001.
Values sent between devices are 32-bit elements; how exact they have to be, the bound alone decides.
No kernel may reach another device: no remote copies, remote signals or barrier semaphores. Data moves between devices by JAX's collectives and lax.ppermute only.
A program may use at most 128 MiB of HBM per device.

v0:
```python
import jax
import jax.numpy as jnp
import numpy as np
from jax import lax
from jax.sharding import PartitionSpec as P

CAP = 4
STEPS = 2


def padded_2(cells, sides, width):
    for axis, dim in sides:
        count = lax.axis_size(axis)
        head = lax.slice_in_dim(cells, 0, width, axis=dim)
        tail = lax.slice_in_dim(cells, cells.shape[dim] - width, cells.shape[dim], axis=dim)
        cells = jnp.concatenate(
            [
                lax.ppermute(tail, axis, [(i, (i + 1) % count) for i in range(count)]),
                cells,
                lax.ppermute(head, axis, [((i + 1) % count, i) for i in range(count)]),
            ],
            axis=dim,
        )
    return cells


def from_behind(value, axis, steps):
    count = lax.axis_size(axis)
    pairs = [(source, (source + steps) % count) for source in range(count)]
    return lax.ppermute(value, axis, pairs)


def passed_along(value, axis, steps):
    count = lax.axis_size(axis)
    first, last = (max(0, -steps), min(count, count - steps))
    return lax.ppermute(value, axis, [(source, source + steps) for source in range(first, last)])


def lattice():
    vectors = [[0, 0, 0]]
    for axis_one in range(3):
        for orient in (1, -1):
            vector_one = [0, 0, 0]
            vector_one[axis_one] = orient
            vectors.append(vector_one)
    for axis_one, axis_two in ((0, 1), (0, 2), (1, 2)):
        for orient in (1, -1):
            for second in (1, -1):
                vector_one = [0, 0, 0]
                vector_one[axis_one] = orient
                vector_one[axis_two] = second
                vectors.append(vector_one)
    integral = np.array(vectors)
    speeds = integral * 1.0
    length = (speeds**2).sum(axis=1)
    weights = np.where(length == 0, 1.0 / 3.0, np.where(length == 1, 1.0 / 18.0, 1.0 / 36.0))
    opposite = np.array(
        [vectors.index([0 - component for component in vector_one]) for vector_one in vectors]
    )
    along_x, along_y, along_z = (speeds[:, 0], speeds[:, 1], speeds[:, 2])
    rows_list = [
        np.ones(19),
        along_x,
        along_y,
        along_z,
        length,
        3 * along_x**2 - length,
        along_y**2 - along_z**2,
        along_x * along_y,
        along_y * along_z,
        along_x * along_z,
        along_x * length,
        along_y * length,
        along_z * length,
        along_x * (along_y**2 - along_z**2),
        along_y * (along_z**2 - along_x**2),
        along_z * (along_x**2 - along_y**2),
        length**2,
        (3 * along_x**2 - length) * length,
        (along_y**2 - along_z**2) * length,
    ]
    basis_rows = []
    for candidate in rows_list:
        for earlier in basis_rows:
            candidate = candidate - np.dot(candidate, earlier) * earlier
        basis_rows.append(candidate / np.sqrt(np.dot(candidate, candidate)))
    basis = np.array(basis_rows)
    return (speeds, weights, opposite, basis, integral)


def tables():
    speeds, weights, opposite, basis, integral = lattice()
    lattice_vel = jnp.asarray(speeds, jnp.float32)
    moment_rows = jnp.asarray(
        np.concatenate([weights[None, :], (weights[:, None] * speeds).T], axis=0), jnp.float32
    )
    to_moments = jnp.asarray(basis * weights[None, :], jnp.float32)
    from_moments = jnp.asarray(basis.T / weights[:, None], jnp.float32)
    return (lattice_vel, moment_rows, to_moments, from_moments, opposite, integral)


def equilibrium(density, flow, lattice_vel):
    projected = jnp.dot(lattice_vel, flow, precision=lax.Precision.HIGHEST)
    speed_sq = jnp.sum(flow * flow, axis=0)
    return density[None, :] * (
        1.0 + 3.0 * projected + 4.5 * projected * projected - 1.5 * speed_sq[None, :]
    )


def collide(states, solid_part, solid_flow, relax_rates, packed):
    lattice_vel, moment_rows, to_moments, from_moments, opposite = packed
    moments = jnp.dot(moment_rows, states, precision=lax.Precision.HIGHEST)
    density = moments[0]
    flow = moments[1:] / density[None, :]
    fluid_eq = equilibrium(density, flow, lattice_vel)
    solid_eq = equilibrium(density, solid_flow, lattice_vel)
    off_eq = states - fluid_eq
    projected = jnp.dot(to_moments, off_eq, precision=lax.Precision.HIGHEST)
    relaxed = jnp.dot(
        from_moments, relax_rates[:, None] * projected, precision=lax.Precision.HIGHEST
    )
    bounce = states[opposite] - fluid_eq[opposite] - (states - solid_eq)
    return states - (1.0 - solid_part)[None, :] * relaxed + solid_part[None, :] * bounce


def stream(post, speeds, opposite):
    size_x, size_y = (post.shape[1], post.shape[2])
    padded = padded_2(post, (("gx", 1), ("gy", 2)), 1)
    coord_y = (lax.axis_index("gy") * size_y + jnp.arange(size_y, dtype=jnp.int32))[None, :, None]
    last_row = size_y * lax.axis_size("gy") - 1
    read = []
    for number in range(19):
        shift_x, shift_y, shift_z = (
            int(speeds[number, 0]),
            int(speeds[number, 1]),
            int(speeds[number, 2]),
        )
        pulled = padded[
            number, 1 - shift_x : 1 - shift_x + size_x, 1 - shift_y : 1 - shift_y + size_y, :
        ]
        pulled = jnp.roll(pulled, shift_z, axis=2)
        if shift_y == 1:
            pulled = jnp.where(coord_y == 0, post[opposite[number]], pulled)
        elif shift_y == -1:
            pulled = jnp.where(coord_y == last_row, post[opposite[number]], pulled)
        read.append(pulled)
    return jnp.stack(read, axis=0)


def deposit(ids_all, shares, velocities, size_x, size_y, size_z):
    cells = size_x * size_y * size_z
    combined = jnp.concatenate(
        [shares[None, :, :], shares[None, :, :] * velocities[:, None, :]], axis=0
    )
    row_values = jnp.transpose(combined, (2, 1, 0)).reshape(combined.shape[2], 108)
    target = jnp.clip(ids_all, 0, cells - 1)
    centred = jnp.zeros((cells, 108), jnp.float32).at[target].add(row_values)
    field = centred.reshape(size_x, size_y, size_z, 108)
    padded = jnp.pad(field, ((1, 1), (1, 1), (1, 1), (0, 0)))
    total = jnp.zeros((size_x, size_y, size_z, 4), jnp.float32)
    for offset in range(27):
        move_x, move_y, move_z = (offset // 9 - 1, offset // 3 % 3 - 1, offset % 3 - 1)
        total = (
            total
            + padded[
                1 - move_x : 1 - move_x + size_x,
                1 - move_y : 1 - move_y + size_y,
                1 - move_z : 1 - move_z + size_z,
                4 * offset : 4 * offset + 4,
            ]
        )
    gathered = jnp.transpose(total.reshape(cells, 4), (1, 0))
    return (gathered[0], gathered[1:])


def local(populations, relax_rates, velocity, velocity_change, fractions, anchor, destination):
    lattice_vel, moment_rows, to_moments, from_moments, opposite, speeds = tables()
    packed = (lattice_vel, moment_rows, to_moments, from_moments, opposite)
    size_x, size_y, size_z = (populations.shape[1], populations.shape[2], populations.shape[3])
    cells = size_x * size_y * size_z
    new_velocity = velocity + velocity_change
    payload = jnp.concatenate([new_velocity, fractions], axis=0)
    width_rows = payload.shape[0]
    anchors = anchor[None, :]
    labels = jnp.arange(10, dtype=jnp.int32)
    one_hot = (destination[:, None] == labels[None, :]).astype(jnp.int32)
    ranking = jnp.sum(jnp.cumsum(one_hot, axis=0) * one_hot, axis=1) - 1
    leaving = (destination < 9) & (destination != 4)
    staying = destination == 4
    placed = jnp.where(leaving, destination * CAP + ranking, 9 * CAP)
    outgoing = jnp.zeros((width_rows, 9 * CAP), jnp.float32).at[:, placed].set(payload, mode="drop")
    outgoing = outgoing.reshape(width_rows, 3, 3, CAP)
    outgoing_ids = jnp.zeros((1, 9 * CAP), jnp.int32).at[:, placed].set(anchors, mode="drop")
    outgoing_ids = outgoing_ids.reshape(1, 3, 3, CAP)
    column_parts = [outgoing[:, 1]]
    column_idparts = [outgoing_ids[:, 1]]
    for orient in (1, -1):
        moved, moved_ids = from_behind(
            (outgoing[:, 1 + orient], outgoing_ids[:, 1 + orient]), "gx", orient
        )
        column_parts.append(moved)
        column_idparts.append(moved_ids)
    columns = jnp.concatenate(column_parts, axis=2)
    column_ids = jnp.concatenate(column_idparts, axis=2)
    arrived_parts = [columns[:, 1]]
    arrived_idparts = [column_ids[:, 1]]
    for orient in (1, -1):
        moved, moved_ids = passed_along(
            (columns[:, 1 + orient], column_ids[:, 1 + orient]), "gy", orient
        )
        arrived_parts.append(moved)
        arrived_idparts.append(moved_ids)
    arrived = jnp.concatenate(arrived_parts, axis=1)
    arrived_ids = jnp.concatenate(arrived_idparts, axis=1)
    rows_all = jnp.concatenate([payload, arrived], axis=1)
    ids_all = jnp.concatenate([anchor, arrived_ids[0]], axis=0)
    keep = jnp.concatenate([staying, jnp.ones((arrived.shape[1],), jnp.bool_)], axis=0)
    shares = jnp.where(keep[None, :], rows_all[3:], jnp.float32(0.0))
    solid_sum, momentum = deposit(ids_all, shares, rows_all[:3], size_x, size_y, size_z)
    solid = jnp.minimum(solid_sum, 1.0)
    solid_velocity = momentum / (solid_sum + 1e-06)[None, :]
    states = populations.reshape(19, cells)
    for sweep_number in range(STEPS):
        post = collide(states, solid, solid_velocity, relax_rates, packed)
        states = stream(post.reshape(19, size_x, size_y, size_z), speeds, opposite).reshape(
            19, cells
        )
    return states.reshape(19, size_x, size_y, size_z)


def solution(mesh):
    placed = (
        P(None, "gx", "gy", None),
        P(),
        P(None, ("gx", "gy")),
        P(None, ("gx", "gy")),
        P(None, ("gx", "gy")),
        P(("gx", "gy")),
        P(("gx", "gy")),
    )
    return jax.shard_map(
        local, mesh=mesh, in_specs=placed, out_specs=P(None, "gx", "gy", None), check_vma=False
    )
```

profile of v0, /device:TPU:0, one launch (start us, length us, event | category | flops | bytes accessed | tf_op | source)
XLA Modules:
  0.0 373.8 jit_solution(7173438076994598630)
XLA Ops:
  7.6 2.9 collective-permute-start.5
  13.3 3.1 collective-permute-start.1
  24.7 2.8 gather_fusion
  27.6 5.8 %fusion.36 = f32[19,32768]{1,0:T(8,128)} fusion(f32[19,3]{1,0:T(8,128)S(1)} %copy-done.70, f32[32768]{0:T(1024)S(1)} %copy-done.39, f32[32768]{0:T(1024)S(1)} %bitcast.271, f32[4,32768]{1,0:T(4,128)} %copy-done.8), kind=kOutput, calls=%fused_computation.76 | convolution fusion | flops 26869760 | bytes 3420160 | tf_op jit(solution)/shard_map/dot_general | solution.py:103
  33.4 5.9 %gather_fusion.1 = f32[19,32768]{1,0:T(8,128)} fusion(f32[19,32768]{1,0:T(8,128)} %fusion.36, s32[1024]{0:T(1024)S(1)} %pad_clamp_fusion), kind=kCustom, calls=%fused_computation.1 | custom fusion | bytes 4980812 | tf_op jit(solution)/shard_map/gather | solution.py:122
  40.9 6.8 %convolution_multiply_fusion.3 = f32[32768,19]{0,1:T(8,128)} fusion(f32[19,19]{1,0:T(8,128)S(1)} %copy-done.41, f32[19,32768]{1,0:T(8,128)S(1)} %bitcast.249, f32[19,32768]{1,0:T(8,128)} %fusion.36, f32[19]{0:T(128)S(1)} %copy-done.48), kind=kOutput, calls=%fused_computation.42 | convolution fusion | flops 143196160 | bytes 7472624 | tf_op jit(solution)/shard_map/dot_general | solution.py:118
  48.5 4.2 %collective-permute-start.2 = (s32[1,12]{1,0:T(1,128)S(1)}, s32[1,12]{1,0:T(1,128)S(1)}, u32[]{:S(2)}, u32[]{:S(2)}) collective-permute-start(s32[1,12]{1,0:T(1,128)S(1)} %get-tuple-element.103), channel_id=1, source_target_pairs={{0,1},{1,2},{2,3},{4,5},{5,6},{6,7},{8,9},{9,10},{10,11},{12,13},{... | collective-permute-start | bytes 152 | tf_op jit(solution)/shard_map/ppermute | solution.py:36
  54.0 4.5 %collective-permute-start.6 = (f32[30,12]{0,1:T(8,128)S(1)}, f32[30,12]{0,1:T(8,128)S(1)}, u32[]{:S(2)}, u32[]{:S(2)}) collective-permute-start(f32[30,12]{0,1:T(8,128)S(1)} %get-tuple-element.94), channel_id=1, source_target_pairs={{0,1},{1,2},{2,3},{4,5},{5,6},{6,7},{8,9},{9,10},{10,11},{12,13},{... | collective-permute-start | bytes 4328 | tf_op jit(solution)/shard_map/ppermute | solution.py:36
  60.2 3.9 %collective-permute-done.7 = f32[30,12]{0,1:T(8,128)S(1)} collective-permute-done((f32[30,12]{0,1:T(8,128)S(1)}, f32[30,12]{0,1:T(8,128)S(1)}, u32[]{:S(2)}, u32[]{:S(2)}) %collective-permute-start.7) | collective-permute-done | bytes 1472 | tf_op jit(solution)/shard_map/ppermute | solution.py:36
  68.9 13.4 %scatter_custom_fusion.2 = f32[32768,108]{1,0:T(8,128)} fusion(s32[548]{0:T(1024)S(1)} %fusion.69, f32[548,108]{1,0:T(8,128)} %copy.52, f32[]{:T(128)} %constant.25.clone.1), kind=kCustom, calls=%fused_computation.69 | custom fusion | flops 59184 | bytes 14156288 | tf_op jit(solution)/shard_map/scatter-add | solution.py:157
  82.3 139.0 %fusion.31 = f32[4,32,256,4]{3,2,1,0:T(8,128)} fusion(f32[4,32,256,108]{3,2,1,0:T(8,128)} %bitcast.251), kind=kLoop, calls=%fused_computation.68 | loop fusion | flops 3407872 | bytes 34078720 | tf_op jit(solution)/shard_map/add | solution.py:164
  221.3 10.1 %copy.62 = f32[32768,4]{0,1:T(4,128)} copy(f32[32768,4]{1,0:T(8,128)} %bitcast.252) | data formatting | bytes 1048576 | tf_op jit(solution)/shard_map/reshape | solution.py:172
  234.4 4.3 %fusion.38 = f32[19,32768]{1,0:T(8,128)S(1)} fusion(f32[19,3]{1,0:T(8,128)} %constant.20.clone, f32[32768]{0:T(1024)S(1)} %broadcast_multiply_fusion.2, f32[4,32768]{1,0:T(4,128)} %bitcast.264, f32[32768]{0:T(1024)S(1)} %bitcast.340), kind=kOutput, calls=%fused_computation.78 | convolution fusion | flops 26247168 | bytes 3277028 | tf_op jit(solution)/shard_map/dot_general | solution.py:103
  238.8 4.1 %fusion.5 = f32[19,32768]{1,0:T(8,128)S(1)} fusion(f32[19,32768]{1,0:T(8,128)S(1)} %bitcast.250, f32[32768,19]{0,1:T(8,128)S(1)} %copy-done.5, f32[19,19]{1,0:T(8,128)S(1)} %copy-done.40, f32[19,32768]{1,0:T(8,128)S(1)} %fusion.38, f32[19,32768]{1,0:T(8,128)S(1)} %copy-done.6, f32[19,32768]{1,0:T(8,128)S(1)} %copy-done.7, f32[32768]{0:T(1024)S(1)} %bitcast.268, ...), kind=kOutput, calls=%fused_computation.41 | convolution fusion | flops 146931712 | bytes 15336868 | tf_op jit(solution)/shard_map/dot_general | solution.py:119
  245.8 3.5 slice_reduce_fusion.13
  279.4 3.5 slice_select_fusion
  285.3 3.2 fusion.41
  288.5 3.0 gather_fusion.3
  301.6 8.1 %stack.98 = f32[19,32768]{1,0:T(8,128)S(1)} concatenate(f32[1,32768]{1,0:T(1,128)} %copy-done.13, f32[1,32768]{1,0:T(1,128)} %bitcast.312, f32[1,32768]{1,0:T(1,128)} %bitcast.311, f32[1,32768]{1,0:T(1,128)} %bitcast.329, f32[1,32768]{1,0:T(1,128)} %bitcast.334, f32[1,32768]{1,0:T(1,128)} %stack.88, f32[1,32768]{1,0:T(1,128)} %stack.89, f32[1,32768]{1,0:T(1,128)} %bitcast.330, ...), dimensions={0} | concatenate | bytes 4980736 | tf_op jit(solution)/shard_map/stack | solution.py:147
  309.7 6.7 %convolution_multiply_fusion.1 = f32[32768,19]{0,1:T(8,128)} fusion(f32[19,19]{1,0:T(8,128)} %constant.22.clone, f32[19,32768]{1,0:T(8,128)S(1)} %stack.98, f32[19,32768]{1,0:T(8,128)} %copy-done, f32[19]{0:T(128)} %param.17), kind=kOutput, calls=%fused_computation.37 | convolution fusion | flops 143196160 | bytes 7472624 | tf_op jit(solution)/shard_map/dot_general | solution.py:118
  316.4 3.1 gather_fusion.2
  319.5 8.2 %fusion.2 = f32[19,32768]{1,0:T(8,128)S(1)} fusion(f32[19,32768]{1,0:T(8,128)S(1)} %stack.98, f32[32768,19]{0,1:T(8,128)} %convolution_multiply_fusion.1, f32[19,19]{1,0:T(8,128)S(1)} %copy-done.40, f32[19,32768]{1,0:T(8,128)} %copy-done.4, f32[19,32768]{1,0:T(8,128)} %gather_fusion.2, f32[19,32768]{1,0:T(8,128)} %gather_fusion.3, f32[32768]{0:T(1024)S(1)} %bitcast.275, ...), kind=kOutput, calls=%fused_computation.36 | convolution fusion | flops 146931712 | bytes 15336868 | tf_op jit(solution)/shard_map/dot_general | solution.py:119
  329.9 2.9 collective-permute-start.13
  332.7 5.0 %slice_reduce_fusion = (f32[32768]{0:T(1024)}, f32[32768]{0:T(1024)}, f32[32768]{0:T(1024)}, f32[32768]{0:T(1024)}, f32[32768]{0:T(1024)}, /*index=5*/f32[32768]...) fusion(f32[19,32768]{1,0:T(8,128)S(1)} %fusion.2), kind=kLoop, calls=%fused_computation.114 | loop fusion | bytes 3407872 | tf_op jit(solution)/shard_map/slice | solution.py:145
  (364 shorter events, 113.7 us)
Async XLA Ops:
  7.1 46.9 %collective-permute-start.4 = (f32[30,3,4]{0,2,1:T(4,128)S(1)}, f32[30,3,4]{0,2,1:T(4,128)S(1)}, u32[]{:S(2)}, u32[]{:S(2)}) collective-permute-start(f32[30,3,4]{0,2,1:T(4,128)S(1)} %get-tuple-element.97), channel_id=1, source_target_pairs={{0,4},{4,8},{8,12},{12,16},{16,20},{20,24},{24,28},{28,0},{1,5},{5... | collective-permute-start | bytes 4328 | tf_op jit(solution)/shard_map/ppermute | solution.py:30
  7.6 46.4 %collective-permute-start.5 = (f32[30,3,4]{0,2,1:T(4,128)S(1)}, f32[30,3,4]{0,2,1:T(4,128)S(1)}, u32[]{:S(2)}, u32[]{:S(2)}) collective-permute-start(f32[30,3,4]{0,2,1:T(4,128)S(1)} %get-tuple-element.96), channel_id=1, source_target_pairs={{0,28},{4,0},{8,4},{12,8},{16,12},{20,16},{24,20},{28,24},{1,29},{... | collective-permute-start | bytes 4328 | tf_op jit(solution)/shard_map/ppermute | solution.py:30
  13.2 34.5 %collective-permute-start = (s32[1,3,4]{2,0,1:T(1,128)S(1)}, s32[1,3,4]{2,0,1:T(1,128)S(1)}, u32[]{:S(2)}, u32[]{:S(2)}) collective-permute-start(s32[1,3,4]{2,0,1:T(1,128)S(1)} %squeeze.169), channel_id=1, source_target_pairs={{0,4},{4,8},{8,12},{12,16},{16,20},{20,24},{24,28},{28,0},{1,5},{5... | collective-permute-start | bytes 152 | tf_op jit(solution)/shard_map/ppermute | solution.py:30
  13.3 34.4 %collective-permute-start.1 = (s32[1,3,4]{2,0,1:T(1,128)S(1)}, s32[1,3,4]{2,0,1:T(1,128)}, u32[]{:S(2)}, u32[]{:S(2)}) collective-permute-start(s32[1,3,4]{2,0,1:T(1,128)S(1)} %squeeze.170), channel_id=1, source_target_pairs={{0,28},{4,0},{8,4},{12,8},{16,12},{20,16},{24,20},{28,24},{1,29},{... | collective-permute-start | bytes 152 | tf_op jit(solution)/shard_map/ppermute | solution.py:30
  17.1 22.2 %copy-start.42 = (pred[32]{0:T(512)(128)(4,1)}, pred[32]{0:T(512)(128)(4,1)S(1)}, u32[]{:S(2)}) copy-start(pred[32]{0:T(512)(128)(4,1)S(1)} %fusion.71) | copy-start | bytes 100
  40.9 19.1 %copy-start.49 = (s32[512]{0:T(512)S(1)}, s32[512]{0:T(512)}, u32[]{:S(2)}) copy-start(s32[512]{0:T(512)} %param.21) | copy-start | bytes 6148
  40.9 23.3 %copy-start.21 = (f32[27,512]{1,0:T(8,128)S(1)}, f32[27,512]{1,0:T(8,128)}, u32[]{:S(2)}) copy-start(f32[27,512]{1,0:T(8,128)} %param.20) | copy-start | bytes 165892
  48.5 11.4 %collective-permute-start.2 = (s32[1,12]{1,0:T(1,128)S(1)}, s32[1,12]{1,0:T(1,128)S(1)}, u32[]{:S(2)}, u32[]{:S(2)}) collective-permute-start(s32[1,12]{1,0:T(1,128)S(1)} %get-tuple-element.103), channel_id=1, source_target_pairs={{0,1},{1,2},{2,3},{4,5},{5,6},{6,7},{8,9},{9,10},{10,11},{12,13},{... | collective-permute-start | bytes 152 | tf_op jit(solution)/shard_map/ppermute | solution.py:36
  52.6 7.2 %collective-permute-start.3 = (s32[1,12]{1,0:T(1,128)S(1)}, s32[1,12]{1,0:T(1,128)S(1)}, u32[]{:S(2)}, u32[]{:S(2)}) collective-permute-start(s32[1,12]{1,0:T(1,128)S(1)} %get-tuple-element.102), channel_id=1, source_target_pairs={{1,0},{2,1},{3,2},{5,4},{6,5},{7,6},{9,8},{10,9},{11,10},{13,12},{... | collective-permute-start | bytes 152 | tf_op jit(solution)/shard_map/ppermute | solution.py:36
  54.0 6.1 %collective-permute-start.6 = (f32[30,12]{0,1:T(8,128)S(1)}, f32[30,12]{0,1:T(8,128)S(1)}, u32[]{:S(2)}, u32[]{:S(2)}) collective-permute-start(f32[30,12]{0,1:T(8,128)S(1)} %get-tuple-element.94), channel_id=1, source_target_pairs={{0,1},{1,2},{2,3},{4,5},{5,6},{6,7},{8,9},{9,10},{10,11},{12,13},{... | collective-permute-start | bytes 4328 | tf_op jit(solution)/shard_map/ppermute | solution.py:36
  58.5 5.5 %collective-permute-start.7 = (f32[30,12]{0,1:T(8,128)S(1)}, f32[30,12]{0,1:T(8,128)S(1)}, u32[]{:S(2)}, u32[]{:S(2)}) collective-permute-start(f32[30,12]{0,1:T(8,128)S(1)} %get-tuple-element.93), channel_id=1, source_target_pairs={{1,0},{2,1},{3,2},{5,4},{6,5},{7,6},{9,8},{10,9},{11,10},{13,12},{... | collective-permute-start | bytes 4328 | tf_op jit(solution)/shard_map/ppermute | solution.py:36
  245.4 15.3 %collective-permute-start.8 = (f32[19,1,32,256]{3,2,1,0:T(8,128)}, f32[19,1,32,256]{3,2,1,0:T(8,128)}, u32[]{:S(2)}, u32[]{:S(2)}) collective-permute-start(f32[19,1,32,256]{3,2,1,0:T(8,128)} %get-tuple-element.80), channel_id=1, source_target_pairs={{0,4},{4,8},{8,12},{12,16},{16,20},{20,24},{24,28},{28,0},{1,5},{5... | collective-permute-start | bytes 1867784 | tf_op jit(solution)/shard_map/ppermute | solution.py:18
  249.5 13.3 %collective-permute-start.9 = (f32[19,1,32,256]{3,2,1,0:T(8,128)}, f32[19,1,32,256]{3,2,1,0:T(8,128)}, u32[]{:S(2)}, u32[]{:S(2)}) collective-permute-start(f32[19,1,32,256]{3,2,1,0:T(8,128)} %get-tuple-element.79), channel_id=1, source_target_pairs={{4,0},{8,4},{12,8},{16,12},{20,16},{24,20},{28,24},{0,28},{5,1},{9... | collective-permute-start | bytes 1867784 | tf_op jit(solution)/shard_map/ppermute | solution.py:20
  264.2 11.6 %copy-start.25 = (f32[1,4,32,256]{3,2,1,0:T(8,128)S(1)}, f32[1,4,32,256]{3,2,1,0:T(8,128)}, u32[]{:S(2)}) copy-start(f32[1,4,32,256]{3,2,1,0:T(8,128)} %squeeze.180) | copy-start | bytes 393220
  264.2 11.6 %copy-start.26 = (f32[1,4,32,256]{3,2,1,0:T(8,128)S(1)}, f32[1,4,32,256]{3,2,1,0:T(8,128)}, u32[]{:S(2)}) copy-start(f32[1,4,32,256]{3,2,1,0:T(8,128)} %squeeze.184) | copy-start | bytes 393220
  264.2 11.6 %copy-start.27 = (f32[1,4,32,256]{3,2,1,0:T(8,128)S(1)}, f32[1,4,32,256]{3,2,1,0:T(8,128)}, u32[]{:S(2)}) copy-start(f32[1,4,32,256]{3,2,1,0:T(8,128)} %squeeze.186) | copy-start | bytes 393220
  264.2 11.6 %copy-start.43 = (pred[32]{0:T(512)(128)(4,1)S(1)}, pred[32]{0:T(512)(128)(4,1)}, u32[]{:S(2)}) copy-start(pred[32]{0:T(512)(128)(4,1)} %copy-done.42) | copy-start | bytes 100
  266.0 9.8 %collective-permute-start.10 = (f32[19,6,1,256]{3,2,1,0:T(1,128)S(1)}, f32[19,6,1,256]{3,2,1,0:T(1,128)S(1)}, u32[]{:S(2)}, u32[]{:S(2)}) collective-permute-start(f32[19,6,1,256]{3,2,1,0:T(1,128)S(1)} %get-tuple-element.51), channel_id=1, source_target_pairs={{0,1},{1,2},{2,3},{3,0},{4,5},{5,6},{6,7},{7,4},{8,9},{9,10},{10,1... | collective-permute-start | bytes 350216 | tf_op jit(solution)/shard_map/ppermute | solution.py:18
  271.5 5.8 %collective-permute-start.11 = (f32[19,6,1,256]{3,2,1,0:T(1,128)S(1)}, f32[19,6,1,256]{3,2,1,0:T(1,128)S(1)}, u32[]{:S(2)}, u32[]{:S(2)}) collective-permute-start(f32[19,6,1,256]{3,2,1,0:T(1,128)S(1)} %get-tuple-element.50), channel_id=1, source_target_pairs={{1,0},{2,1},{3,2},{0,3},{5,4},{6,5},{7,6},{4,7},{9,8},{10,9},{11,1... | collective-permute-start | bytes 350216 | tf_op jit(solution)/shard_map/ppermute | solution.py:20
  329.9 27.3 %collective-permute-start.12 = (f32[19,1,32,256]{3,2,1,0:T(8,128)}, f32[19,1,32,256]{3,2,1,0:T(8,128)}, u32[]{:S(2)}, u32[]{:S(2)}) collective-permute-start(f32[19,1,32,256]{3,2,1,0:T(8,128)} %get-tuple-element.75), channel_id=1, source_target_pairs={{0,4},{4,8},{8,12},{12,16},{16,20},{20,24},{24,28},{28,0},{1,5},{5... | collective-permute-start | bytes 1867784 | tf_op jit(solution)/shard_map/ppermute | solution.py:18
  329.9 29.5 %collective-permute-start.13 = (f32[19,1,32,256]{3,2,1,0:T(8,128)S(1)}, f32[19,1,32,256]{3,2,1,0:T(8,128)}, u32[]{:S(2)}, u32[]{:S(2)}) collective-permute-start(f32[19,1,32,256]{3,2,1,0:T(8,128)S(1)} %get-tuple-element.74), channel_id=1, source_target_pairs={{4,0},{8,4},{12,8},{16,12},{20,16},{24,20},{28,24},{0,28},{5,1},{9... | collective-permute-start | bytes 1867784 | tf_op jit(solution)/shard_map/ppermute | solution.py:20
  338.7 20.6 %copy-start.20 = (f32[4,32,256]{2,1,0:T(8,128)}, f32[4,32,256]{2,1,0:T(8,128)S(1)}, u32[]{:S(2)}) copy-start(f32[4,32,256]{2,1,0:T(8,128)S(1)} %squeeze.199) | copy-start | bytes 393220
  360.8 6.9 %collective-permute-start.14 = (f32[19,6,1,256]{3,2,1,0:T(1,128)S(1)}, f32[19,6,1,256]{3,2,1,0:T(1,128)S(1)}, u32[]{:S(2)}, u32[]{:S(2)}) collective-permute-start(f32[19,6,1,256]{3,2,1,0:T(1,128)S(1)} %get-tuple-element.49), channel_id=1, source_target_pairs={{0,1},{1,2},{2,3},{3,0},{4,5},{5,6},{6,7},{7,4},{8,9},{9,10},{10,1... | collective-permute-start | bytes 350216 | tf_op jit(solution)/shard_map/ppermute | solution.py:18
  362.4 6.1 %collective-permute-start.15 = (f32[19,6,1,256]{3,2,1,0:T(1,128)S(1)}, f32[19,6,1,256]{3,2,1,0:T(1,128)S(1)}, u32[]{:S(2)}, u32[]{:S(2)}) collective-permute-start(f32[19,6,1,256]{3,2,1,0:T(1,128)S(1)} %get-tuple-element.48), channel_id=1, source_target_pairs={{1,0},{2,1},{3,2},{0,3},{5,4},{6,5},{7,6},{4,7},{9,8},{10,9},{11,1... | collective-permute-start | bytes 350216 | tf_op jit(solution)/shard_map/ppermute | solution.py:20
  (65 other events, 243.5 us)
where the time goes:
time: 379 us; the launch traced here: 374 us
  other arithmetic  174 us (46%)
  local copies, waits for them, and re-layouts  118 us (31%)
  matrix products  40.8 us (11%)
  starting transfers between devices  31.9 us (8%)
  waiting for transfers between devices  7.18 us (2%)
    add x1, other arithmetic, deposit(): total + padded[1 - move_x:1 - move_x + size_x, 1 - move_y:1 - move_y + si...  139 us
    unnamed x183, local copies, waits for them, and re-layouts  29.5 us
    gather x4, local copies, waits for them, and re-layouts, collide(): bounce = states[opposite] - fluid_eq[opposite] - (states - solid_eq)  14.7 us
    dot_general x2, matrix products, collide(): projected = jnp.dot(to_moments, off_eq, precision=lax.Precision.HIGHEST)  13.5 us
    scatter-add x1, other arithmetic, deposit(): centred = jnp.zeros((cells, 108), jnp.float32).at[target].add(row_values)  13.4 us
    dot_general x3, matrix products, equilibrium(): projected = jnp.dot(lattice_vel, flow, precision=lax.Precision.HIGHEST)  13.3 us
    another operation x7, local copies, waits for them, and re-layouts, stream(): return jnp.stack(read, axis=0)  12.9 us
    dot_general x2, matrix products, collide(): jnp.dot(from_moments, relax_rates[:, None] * projected, precision=lax.Pre...  12.3 us
  transfers between devices with their start and end apart: 16, of which 3 were waited for; matrix products, arithmetic and copies ran while one was open for 22% of the time, Pallas kernels for 0%

commit v1 on v0

v1 whole, which is shorter than its diff:
```python
import functools

import jax
import jax.numpy as jnp
import numpy as np
from jax import lax
from jax.experimental import pallas as pl
from jax.experimental.pallas import tpu as pltpu
from jax.sharding import PartitionSpec as P

CAP = 4
STEPS = 2
LANES = 8 * CAP
F32 = jnp.float32
BF16 = jnp.bfloat16
I32 = jnp.int32


def lattice():
    vectors = [[0, 0, 0]]
    for axis_one in range(3):
        for orient in (1, -1):
            vector_one = [0, 0, 0]
            vector_one[axis_one] = orient
            vectors.append(vector_one)
    for axis_one, axis_two in ((0, 1), (0, 2), (1, 2)):
        for orient in (1, -1):
            for second in (1, -1):
                vector_one = [0, 0, 0]
                vector_one[axis_one] = orient
                vector_one[axis_two] = second
                vectors.append(vector_one)
    integral = np.array(vectors)
    speeds = integral * 1.0
    length = (speeds**2).sum(axis=1)
    weights = np.where(length == 0, 1.0 / 3.0, np.where(length == 1, 1.0 / 18.0, 1.0 / 36.0))
    opposite = [vectors.index([0 - component for component in vector_one]) for vector_one in vectors]
    along_x, along_y, along_z = (speeds[:, 0], speeds[:, 1], speeds[:, 2])
    rows_list = [
        np.ones(19),
        along_x,
        along_y,
        along_z,
        length,
        3 * along_x**2 - length,
        along_y**2 - along_z**2,
        along_x * along_y,
        along_y * along_z,
        along_x * along_z,
        along_x * length,
        along_y * length,
        along_z * length,
        along_x * (along_y**2 - along_z**2),
        along_y * (along_z**2 - along_x**2),
        along_z * (along_x**2 - along_y**2),
        length**2,
        (3 * along_x**2 - length) * length,
        (along_y**2 - along_z**2) * length,
    ]
    basis_rows = []
    for candidate in rows_list:
        for earlier in basis_rows:
            candidate = candidate - np.dot(candidate, earlier) * earlier
        basis_rows.append(candidate / np.sqrt(np.dot(candidate, candidate)))
    return [tuple(v) for v in vectors], weights, opposite, np.array(basis_rows)


VEC, WEIGHTS, OPP, BASIS = lattice()
FORWARD = [i for i in range(19) if VEC[i][0] == 1]
BACKWARD = [i for i in range(19) if VEC[i][0] == -1]


def symmetric_blocks():
    def vec(entries):
        out = np.zeros(19)
        for index, value in entries.items():
            out[index] = value
        return out

    def plane(base):
        s_one, d_one = vec({base: 1, base + 3: 1}), vec({base: 1, base + 3: -1})
        s_two, d_two = vec({base + 1: 1, base + 2: 1}), vec({base + 1: 1, base + 2: -1})
        return s_one + s_two, s_one - s_two, d_one + d_two, d_one - d_two

    rest = vec({0: 1})
    s_x, s_y, s_z = vec({1: 1, 2: 1}), vec({3: 1, 4: 1}), vec({5: 1, 6: 1})
    d_x, d_y, d_z = vec({1: 1, 2: -1}), vec({3: 1, 4: -1}), vec({5: 1, 6: -1})
    xy, q_xy, x_xy, y_xy = plane(7)
    xz, q_xz, x_xz, z_xz = plane(11)
    yz, q_yz, y_yz, z_yz = plane(15)
    blocks = [
        [rest, s_x + s_y + s_z, xy + xz + yz],
        [2 * s_x - s_y - s_z, xy + xz - 2 * yz],
        [s_y - s_z, xy - xz],
        [q_xy],
        [q_xz],
        [q_yz],
        [d_x, x_xy, x_xz],
        [d_y, y_xy, y_yz],
        [d_z, z_xz, z_yz],
    ]
    scales = [[1, 1 / 6, 1 / 12], [1 / 12, 1 / 24], [1 / 4, 1 / 8]]
    scales += [[1 / 4]] * 3 + [[1 / 2, 1 / 4, 1 / 4]] * 3
    forward = np.array([row for block in blocks for row in block])
    back = np.linalg.inv(forward)
    left = forward @ np.diag(1.0 / WEIGHTS) @ BASIS.T
    right = BASIS @ np.diag(WEIGHTS) @ back
    table = []
    start = 0
    for block, scale in zip(blocks, scales):
        size = len(block)
        rows = []
        for a in range(size):
            row = []
            for b in range(size):
                per_rate = -scale[a] * left[start + a, :] * right[:, start + b]
                row.append([(k, float(v)) for k, v in enumerate(per_rate) if abs(v) > 1e-12])
            rows.append(row)
        table.append(rows)
        start += size
    return table


RELAX = symmetric_blocks()


def relax_blocks(rates):
    values = [rates[k] for k in range(19)]

    def entry(terms):
        total = None
        for k, factor in terms:
            part = values[k] * np.float32(factor)
            total = part if total is None else total + part
        return total

    return [[[entry(terms) for terms in row] for row in block] for block in RELAX]


def apply_block(block, values):
    out = []
    for row in block:
        total = None
        for factor, value in zip(row, values):
            part = factor * value
            total = part if total is None else total + part
        out.append(total)
    return out


def collide(h, solid, s_x, s_y, s_z, blocks):
    def plane(base):
        s_one, d_one = h[base] + h[base + 3], h[base] - h[base + 3]
        s_two, d_two = h[base + 1] + h[base + 2], h[base + 1] - h[base + 2]
        return s_one + s_two, s_one - s_two, d_one + d_two, d_one - d_two

    sum_x, dif_x = h[1] + h[2], h[1] - h[2]
    sum_y, dif_y = h[3] + h[4], h[3] - h[4]
    sum_z, dif_z = h[5] + h[6], h[5] - h[6]
    xy, q_xy, x_xy, y_xy = plane(7)
    xz, q_xz, x_xz, z_xz = plane(11)
    yz, q_yz, y_yz, z_yz = plane(15)
    axes = sum_x + sum_y + sum_z
    edges = xy + xz + yz
    density = h[0] * (1.0 / 3.0) + axes * (1.0 / 18.0) + edges * (1.0 / 36.0)
    m_x = dif_x * (1.0 / 18.0) + (x_xy + x_xz) * (1.0 / 36.0)
    m_y = dif_y * (1.0 / 18.0) + (y_xy + y_yz) * (1.0 / 36.0)
    m_z = dif_z * (1.0 / 18.0) + (z_xz + z_yz) * (1.0 / 36.0)
    inverse = 1.0 / density
    u_x, u_y, u_z = m_x * inverse, m_y * inverse, m_z * inverse
    e_xx, e_yy, e_zz = m_x * u_x, m_y * u_y, m_z * u_z
    e_xy, e_xz, e_yz = m_x * u_y, m_x * u_z, m_y * u_z
    energy = e_xx + e_yy + e_zz
    turn = e_yy - e_zz
    lean = 3.0 * e_xx - energy
    rest_off = h[0] - density + 1.5 * energy
    axes_off = axes - 6.0 * density
    edges_off = edges - 12.0 * density - 18.0 * energy
    a_one = 3.0 * sum_x - axes - 9.0 * lean
    b_one = edges - 3.0 * yz - 18.0 * lean
    a_two = sum_y - sum_z - 9.0 * turn
    b_two = xy - xz - 18.0 * turn
    q_xy = q_xy - 36.0 * e_xy
    q_xz = q_xz - 36.0 * e_xz
    q_yz = q_yz - 36.0 * e_yz

    r_rest, r_axes, r_edges = apply_block(blocks[0], [rest_off, axes_off, edges_off])
    r_a_one, r_b_one = apply_block(blocks[1], [a_one, b_one])
    r_a_two, r_b_two = apply_block(blocks[2], [a_two, b_two])
    fluid = 1.0 - solid
    mixed = solid * density
    w_x, w_y, w_z = solid * m_x, solid * m_y, solid * m_z
    n_x, n_y, n_z = mixed * s_x, mixed * s_y, mixed * s_z
    p_x = n_x * s_x - solid * e_xx
    p_y = n_y * s_y - solid * e_yy
    p_z = n_z * s_z - solid * e_zz
    total = 1.5 * (p_x + p_y + p_z)
    lean_s = 2.25 * p_x - 0.5 * total
    turn_s = 2.25 * (p_y - p_z)
    rest = fluid * r_rest - total
    axes = fluid * r_axes
    edges = fluid * r_edges + total
    a_one = fluid * r_a_one + lean_s
    b_one = fluid * r_b_one + lean_s
    a_two = fluid * r_a_two + turn_s
    b_two = fluid * r_b_two + turn_s
    q_xy = fluid * apply_block(blocks[3], [q_xy])[0] + 9.0 * (n_x * s_y - solid * e_xy)
    q_xz = fluid * apply_block(blocks[4], [q_xz])[0] + 9.0 * (n_x * s_z - solid * e_xz)
    q_yz = fluid * apply_block(blocks[5], [q_yz])[0] + 9.0 * (n_y * s_z - solid * e_yz)

    def odd(block, axis, one, two, m, n, w):
        six = 6.0 * m
        axis = axis - six
        twelve = six + six
        one = one - twelve
        two = two - twelve
        r_axis, r_one, r_two = apply_block(block, [axis, one, two])
        push = 3.0 * (n - w)
        half = 0.5 * solid
        return (
            fluid * r_axis - solid * axis + push,
            fluid * r_one - half * one + push,
            fluid * r_two - half * two + push,
        )

    d_x, x_xy, x_xz = odd(blocks[6], dif_x, x_xy, x_xz, m_x, n_x, w_x)
    d_y, y_xy, y_yz = odd(blocks[7], dif_y, y_xy, y_yz, m_y, n_y, w_y)
    d_z, z_xz, z_yz = odd(blocks[8], dif_z, z_xz, z_yz, m_z, n_z, w_z)
    out = [None] * 19
    out[0] = h[0] + rest
    even = axes + 2.0 * a_one
    out[1], out[2] = h[1] + (even + d_x), h[2] + (even - d_x)
    base = axes - a_one
    even = base + a_two
    out[3], out[4] = h[3] + (even + d_y), h[4] + (even - d_y)
    even = base - a_two
    out[5], out[6] = h[5] + (even + d_z), h[6] + (even - d_z)

    def spread(start, even, twist, one, two):
        same, cross = even + twist, even - twist
        plus, minus = one + two, one - two
        out[start] = h[start] + (same + plus)
        out[start + 3] = h[start + 3] + (same - plus)
        out[start + 1] = h[start + 1] + (cross + minus)
        out[start + 2] = h[start + 2] + (cross - minus)

    base = edges + b_one
    spread(7, base + b_two, q_xy, x_xy, y_xy)
    spread(11, base - b_two, q_xz, x_xz, z_xz)
    spread(15, edges - 2.0 * b_one, q_yz, y_yz, z_yz)
    return out


def iota(shape, dim):
    return lax.broadcasted_iota(I32, shape, dim)


def cells_of(anchor, size_y, size_z):
    plane = size_y * size_z
    a_x = lax.div(anchor, jnp.int32(plane))
    rest = anchor - a_x * plane
    a_y = lax.div(rest, jnp.int32(size_z))
    return a_x, a_y, rest - a_y * size_z


def halves(value):
    high = value.astype(BF16)
    return high, (value - high.astype(F32)).astype(BF16)


def dot_t(left, right):
    return lax.dot_general(left, right, (((1,), (1,)), ((), ())), preferred_element_type=F32)


def deposited(groups, shares, velocity, a_x, a_y, a_z, size_y, size_z):
    big = 8 * size_y
    centre = a_x * big + a_y
    lanes = centre.shape[1]
    totals = None
    rows_z = iota((size_z, lanes), 0)
    for off_z in range(3):
        weights = []
        for rows_x, rows_y in groups:
            away = rows_x * big + rows_y - centre
            weight = jnp.zeros(away.shape, F32)
            for off in range(9):
                move = (off // 3 - 1) * big + off % 3 - 1
                row = 3 * off + off_z
                weight = jnp.where(away == move, shares[row : row + 1, :], weight)
            weights.append([weight] + [weight * velocity[k : k + 1, :] for k in range(3)])
        rows = jnp.concatenate([w for block in weights for w in block], axis=0)
        high, low = halves(rows)
        hot = jnp.where(rows_z == a_z + (off_z - 1), 1.0, 0.0).astype(BF16)
        part = dot_t(high, hot) + dot_t(low, hot)
        totals = part if totals is None else totals + part
    return totals


def pack_kernel(velocity, change, fractions, anchor, destination, table, own, ahead, behind):
    rows = destination.shape[1]
    dest = destination[...]
    kinds = iota((16, rows), 0)
    hot = jnp.where(dest == kinds, 1.0, 0.0)
    order = jnp.where(iota((128, 128), 0) <= iota((128, 128), 1), 1.0, 0.0).astype(BF16)
    seen = jnp.zeros((16, 1), F32)
    ranks = []
    for start in range(0, rows, 128):
        counted = seen + lax.dot_general(
            hot[:, start : start + 128].astype(BF16),
            order,
            (((1,), (0,)), ((), ())),
            preferred_element_type=F32,
        )
        ranks.append(counted)
        seen = counted[:, 127:128]
    rank = jnp.concatenate(ranks, axis=1)
    kind = iota((16, 1), 0)
    begin = jnp.where(
        kind < 3,
        5 * CAP + CAP * kind,
        jnp.where(kind == 3, 0, jnp.where(kind == 5, CAP, 2 * CAP + CAP * (kind - 6))),
    ).astype(F32)
    leaving = (dest < 9) & (dest != 4)
    slot = jnp.sum(hot * (begin + rank - 1.0), axis=0, keepdims=True)
    slot = jnp.where(leaving, slot, -1.0).astype(I32)
    chosen = jnp.where(iota((128, rows), 0) == slot, 1.0, 0.0).astype(BF16)
    new_velocity = velocity[...] + change[...]
    payload = jnp.concatenate(
        [fractions[...], new_velocity, anchor[...].astype(F32), jnp.zeros((1, rows), F32)], axis=0
    )
    high = payload.astype(BF16)
    rest = payload - high.astype(F32)
    middle, low = halves(rest)
    packed = dot_t(high, chosen) + dot_t(middle, chosen) + dot_t(low, chosen)
    lane = iota((32, 128), 1)
    own[...] = jnp.where(lane < 2 * CAP, packed, 0.0)
    ahead[...] = jnp.where((lane >= 2 * CAP) & (lane < 5 * CAP), packed, 0.0)
    behind[...] = jnp.where(lane >= 5 * CAP, packed, 0.0)
    table[...] = jnp.where((iota((32, rows), 0) < 27) & (dest != 4), 0.0, payload)


def edge_kernel(size_x, size_y, size_z, populations, table, up, down):
    for i in range(19):
        for x in range(size_x):
            at = i * 2 * size_x + 2 * x
            down[at : at + 2, :] = populations[i, x, 0:2, :]
            up[at : at + 2, :] = populations[i, x, size_y - 2 : size_y, :]
    a_x, a_y, a_z = cells_of(table[30:31, :].astype(I32), size_y, size_z)
    rows = 2 * size_x
    index = iota((rows, 1), 0)
    rows_x, low = lax.div(index, jnp.int32(2)), lax.rem(index, jnp.int32(2))
    sums = deposited(
        [(rows_x, low), (rows_x, low + (size_y - 2))],
        table[0:27, :],
        table[27:30, :],
        a_x,
        a_y,
        a_z,
        size_y,
        size_z,
    )
    first = 19 * rows
    down[first : first + 4 * rows, :] = sums[: 4 * rows]
    up[first : first + 4 * rows, :] = sums[4 * rows :]


def stay_kernel(size_x, size_y, size_z, table, from_up, from_down, sums, outer):
    a_x, a_y, a_z = cells_of(table[30:31, :].astype(I32), size_y, size_z)
    index = iota((size_x * size_y, 1), 0)
    rows_x = lax.div(index, jnp.int32(size_y))
    totals = deposited(
        [(rows_x, index - rows_x * size_y)],
        table[0:27, :],
        table[27:30, :],
        a_x,
        a_y,
        a_z,
        size_y,
        size_z,
    )
    cells = size_x * size_y
    blank = jnp.zeros((8, size_z), F32)
    ones = jnp.ones((8, size_z), F32)
    for c in range(4):
        for x in range(size_x):
            at = c * cells + x * size_y
            sums[c, x, 0:size_y, :] = totals[at : at + size_y]
            sums[c, x, size_y : size_y + 8, :] = blank
            at = 19 * 2 * size_x + c * 2 * size_x + 2 * x
            sums[c, x, size_y : size_y + 2, :] = from_up[at : at + 2, :]
            sums[c, x, size_y + 6 : size_y + 8, :] = from_down[at : at + 2, :]
    for i in range(19):
        for x in range(size_x):
            at = i * 2 * size_x + 2 * x
            outer[i, x, :, :] = ones
            outer[i, x, 0:2, :] = from_up[at : at + 2, :]
            outer[i, x, 6:8, :] = from_down[at : at + 2, :]


def store_padded(target, i, x, tile, value, tiles):
    if tile == tiles:
        target[i, x, 0:8, :] = value
        target[i, x, 8 + 8 * tiles : 16 + 8 * tiles, :] = value
    else:
        target[i, x, 8 + 8 * tile : 16 + 8 * tile, :] = value
        if tile == 0:
            target[i, x, 16 + 8 * tiles : 24 + 8 * tiles, :] = value


def turned(value, shift, size_z):
    return value if shift == 0 else pltpu.roll(value, shift % size_z, 1)


def first_kernel(
    size_x, size_y, size_z, count, shifts, rates, sums, outer, populations, *refs
):
    columns = refs[: len(shifts)]
    post, solid, ahead, behind = refs[len(shifts) :]
    tiles = size_y // 8
    here = lax.axis_index("gy")
    per_group = 128 // LANES
    tables, offsets = [], []
    lane = iota((1, 128), 1)
    spot = lane % LANES
    group = spot // CAP
    across = jnp.where(
        (group == 0) | (group == 2) | (group == 5), -1, jnp.where((group == 3) | (group == 6), 0, 1)
    )
    for start in range(0, len(shifts), per_group):
        table = None
        offset = jnp.zeros((1, 128), I32)
        for k, shift in enumerate(shifts[start : start + per_group]):
            part = columns[start + k][...]
            part = part if k == 0 else pltpu.roll(part, k * LANES, 1)
            table = part if table is None else table + part
            source = lax.rem(here - shift + 2 * count, count)
            offset = jnp.where(lane // LANES == k, source - here, offset)
        tables.append(table)
        offsets.append((offset + across) * size_y)
    table = jnp.concatenate(tables, axis=1)
    offset = jnp.concatenate(offsets, axis=1)
    a_x, a_y, a_z = cells_of(table[30:31, :].astype(I32), size_y, size_z)
    wide = size_y + 8
    index = iota((size_x * wide, 1), 0)
    rows_x = lax.div(index, jnp.int32(wide))
    row = index - rows_x * wide
    rows_y = jnp.where(row < size_y + 2, row, jnp.where(row >= size_y + 6, row - wide, -3 * size_y))
    totals = deposited(
        [(rows_x, rows_y)], table[0:27, :], table[27:30, :], a_x, a_y + offset, a_z, size_y, size_z
    )
    blocks = relax_blocks(rates)
    cells = size_x * wide
    for x in range(size_x):
        for tile in range(tiles + 1):
            parts = []
            for c in range(4):
                at = c * cells + x * wide + 8 * tile
                parts.append(totals[at : at + 8] + sums[c, x, 8 * tile : 8 * tile + 8, :])
            scale = 1.0 / (parts[0] + 1e-06)
            share = jnp.minimum(parts[0], 1.0)
            flow = [parts[k] * scale for k in (1, 2, 3)]
            for c, value in enumerate([share] + flow):
                solid[c, x, 8 * tile : 8 * tile + 8, :] = value
            if tile == tiles:
                h = [outer[i, x, :, :] for i in range(19)]
            else:
                h = [populations[i, x, 8 * tile : 8 * tile + 8, :] for i in range(19)]
            out = collide(h, share, *flow, blocks)
            for i in range(19):
                store_padded(post, i, x, tile, out[i], tiles)
    faces(post, ahead, behind, size_x, size_z, tiles, tiles + 1)


def faces(post, ahead, behind, size_x, size_z, tiles, number):
    for target, numbers, x in ((ahead, FORWARD, size_x - 1), (behind, BACKWARD, 0)):
        for k, i in enumerate(numbers):
            _, c_y, c_z = VEC[i]
            for tile in range(number):
                at = 8 + 8 * tile - c_y
                target[k, 8 * tile : 8 * tile + 8, :] = turned(post[i, x, at : at + 8, :], c_z, size_z)


def streamed(post, from_behind, from_ahead, x, tile, size_x, size_y, size_z, at_low, at_high):
    tiles = size_y // 8
    out = []
    row = iota((8, size_z), 0)
    for i in range(19):
        c_x, c_y, c_z = VEC[i]
        if x - c_x < 0:
            value = from_behind[FORWARD.index(i), 8 * tile : 8 * tile + 8, :]
        elif x - c_x >= size_x:
            value = from_ahead[BACKWARD.index(i), 8 * tile : 8 * tile + 8, :]
        else:
            at = 8 + 8 * tile - c_y
            value = turned(post[i, x - c_x, at : at + 8, :], c_z, size_z)
        if c_y == 1 and tile == 0:
            back = post[OPP[i], x, 8:16, :]
            value = jnp.where((row == 0) & at_low, back, value)
        if c_y == -1 and tile == tiles - 1:
            back = post[OPP[i], x, 8 * tiles : 8 + 8 * tiles, :]
            value = jnp.where((row == 7) & at_high, back, value)
        out.append(value)
    return out


def second_kernel(
    size_x, size_y, size_z, count, rates, post, solid, from_behind, from_ahead, later, ahead, behind
):
    tiles = size_y // 8
    here = lax.axis_index("gy")
    at_low, at_high = here == 0, here == count - 1
    blocks = relax_blocks(rates)
    for x in range(size_x):
        for tile in range(tiles + 1):
            h = streamed(
                post, from_behind, from_ahead, x, tile, size_x, size_y, size_z, at_low, at_high
            )
            s = [solid[c, x, 8 * tile : 8 * tile + 8, :] for c in range(4)]
            out = collide(h, *s, blocks)
            for i in range(19):
                store_padded(later, i, x, tile, out[i], tiles)
    faces(later, ahead, behind, size_x, size_z, tiles, tiles)


def last_kernel(size_x, size_y, size_z, count, post, from_behind, from_ahead, advanced):
    here = lax.axis_index("gy")
    at_low, at_high = here == 0, here == count - 1
    for x in range(size_x):
        for tile in range(size_y // 8):
            h = streamed(
                post, from_behind, from_ahead, x, tile, size_x, size_y, size_z, at_low, at_high
            )
            for i in range(19):
                advanced[i, x, 8 * tile : 8 * tile + 8, :] = h[i]


def shape(*sizes):
    return jax.ShapeDtypeStruct(sizes, F32)


def call(kernel, out_shape, limit, in_specs=None):
    extra = {} if in_specs is None else {"in_specs": in_specs}
    return pl.pallas_call(
        kernel,
        out_shape=out_shape,
        compiler_params=pltpu.CompilerParams(vmem_limit_bytes=limit * 2**20),
        **extra,
    )


def around(value, axis, steps):
    count = lax.axis_size(axis)
    return lax.ppermute(value, axis, [(i, (i + steps) % count) for i in range(count)])


def local(populations, relax_rates, velocity, velocity_change, fractions, anchor, destination):
    _, size_x, size_y, size_z = populations.shape
    count = lax.axis_size("gy")
    rows = anchor.shape[0]
    sizes = (size_x, size_y, size_z)
    scalars = pl.BlockSpec(memory_space=pltpu.SMEM)
    blocks = pl.BlockSpec(memory_space=pltpu.VMEM)
    column_shape = shape(32, 128)
    table, own, ahead, behind = call(
        pack_kernel, (shape(32, rows), column_shape, column_shape, column_shape), 8
    )(velocity, velocity_change, fractions, anchor[None, :], destination[None, :])
    column = own + around(ahead, "gx", 1) + around(behind, "gx", -1)
    edge_rows = 23 * 2 * size_x
    up, down = call(
        functools.partial(edge_kernel, *sizes), (shape(edge_rows, size_z),) * 2, 8
    )(populations, table)
    from_down = around(up, "gy", 1)
    from_up = around(down, "gy", -1)
    shifts = [0]
    for shift in (1, -1, 2, -2):
        if all((shift - other) % count for other in shifts):
            shifts.append(shift)
    columns = [column] + [around(column, "gy", shift) for shift in shifts[1:]]
    sums, outer = call(
        functools.partial(stay_kernel, *sizes),
        (shape(4, size_x, size_y + 8, size_z), shape(19, size_x, 8, size_z)),
        16,
    )(table, from_up, from_down)
    padded = shape(19, size_x, size_y + 24, size_z)
    post, solid, ahead, behind = call(
        functools.partial(first_kernel, *sizes, count, shifts),
        (
            padded,
            shape(4, size_x, size_y + 8, size_z),
            shape(5, size_y + 8, size_z),
            shape(5, size_y + 8, size_z),
        ),
        24,
        [scalars] + [blocks] * (3 + len(shifts)),
    )(relax_rates, sums, outer, populations, *columns)
    from_behind, from_ahead = around(ahead, "gx", 1), around(behind, "gx", -1)
    later, ahead, behind = call(
        functools.partial(second_kernel, *sizes, count),
        (padded, shape(5, size_y, size_z), shape(5, size_y, size_z)),
        24,
        [scalars] + [blocks] * 4,
    )(relax_rates, post, solid, from_behind, from_ahead)
    from_behind, from_ahead = around(ahead, "gx", 1), around(behind, "gx", -1)
    return call(
        functools.partial(last_kernel, *sizes, count), shape(19, *sizes), 24, [blocks] * 3
    )(later, from_behind, from_ahead)


def solution(mesh):
    placed = (
        P(None, "gx", "gy", None),
        P(),
        P(None, ("gx", "gy")),
        P(None, ("gx", "gy")),
        P(None, ("gx", "gy")),
        P(("gx", "gy")),
        P(("gx", "gy")),
    )
    return jax.shard_map(
        local, mesh=mesh, in_specs=placed, out_specs=P(None, "gx", "gy", None), check_vma=False
    )
```

time: 379 us -> 49.1 us (0.13); the launches traced: 374 us -> 48.8 us
  other arithmetic: 174 us -> 0.01 us
  local copies, waits for them, and re-layouts: 118 us -> 5.95 us
  matrix products: 40.8 us -> 0 us
  starting transfers between devices: 31.9 us -> 17.6 us
  Pallas kernels: 0 us -> 11.8 us
  waiting for transfers between devices: 7.18 us -> 13.4 us
    add x2 -> x1, other arithmetic: 140 us -> 0.01 us  [local(): column = own + around(ahead, 'gx', 1) + around(behind, 'gx', -1)]
    dot_general x8 -> x0, matrix products: 40.8 us -> none  [the longest x2 13.5 us: collide(): projected = jnp.dot(to_moments, off_eq, precision=lax.Precision.HIGHEST)]
    unnamed x183 -> x16, local copies, waits for them, and re-layouts: 29.5 us -> 5.95 us
    squeeze x31 -> x0, local copies, waits for them, and re-layouts: 22.1 us -> none  [the longest x8 11.8 us: stream(): pulled = jnp.where(coord_y == 0, post[opposite[number]], pulled)]
    slice x29 -> x0, local copies, waits for them, and re-layouts: 15 us -> none  [the longest x2 8.52 us: stream(): pulled = jnp.where(coord_y == last_row, post[opposite[number]], pulled)]
    gather x4 -> x0, local copies, waits for them, and re-layouts: 14.7 us -> none  [collide(): bounce = states[opposite] - fluid_eq[opposite] - (states - solid_eq)]
    ppermute x16 -> x11, starting transfers between devices: 31.9 us -> 17.6 us  [around(): lax.ppermute(value, axis, [(i, (i + steps) % count) for i in range(count)])]
    reshape x5 -> x0, local copies, waits for them, and re-layouts: 13.7 us -> none  [the longest x1 10.1 us: deposit(): gathered = jnp.transpose(total.reshape(cells, 4), (1, 0))]
  transfers between devices with their start and end apart: 16 -> 11, of which waited for: 3 -> 4; matrix products, arithmetic and copies ran while one was open for 22% -> 0% of each run, Pallas kernels for 0% -> 5%
where the time goes in v1:
time: 49.1 us; the launch traced here: 48.8 us
  starting transfers between devices  17.6 us (36%)
  waiting for transfers between devices  13.4 us (27%)
  Pallas kernels  11.8 us (24%)
  local copies, waits for them, and re-layouts  5.95 us (12%)
    ppermute x11, starting transfers between devices, around(): lax.ppermute(value, axis, [(i, (i + steps) % count) for i in range(count)])  17.6 us
    ppermute x11, waiting for transfers between devices, around(): lax.ppermute(value, axis, [(i, (i + steps) % count) for i in range(count)])  13.4 us
    unnamed x16, local copies, waits for them, and re-layouts  5.95 us
    pallas_call x1, Pallas kernels, local(): call(functools.partial(second_kernel, *sizes, count), (padded, shape(5, s...  3.53 us
    pallas_call x1, Pallas kernels, local(): call(functools.partial(first_kernel, *sizes, count, shifts), (padded, sha...  3.48 us
    pallas_call x1, Pallas kernels, local(): call(functools.partial(last_kernel, *sizes, count), shape(19, *sizes), 24...  1.89 us
    pallas_call x1, Pallas kernels, local(): call(functools.partial(stay_kernel, *sizes), (shape(4, size_x, size_y + 8...  1.62 us
  transfers between devices with their start and end apart: 11, of which 4 were waited for; matrix products, arithmetic and copies ran while one was open for 0% of the time, Pallas kernels for 5%

profile of v1, /device:TPU:0, one launch (start us, length us, event | category | flops | bytes accessed | tf_op | source)
XLA Modules:
  0.0 48.8 jit_solution(1468440815992568375)
XLA Ops:
  0.0 0.8 %copy-done.2 = f32[27,512]{1,0:T(8,128)S(1)} copy-done((f32[27,512]{1,0:T(8,128)S(1)}, f32[27,512]{1,0:T(8,128)}, u32[]{:S(2)}) %copy-start.2) | copy-done | bytes 55320
  0.8 0.7 %copy-done.3 = f32[3,512]{1,0:T(4,128)S(1)} copy-done((f32[3,512]{1,0:T(4,128)S(1)}, f32[3,512]{1,0:T(4,128)}, u32[]{:S(2)}) %copy-start.3) | copy-done | bytes 6168
  1.5 0.7 %copy-done.4 = f32[3,512]{1,0:T(4,128)S(1)} copy-done((f32[3,512]{1,0:T(4,128)S(1)}, f32[3,512]{1,0:T(4,128)}, u32[]{:S(2)}) %copy-start.4) | copy-done | bytes 6168
  2.2 0.7 %copy-done.6 = s32[512]{0:T(512)S(1)} copy-done((s32[512]{0:T(512)S(1)}, s32[512]{0:T(512)}, u32[]{:S(2)}) %copy-start.6) | copy-done | bytes 2072
  2.9 0.7 %copy-done.7 = s32[512]{0:T(512)S(1)} copy-done((s32[512]{0:T(512)S(1)}, s32[512]{0:T(512)}, u32[]{:S(2)}) %copy-start.7) | copy-done | bytes 2072
  3.6 0.6 %shard_map.73 = (f32[32,512]{1,0:T(8,128)S(1)}, f32[32,128]{1,0:T(8,128)S(1)}, f32[32,128]{1,0:T(8,128)S(1)}, f32[32,128]{1,0:T(8,128)S(1)}) custom-call(f32[3,512]{1,0:T(4,128)S(1)} %copy-done.3, f32[3,512]{1,0:T(4,128)S(1)} %copy-done.4, f32[27,512]{1,0:T(8,128)S(1)} %copy-done.2, s32[1,512]{1,0:T(1,128)S(1)} %bitcast.2, s32[1,512]{1,0:T(1,128)S(1)} %bitcast.3), custom_call_target="tpu_custom_call" | custom-call | tf_op jit(solution)/shard_map/pallas_call | solution.py:564
  4.7 2.9 %collective-permute-start.3 = (f32[32,128]{1,0:T(8,128)S(1)}, f32[32,128]{1,0:T(8,128)S(1)}, u32[]{:S(2)}, u32[]{:S(2)}) collective-permute-start(f32[32,128]{1,0:T(8,128)S(1)} %get-tuple-element.27), channel_id=1, source_target_pairs={{0,28},{4,0},{8,4},{12,8},{16,12},{20,16},{24,20},{28,24},{1,29},{... | collective-permute-start | bytes 49160 | tf_op jit(solution)/shard_map/ppermute | solution.py:553
  7.6 1.7 %copy-done = f32[19,4,32,256]{3,2,1,0:T(8,128)S(1)} copy-done((f32[19,4,32,256]{3,2,1,0:T(8,128)S(1)}, f32[19,4,32,256]{3,2,1,0:T(8,128)}, u32[]{:S(2)}) %copy-start) | copy-done | bytes 2490392
  9.3 0.7 %shard_map.74 = (f32[184,256]{1,0:T(8,128)S(1)}, f32[184,256]{1,0:T(8,128)S(1)}) custom-call(f32[19,4,32,256]{3,2,1,0:T(8,128)S(1)} %copy-done, f32[32,512]{1,0:T(8,128)S(1)} %get-tuple-element.20.table), custom_call_target="tpu_custom_call" | custom-call | tf_op jit(solution)/shard_map/pallas_call | solution.py:569
  10.0 4.3 %collective-permute-start = (f32[184,256]{1,0:T(8,128)S(1)}, f32[184,256]{1,0:T(8,128)S(1)}, u32[]{:S(2)}, u32[]{:S(2)}) collective-permute-start(f32[184,256]{1,0:T(8,128)S(1)} %get-tuple-element.21), channel_id=1, source_target_pairs={{0,3},{1,0},{2,1},{3,2},{4,7},{5,4},{6,5},{7,6},{8,11},{9,8},{10,9... | collective-permute-start | bytes 565256 | tf_op jit(solution)/shard_map/ppermute | solution.py:553
  14.4 1.1 %collective-permute-start.6 = (f32[32,128]{1,0:T(8,128)S(1)}, f32[32,128]{1,0:T(8,128)S(1)}, u32[]{:S(2)}, u32[]{:S(2)}) collective-permute-start(f32[32,128]{1,0:T(8,128)S(1)} %add_add_fusion.refs_0_), channel_id=1, source_target_pairs={{0,2},{1,3},{2,0},{3,1},{4,6},{5,7},{6,4},{7,5},{8,10},{9,11},{10,... | collective-permute-start | bytes 49160 | tf_op jit(solution)/shard_map/ppermute | solution.py:553
  15.4 2.9 %collective-permute-start.5 = (f32[32,128]{1,0:T(8,128)S(1)}, f32[32,128]{1,0:T(8,128)S(1)}, u32[]{:S(2)}, u32[]{:S(2)}) collective-permute-start(f32[32,128]{1,0:T(8,128)S(1)} %add_add_fusion.refs_0_), channel_id=1, source_target_pairs={{0,3},{1,0},{2,1},{3,2},{4,7},{5,4},{6,5},{7,6},{8,11},{9,8},{10,9... | collective-permute-start | bytes 49160 | tf_op jit(solution)/shard_map/ppermute | solution.py:553
  18.8 0.7 %collective-permute-done.from_up = f32[184,256]{1,0:T(8,128)S(1)} collective-permute-done((f32[184,256]{1,0:T(8,128)S(1)}, f32[184,256]{1,0:T(8,128)S(1)}, u32[]{:S(2)}, u32[]{:S(2)}) %collective-permute-start) | collective-permute-done | bytes 188448 | tf_op jit(solution)/shard_map/ppermute | solution.py:553
  19.5 3.5 %collective-permute-done.1.from_down = f32[184,256]{1,0:T(8,128)S(1)} collective-permute-done((f32[184,256]{1,0:T(8,128)S(1)}, f32[184,256]{1,0:T(8,128)S(1)}, u32[]{:S(2)}, u32[]{:S(2)}) %collective-permute-start.1) | collective-permute-done | bytes 188448 | tf_op jit(solution)/shard_map/ppermute | solution.py:553
  23.0 1.6 %shard_map.75 = (f32[4,4,40,256]{3,2,1,0:T(8,128)S(1)}, f32[19,4,8,256]{3,2,1,0:T(8,128)S(1)}) custom-call(f32[32,512]{1,0:T(8,128)S(1)} %get-tuple-element.20.table, f32[184,256]{1,0:T(8,128)S(1)} %collective-permute-done.from_up, f32[184,256]{1,0:T(8,128)S(1)} %collective-permute-done.1.from_down), custom_call_target="tpu_custom_call" | custom-call | tf_op jit(solution)/shard_map/pallas_call | solution.py:579
  24.7 0.6 %copy-done.5 = f32[19]{0:T(128)S(1)} copy-done((f32[19]{0:T(128)S(1)}, f32[19]{0:T(128)}, u32[]{:S(2)}) %copy-start.5) | copy-done | bytes 100
  25.3 3.5 %shard_map.76 = (f32[19,4,56,256]{3,2,1,0:T(8,128)S(1)}, f32[4,4,40,256]{3,2,1,0:T(8,128)S(1)}, f32[5,40,256]{2,1,0:T(8,128)S(1)}, f32[5,40,256]{2,1,0:T(8,128)S(1)}) custom-call(f32[19]{0:T(128)S(1)} %copy-done.5, f32[4,4,40,256]{3,2,1,0:T(8,128)S(1)} %get-tuple-element.23.sums, f32[19,4,8,256]{3,2,1,0:T(8,128)S(1)} %get-tuple-element.24.outer, ...), custom_call_target="tpu_custom_call" | custom-call | tf_op jit(solution)/shard_map/pallas_call | solution.py:585
  28.9 2.6 %collective-permute-start.8 = (f32[5,40,256]{2,1,0:T(8,128)S(1)}, f32[5,40,256]{2,1,0:T(8,128)S(1)}, u32[]{:S(2)}, u32[]{:S(2)}) collective-permute-start(f32[5,40,256]{2,1,0:T(8,128)S(1)} %get-tuple-element.31), channel_id=1, source_target_pairs={{0,28},{4,0},{8,4},{12,8},{16,12},{20,16},{24,20},{28,24},{1,29},{... | collective-permute-start | bytes 614408 | tf_op jit(solution)/shard_map/ppermute | solution.py:553
  31.5 4.8 %collective-permute-done.7.from_behind = f32[5,40,256]{2,1,0:T(8,128)S(1)} collective-permute-done((f32[5,40,256]{2,1,0:T(8,128)S(1)}, f32[5,40,256]{2,1,0:T(8,128)S(1)}, u32[]{:S(2)}, u32[]{:S(2)}) %collective-permute-start.7) | collective-permute-done | bytes 204832 | tf_op jit(solution)/shard_map/ppermute | solution.py:553
  36.3 3.5 %shard_map.77 = (f32[19,4,56,256]{3,2,1,0:T(8,128)S(1)}, f32[5,32,256]{2,1,0:T(8,128)S(1)}, f32[5,32,256]{2,1,0:T(8,128)S(1)}) custom-call(f32[19]{0:T(128)S(1)} %copy-done.5, f32[19,4,56,256]{3,2,1,0:T(8,128)S(1)} %get-tuple-element.28.post, f32[4,4,40,256]{3,2,1,0:T(8,128)S(1)} %get-tuple-element.29.solid, ...), custom_call_target="tpu_custom_call" | custom-call | tf_op jit(solution)/shard_map/pallas_call | solution.py:597
  39.8 0.8 %collective-permute-start.9 = (f32[5,32,256]{2,1,0:T(8,128)S(1)}, f32[5,32,256]{2,1,0:T(8,128)S(1)}, u32[]{:S(2)}, u32[]{:S(2)}) collective-permute-start(f32[5,32,256]{2,1,0:T(8,128)S(1)} %get-tuple-element.33), channel_id=1, source_target_pairs={{0,4},{4,8},{8,12},{12,16},{16,20},{20,24},{24,28},{28,0},{1,5},{5... | collective-permute-start | bytes 491528 | tf_op jit(solution)/shard_map/ppermute | solution.py:553
  40.6 1.9 %collective-permute-start.10 = (f32[5,32,256]{2,1,0:T(8,128)S(1)}, f32[5,32,256]{2,1,0:T(8,128)S(1)}, u32[]{:S(2)}, u32[]{:S(2)}) collective-permute-start(f32[5,32,256]{2,1,0:T(8,128)S(1)} %get-tuple-element.34), channel_id=1, source_target_pairs={{0,28},{4,0},{8,4},{12,8},{16,12},{20,16},{24,20},{28,24},{1,29},{... | collective-permute-start | bytes 491528 | tf_op jit(solution)/shard_map/ppermute | solution.py:553
  42.5 4.4 %collective-permute-done.9.from_behind = f32[5,32,256]{2,1,0:T(8,128)S(1)} collective-permute-done((f32[5,32,256]{2,1,0:T(8,128)S(1)}, f32[5,32,256]{2,1,0:T(8,128)S(1)}, u32[]{:S(2)}, u32[]{:S(2)}) %collective-permute-start.9) | collective-permute-done | bytes 163872 | tf_op jit(solution)/shard_map/ppermute | solution.py:553
  46.9 1.9 %shard_map.78 = f32[19,4,32,256]{3,2,1,0:T(8,128)} custom-call(f32[19,4,56,256]{3,2,1,0:T(8,128)S(1)} %get-tuple-element.32.post, f32[5,32,256]{2,1,0:T(8,128)S(1)} %collective-permute-done.9.from_behind, f32[5,32,256]{2,1,0:T(8,128)S(1)} %collective-permute-done.10.from_ahead), custom_call_target="tpu_custom_call" | custom-call | tf_op jit(solution)/shard_map/pallas_call | solution.py:604
  (21 shorter events, 1.1 us)
Async XLA Ops:
  0.0 0.8 %copy-start.2 = (f32[27,512]{1,0:T(8,128)S(1)}, f32[27,512]{1,0:T(8,128)}, u32[]{:S(2)}) copy-start(f32[27,512]{1,0:T(8,128)} %fractions.1) | copy-start | bytes 165892
  0.8 0.7 %copy-start.3 = (f32[3,512]{1,0:T(4,128)S(1)}, f32[3,512]{1,0:T(4,128)}, u32[]{:S(2)}) copy-start(f32[3,512]{1,0:T(4,128)} %velocity.1) | copy-start | bytes 18436
  1.5 0.7 %copy-start.4 = (f32[3,512]{1,0:T(4,128)S(1)}, f32[3,512]{1,0:T(4,128)}, u32[]{:S(2)}) copy-start(f32[3,512]{1,0:T(4,128)} %change.1) | copy-start | bytes 18436
  2.2 0.7 %copy-start.6 = (s32[512]{0:T(512)S(1)}, s32[512]{0:T(512)}, u32[]{:S(2)}) copy-start(s32[512]{0:T(512)} %param.12) | copy-start | bytes 6148
  2.9 0.7 %copy-start.7 = (s32[512]{0:T(512)S(1)}, s32[512]{0:T(512)}, u32[]{:S(2)}) copy-start(s32[512]{0:T(512)} %param.13) | copy-start | bytes 6148
  4.2 10.2 %collective-permute-start.2 = (f32[32,128]{1,0:T(8,128)S(1)}, f32[32,128]{1,0:T(8,128)S(1)}, u32[]{:S(2)}, u32[]{:S(2)}) collective-permute-start(f32[32,128]{1,0:T(8,128)S(1)} %get-tuple-element.26), channel_id=1, source_target_pairs={{0,4},{4,8},{8,12},{12,16},{16,20},{20,24},{24,28},{28,0},{1,5},{5... | collective-permute-start | bytes 49160 | tf_op jit(solution)/shard_map/ppermute | solution.py:553
  4.7 9.7 %collective-permute-start.3 = (f32[32,128]{1,0:T(8,128)S(1)}, f32[32,128]{1,0:T(8,128)S(1)}, u32[]{:S(2)}, u32[]{:S(2)}) collective-permute-start(f32[32,128]{1,0:T(8,128)S(1)} %get-tuple-element.27), channel_id=1, source_target_pairs={{0,28},{4,0},{8,4},{12,8},{16,12},{20,16},{24,20},{28,24},{1,29},{... | collective-permute-start | bytes 49160 | tf_op jit(solution)/shard_map/ppermute | solution.py:553
  7.6 1.7 %copy-start = (f32[19,4,32,256]{3,2,1,0:T(8,128)S(1)}, f32[19,4,32,256]{3,2,1,0:T(8,128)}, u32[]{:S(2)}) copy-start(f32[19,4,32,256]{3,2,1,0:T(8,128)} %populations.3) | copy-start | bytes 7471108
  9.3 15.4 %copy-start.1 = (f32[19,4,32,256]{3,2,1,0:T(8,128)S(1)}, f32[19,4,32,256]{3,2,1,0:T(8,128)}, u32[]{:S(2)}) copy-start(f32[19,4,32,256]{3,2,1,0:T(8,128)} %populations.3) | copy-start | bytes 7471108
  10.0 9.5 %collective-permute-start = (f32[184,256]{1,0:T(8,128)S(1)}, f32[184,256]{1,0:T(8,128)S(1)}, u32[]{:S(2)}, u32[]{:S(2)}) collective-permute-start(f32[184,256]{1,0:T(8,128)S(1)} %get-tuple-element.21), channel_id=1, source_target_pairs={{0,3},{1,0},{2,1},{3,2},{4,7},{5,4},{6,5},{7,6},{8,11},{9,8},{10,9... | collective-permute-start | bytes 565256 | tf_op jit(solution)/shard_map/ppermute | solution.py:553
  14.3 8.7 %collective-permute-start.1 = (f32[184,256]{1,0:T(8,128)S(1)}, f32[184,256]{1,0:T(8,128)S(1)}, u32[]{:S(2)}, u32[]{:S(2)}) collective-permute-start(f32[184,256]{1,0:T(8,128)S(1)} %get-tuple-element.22), channel_id=1, source_target_pairs={{0,1},{1,2},{2,3},{3,0},{4,5},{5,6},{6,7},{7,4},{8,9},{9,10},{10,1... | collective-permute-start | bytes 565256 | tf_op jit(solution)/shard_map/ppermute | solution.py:553
  14.4 10.3 %collective-permute-start.6 = (f32[32,128]{1,0:T(8,128)S(1)}, f32[32,128]{1,0:T(8,128)S(1)}, u32[]{:S(2)}, u32[]{:S(2)}) collective-permute-start(f32[32,128]{1,0:T(8,128)S(1)} %add_add_fusion.refs_0_), channel_id=1, source_target_pairs={{0,2},{1,3},{2,0},{3,1},{4,6},{5,7},{6,4},{7,5},{8,10},{9,11},{10,... | collective-permute-start | bytes 49160 | tf_op jit(solution)/shard_map/ppermute | solution.py:553
  15.4 9.2 %collective-permute-start.5 = (f32[32,128]{1,0:T(8,128)S(1)}, f32[32,128]{1,0:T(8,128)S(1)}, u32[]{:S(2)}, u32[]{:S(2)}) collective-permute-start(f32[32,128]{1,0:T(8,128)S(1)} %add_add_fusion.refs_0_), channel_id=1, source_target_pairs={{0,3},{1,0},{2,1},{3,2},{4,7},{5,4},{6,5},{7,6},{8,11},{9,8},{10,9... | collective-permute-start | bytes 49160 | tf_op jit(solution)/shard_map/ppermute | solution.py:553
  18.3 6.4 %collective-permute-start.4 = (f32[32,128]{1,0:T(8,128)S(1)}, f32[32,128]{1,0:T(8,128)S(1)}, u32[]{:S(2)}, u32[]{:S(2)}) collective-permute-start(f32[32,128]{1,0:T(8,128)S(1)} %add_add_fusion.refs_0_), channel_id=1, source_target_pairs={{0,1},{1,2},{2,3},{3,0},{4,5},{5,6},{6,7},{7,4},{8,9},{9,10},{10,1... | collective-permute-start | bytes 49160 | tf_op jit(solution)/shard_map/ppermute | solution.py:553
  24.7 0.7 %copy-start.5 = (f32[19]{0:T(128)S(1)}, f32[19]{0:T(128)}, u32[]{:S(2)}) copy-start(f32[19]{0:T(128)} %rates.3) | copy-start | bytes 232
  28.8 7.4 %collective-permute-start.7 = (f32[5,40,256]{2,1,0:T(8,128)S(1)}, f32[5,40,256]{2,1,0:T(8,128)S(1)}, u32[]{:S(2)}, u32[]{:S(2)}) collective-permute-start(f32[5,40,256]{2,1,0:T(8,128)S(1)} %get-tuple-element.30), channel_id=1, source_target_pairs={{0,4},{4,8},{8,12},{12,16},{16,20},{20,24},{24,28},{28,0},{1,5},{5... | collective-permute-start | bytes 614408 | tf_op jit(solution)/shard_map/ppermute | solution.py:553
  28.9 7.4 %collective-permute-start.8 = (f32[5,40,256]{2,1,0:T(8,128)S(1)}, f32[5,40,256]{2,1,0:T(8,128)S(1)}, u32[]{:S(2)}, u32[]{:S(2)}) collective-permute-start(f32[5,40,256]{2,1,0:T(8,128)S(1)} %get-tuple-element.31), channel_id=1, source_target_pairs={{0,28},{4,0},{8,4},{12,8},{16,12},{20,16},{24,20},{28,24},{1,29},{... | collective-permute-start | bytes 614408 | tf_op jit(solution)/shard_map/ppermute | solution.py:553
  39.8 7.1 %collective-permute-start.9 = (f32[5,32,256]{2,1,0:T(8,128)S(1)}, f32[5,32,256]{2,1,0:T(8,128)S(1)}, u32[]{:S(2)}, u32[]{:S(2)}) collective-permute-start(f32[5,32,256]{2,1,0:T(8,128)S(1)} %get-tuple-element.33), channel_id=1, source_target_pairs={{0,4},{4,8},{8,12},{12,16},{16,20},{20,24},{24,28},{28,0},{1,5},{5... | collective-permute-start | bytes 491528 | tf_op jit(solution)/shard_map/ppermute | solution.py:553
  40.6 6.3 %collective-permute-start.10 = (f32[5,32,256]{2,1,0:T(8,128)S(1)}, f32[5,32,256]{2,1,0:T(8,128)S(1)}, u32[]{:S(2)}, u32[]{:S(2)}) collective-permute-start(f32[5,32,256]{2,1,0:T(8,128)S(1)} %get-tuple-element.34), channel_id=1, source_target_pairs={{0,28},{4,0},{8,4},{12,8},{16,12},{20,16},{24,20},{28,24},{1,29},{... | collective-permute-start | bytes 491528 | tf_op jit(solution)/shard_map/ppermute | solution.py:553

commit v2 on v1

--- a/solution.py
+++ b/solution.py
@@ -124,17 +124,32 @@
 RELAX = symmetric_blocks()
 
 
-def relax_blocks(rates):
+def relax_rows(rates, target):
     values = [rates[k] for k in range(19)]
-
-    def entry(terms):
-        total = None
-        for k, factor in terms:
-            part = values[k] * np.float32(factor)
-            total = part if total is None else total + part
-        return total
-
-    return [[[entry(terms) for terms in row] for row in block] for block in RELAX]
+    at = 0
+    for block in RELAX:
+        for row in block:
+            for terms in row:
+                total = None
+                for k, factor in terms:
+                    part = values[k] * np.float32(factor)
+                    total = part if total is None else total + part
+                target[at] = jnp.full((8, 128), total, F32)
+                at += 1
+
+
+def relax_blocks(table):
+    blocks, at = [], 0
+    for block in RELAX:
+        rows = []
+        for row in block:
+            rows.append([table[at + k] for k in range(len(row))])
+            at += len(row)
+        blocks.append(rows)
+    return blocks
+
+
+ENTRIES = sum(len(row) for block in RELAX for row in block)
 
 
 def apply_block(block, values):
@@ -272,8 +287,7 @@
     return lax.dot_general(left, right, (((1,), (1,)), ((), ())), preferred_element_type=F32)
 
 
-def deposited(groups, shares, velocity, a_x, a_y, a_z, size_y, size_z):
-    big = 8 * size_y
+def deposited(groups, shares, velocity, a_x, a_y, a_z, size_z, big):
     centre = a_x * big + a_y
     lanes = centre.shape[1]
     totals = None
@@ -296,12 +310,40 @@
     return totals
 
 
-def pack_kernel(velocity, change, fractions, anchor, destination, table, own, ahead, behind):
+def pack_kernel(
+    velocity_in,
+    change_in,
+    fractions_in,
+    anchor_in,
+    destination_in,
+    table,
+    own,
+    ahead,
+    behind,
+    velocity,
+    change,
+    fractions,
+    anchor,
+    destination,
+    done,
+):
+    pairs = (
+        (destination_in, destination),
+        (velocity_in, velocity),
+        (change_in, change),
+        (fractions_in, fractions),
+        (anchor_in, anchor),
+    )
+    copies = [pltpu.make_async_copy(a, b, done.at[k]) for k, (a, b) in enumerate(pairs)]
+    for copy in copies:
+        copy.start()
     rows = destination.shape[1]
+    order = jnp.where(iota((128, 128), 0) <= iota((128, 128), 1), 1.0, 0.0).astype(BF16)
+    for copy in copies:
+        copy.wait()
     dest = destination[...]
     kinds = iota((16, rows), 0)
     hot = jnp.where(dest == kinds, 1.0, 0.0)
-    order = jnp.where(iota((128, 128), 0) <= iota((128, 128), 1), 1.0, 0.0).astype(BF16)
     seen = jnp.zeros((16, 1), F32)
     ranks = []
     for start in range(0, rows, 128):
@@ -329,8 +371,7 @@
         [fractions[...], new_velocity, anchor[...].astype(F32), jnp.zeros((1, rows), F32)], axis=0
     )
     high = payload.astype(BF16)
-    rest = payload - high.astype(F32)
-    middle, low = halves(rest)
+    middle, low = halves(payload - high.astype(F32))
     packed = dot_t(high, chosen) + dot_t(middle, chosen) + dot_t(low, chosen)
     lane = iota((32, 128), 1)
     own[...] = jnp.where(lane < 2 * CAP, packed, 0.0)
@@ -339,12 +380,7 @@
     table[...] = jnp.where((iota((32, rows), 0) < 27) & (dest != 4), 0.0, payload)
 
 
-def edge_kernel(size_x, size_y, size_z, populations, table, up, down):
-    for i in range(19):
-        for x in range(size_x):
-            at = i * 2 * size_x + 2 * x
-            down[at : at + 2, :] = populations[i, x, 0:2, :]
-            up[at : at + 2, :] = populations[i, x, size_y - 2 : size_y, :]
+def edge_kernel(size_x, size_y, size_z, populations, table, one, two):
     a_x, a_y, a_z = cells_of(table[30:31, :].astype(I32), size_y, size_z)
     rows = 2 * size_x
     index = iota((rows, 1), 0)
@@ -356,15 +392,43 @@
         a_x,
         a_y,
         a_z,
-        size_y,
         size_z,
+        8 * size_y,
     )
     first = 19 * rows
-    down[first : first + 4 * rows, :] = sums[: 4 * rows]
-    up[first : first + 4 * rows, :] = sums[4 * rows :]
-
-
-def stay_kernel(size_x, size_y, size_z, table, from_up, from_down, sums, outer):
+
+    def write(down, up):
+        for i in range(19):
+            for x in range(size_x):
+                at = i * rows + 2 * x
+                down[at : at + 2, :] = populations[i, x, 0:2, :]
+                up[at : at + 2, :] = populations[i, x, size_y - 2 : size_y, :]
+        down[first : first + 4 * rows, :] = sums[: 4 * rows]
+        up[first : first + 4 * rows, :] = sums[4 * rows :]
+
+    even = lax.rem(lax.axis_index("gy"), 2) == 0
+
+    @pl.when(even)
+    def _():
+        write(two, one)
+
+    @pl.when(jnp.logical_not(even))
+    def _():
+        write(one, two)
+
+
+def merge_kernel(first, fold, own, from_behind, from_ahead, one_in, two_in, column, one, two):
+    del one_in, two_in
+    merged = own[...] + from_behind[...] + from_ahead[...]
+    column[...] = merged
+    deep = 32 // fold
+    for k in range(fold):
+        for target in (one, two):
+            target[first : first + deep, 128 * k : 128 * k + 128] = merged[deep * k : deep * k + deep]
+
+
+def stay_kernel(size_x, size_y, size_z, rates, table, sums, entries):
+    relax_rows(rates, entries)
     a_x, a_y, a_z = cells_of(table[30:31, :].astype(I32), size_y, size_z)
     index = iota((size_x * size_y, 1), 0)
     rows_x = lax.div(index, jnp.int32(size_y))
@@ -375,182 +439,303 @@
         a_x,
         a_y,
         a_z,
-        size_y,
         size_z,
+        8 * size_y,
     )
     cells = size_x * size_y
-    blank = jnp.zeros((8, size_z), F32)
-    ones = jnp.ones((8, size_z), F32)
     for c in range(4):
         for x in range(size_x):
             at = c * cells + x * size_y
-            sums[c, x, 0:size_y, :] = totals[at : at + size_y]
-            sums[c, x, size_y : size_y + 8, :] = blank
-            at = 19 * 2 * size_x + c * 2 * size_x + 2 * x
-            sums[c, x, size_y : size_y + 2, :] = from_up[at : at + 2, :]
-            sums[c, x, size_y + 6 : size_y + 8, :] = from_down[at : at + 2, :]
-    for i in range(19):
-        for x in range(size_x):
-            at = i * 2 * size_x + 2 * x
-            outer[i, x, :, :] = ones
-            outer[i, x, 0:2, :] = from_up[at : at + 2, :]
-            outer[i, x, 6:8, :] = from_down[at : at + 2, :]
-
-
-def store_padded(target, i, x, tile, value, tiles):
-    if tile == tiles:
-        target[i, x, 0:8, :] = value
-        target[i, x, 8 + 8 * tiles : 16 + 8 * tiles, :] = value
-    else:
-        target[i, x, 8 + 8 * tile : 16 + 8 * tile, :] = value
-        if tile == 0:
-            target[i, x, 16 + 8 * tiles : 24 + 8 * tiles, :] = value
-
-
-def turned(value, shift, size_z):
-    return value if shift == 0 else pltpu.roll(value, shift % size_z, 1)
-
-
-def first_kernel(
-    size_x, size_y, size_z, count, shifts, rates, sums, outer, populations, *refs
-):
-    columns = refs[: len(shifts)]
-    post, solid, ahead, behind = refs[len(shifts) :]
-    tiles = size_y // 8
+            sums[c, x, :, :] = totals[at : at + size_y]
+
+
+def outer_kernel(size_x, size_z, one, two, sums, outer):
+    blank = jnp.zeros((8, size_z), F32)
+    ones = jnp.ones((8, size_z), F32)
+    rows = 2 * size_x
+
+    def write(above, below):
+        for c in range(4):
+            for x in range(size_x):
+                at = (19 + c) * rows + 2 * x
+                sums[c, x, :, :] = blank
+                sums[c, x, 0:2, :] = above[at : at + 2, :]
+                sums[c, x, 6:8, :] = below[at : at + 2, :]
+        for i in range(19):
+            for x in range(size_x):
+                at = i * rows + 2 * x
+                outer[i, x, :, :] = ones
+                outer[i, x, 0:2, :] = above[at : at + 2, :]
+                outer[i, x, 6:8, :] = below[at : at + 2, :]
+
+    even = lax.rem(lax.axis_index("gy"), 2) == 0
+
+    @pl.when(even)
+    def _():
+        write(one, two)
+
+    @pl.when(jnp.logical_not(even))
+    def _():
+        write(two, one)
+
+
+def pair_source(here, parity, count):
+    other = jnp.where(lax.rem(here, 2) == parity, here + 1, here - 1)
+    return jnp.where((other >= 0) & (other < count), other, here + 2 * count)
+
+
+def arrivals(size_y, size_z, count, shifts, first, column, one, two, rest):
     here = lax.axis_index("gy")
-    per_group = 128 // LANES
-    tables, offsets = [], []
+    fold = size_z // 128
+    deep = 32 // fold
+
+    def unfolded(message):
+        return jnp.concatenate(
+            [message[first : first + deep, 128 * k : 128 * k + 128] for k in range(fold)], axis=0
+        )
+
+    parts = [column[...], unfolded(one), unfolded(two)] + [r[...] for r in rest]
+    sources = [here, pair_source(here, 0, count), pair_source(here, 1, count)]
+    sources += [lax.rem(here - shift + 2 * count, count) for shift in shifts]
     lane = iota((1, 128), 1)
-    spot = lane % LANES
-    group = spot // CAP
+    spot = lax.rem(lane, jnp.int32(LANES))
+    group = lax.div(spot, jnp.int32(CAP))
     across = jnp.where(
         (group == 0) | (group == 2) | (group == 5), -1, jnp.where((group == 3) | (group == 6), 0, 1)
     )
-    for start in range(0, len(shifts), per_group):
+    per_group = 128 // LANES
+    tables, offsets = [], []
+    for start in range(0, len(parts), per_group):
         table = None
-        offset = jnp.zeros((1, 128), I32)
-        for k, shift in enumerate(shifts[start : start + per_group]):
-            part = columns[start + k][...]
+        offset = jnp.full((1, 128), 2 * count, I32)
+        for k, part in enumerate(parts[start : start + per_group]):
             part = part if k == 0 else pltpu.roll(part, k * LANES, 1)
             table = part if table is None else table + part
-            source = lax.rem(here - shift + 2 * count, count)
-            offset = jnp.where(lane // LANES == k, source - here, offset)
+            offset = jnp.where(lax.div(lane, jnp.int32(LANES)) == k, sources[start + k] - here, offset)
         tables.append(table)
         offsets.append((offset + across) * size_y)
     table = jnp.concatenate(tables, axis=1)
-    offset = jnp.concatenate(offsets, axis=1)
     a_x, a_y, a_z = cells_of(table[30:31, :].astype(I32), size_y, size_z)
+    return table, a_x, a_y + jnp.concatenate(offsets, axis=1), a_z
+
+
+def store_padded(target, i, x, tile, part, value, tiles):
+    lanes = slice(128 * part, 128 * part + 128)
+    if tile == tiles:
+        target[i, x, 0:8, lanes] = value
+        target[i, x, 8 + 8 * tiles : 16 + 8 * tiles, lanes] = value
+    else:
+        target[i, x, 8 + 8 * tile : 16 + 8 * tile, lanes] = value
+        if tile == 0:
+            target[i, x, 16 + 8 * tiles : 24 + 8 * tiles, lanes] = value
+
+
+def turned(value, shift, size_z):
+    return value if shift == 0 else pltpu.roll(value, shift % size_z, 1)
+
+
+def first_kernel(
+    size_x, size_y, size_z, count, shifts, first, planes, entries, sums, outer_sums, outer,
+    populations, column, one, two, *refs
+):
+    rest, (post, solid), faces_out = refs[: len(shifts)], refs[len(shifts) : len(shifts) + 2], refs[len(shifts) + 2 :]
+    tiles = size_y // 8
+    table, a_x, a_y, a_z = arrivals(size_y, size_z, count, shifts, first, column, one, two, rest)
     wide = size_y + 8
-    index = iota((size_x * wide, 1), 0)
-    rows_x = lax.div(index, jnp.int32(wide))
-    row = index - rows_x * wide
+    index = iota((len(planes) * wide, 1), 0)
+    number = lax.div(index, jnp.int32(wide))
+    row = index - number * wide
+    rows_x = number + planes[0] if len(planes) == planes[-1] - planes[0] + 1 else number * (size_x - 1)
     rows_y = jnp.where(row < size_y + 2, row, jnp.where(row >= size_y + 6, row - wide, -3 * size_y))
+    big = 4 * size_y * (count + 2)
     totals = deposited(
-        [(rows_x, rows_y)], table[0:27, :], table[27:30, :], a_x, a_y + offset, a_z, size_y, size_z
+        [(rows_x, rows_y)], table[0:27, :], table[27:30, :], a_x, a_y, a_z, size_z, big
     )
-    blocks = relax_blocks(rates)
-    cells = size_x * wide
-    for x in range(size_x):
+    blocks = relax_blocks(entries)
+    cells = len(planes) * wide
+    for p, x in enumerate(planes):
         for tile in range(tiles + 1):
-            parts = []
-            for c in range(4):
-                at = c * cells + x * wide + 8 * tile
-                parts.append(totals[at : at + 8] + sums[c, x, 8 * tile : 8 * tile + 8, :])
-            scale = 1.0 / (parts[0] + 1e-06)
-            share = jnp.minimum(parts[0], 1.0)
-            flow = [parts[k] * scale for k in (1, 2, 3)]
-            for c, value in enumerate([share] + flow):
-                solid[c, x, 8 * tile : 8 * tile + 8, :] = value
-            if tile == tiles:
-                h = [outer[i, x, :, :] for i in range(19)]
-            else:
-                h = [populations[i, x, 8 * tile : 8 * tile + 8, :] for i in range(19)]
-            out = collide(h, share, *flow, blocks)
-            for i in range(19):
-                store_padded(post, i, x, tile, out[i], tiles)
-    faces(post, ahead, behind, size_x, size_z, tiles, tiles + 1)
-
-
-def faces(post, ahead, behind, size_x, size_z, tiles, number):
-    for target, numbers, x in ((ahead, FORWARD, size_x - 1), (behind, BACKWARD, 0)):
+            rows = slice(8 * tile, 8 * tile + 8)
+            for part in range(size_z // 128):
+                lanes = slice(128 * part, 128 * part + 128)
+                parts = []
+                for c in range(4):
+                    at = c * cells + p * wide + 8 * tile
+                    staying = outer_sums[c, x, :, lanes] if tile == tiles else sums[c, x, rows, lanes]
+                    parts.append(totals[at : at + 8, lanes] + staying)
+                scale = 1.0 / (parts[0] + 1e-06)
+                share = jnp.minimum(parts[0], 1.0)
+                flow = [parts[k] * scale for k in (1, 2, 3)]
+                for c, value in enumerate([share] + flow):
+                    solid[c, p, rows, lanes] = value
+                if tile == tiles:
+                    h = [outer[i, x, :, lanes] for i in range(19)]
+                else:
+                    h = [populations[i, x, rows, lanes] for i in range(19)]
+                out = collide(h, share, *flow, blocks)
+                for i in range(19):
+                    store_padded(post, i, p, tile, part, out[i], tiles)
+    if faces_out:
+        faces(post, *faces_out, size_y, size_z, True)
+
+
+def faces(post, ahead, behind, size_y, size_z, outer):
+    tiles = size_y // 8
+    for target, numbers, p in ((ahead, FORWARD, 1), (behind, BACKWARD, 0)):
         for k, i in enumerate(numbers):
             _, c_y, c_z = VEC[i]
-            for tile in range(number):
+            for tile in range(tiles):
                 at = 8 + 8 * tile - c_y
-                target[k, 8 * tile : 8 * tile + 8, :] = turned(post[i, x, at : at + 8, :], c_z, size_z)
-
-
-def streamed(post, from_behind, from_ahead, x, tile, size_x, size_y, size_z, at_low, at_high):
+                to = k * size_y + 8 * tile
+                target[to : to + 8, :] = turned(post[i, p, at : at + 8, :], c_z, size_z)
+            if outer:
+                at = 8 + size_y - c_y
+                value = turned(post[i, p, at : at + 8, :], c_z, size_z)
+                to = 5 * size_y + 2 * k
+                target[to : to + 1, :] = value[0:1]
+                target[to + 1 : to + 2, :] = value[7:8]
+
+
+def streamed(ends, middle, message_behind, message_ahead, i, x, tile, size_x, size_y, size_z, walls):
     tiles = size_y // 8
-    out = []
     row = iota((8, size_z), 0)
+    c_x, c_y, c_z = VEC[i]
+
+    def plane(x):
+        if x == 0:
+            return ends, 0
+        if x == size_x - 1:
+            return ends, 1
+        return middle, x - 1
+
+    from_x = x - c_x
+    if 0 <= from_x < size_x:
+        source, p = plane(from_x)
+        at = 8 + 8 * tile - c_y
+        value = turned(source[i, p, at : at + 8, :], c_z, size_z)
+    else:
+        message, numbers = (message_behind, FORWARD) if from_x < 0 else (message_ahead, BACKWARD)
+        k = numbers.index(i)
+        if tile < tiles:
+            at = k * size_y + 8 * tile
+            value = message[at : at + 8, :]
+        else:
+            at = 5 * size_y + 2 * k
+            value = jnp.where(row < 4, message[at : at + 1, :], message[at + 1 : at + 2, :])
+    source, p = plane(x)
+    if c_y == 1 and tile == 0:
+        value = jnp.where((row == 0) & walls[0], source[OPP[i], p, 8:16, :], value)
+    if c_y == -1 and tile == tiles - 1:
+        back = source[OPP[i], p, size_y : 8 + size_y, :]
+        value = jnp.where((row == 7) & walls[1], back, value)
+    return value
+
+
+def walls_of(count):
+    here = lax.axis_index("gy")
+    return here == 0, here == count - 1
+
+
+def second_kernel(size_x, size_y, size_z, count, planes, entries, ends, middle, solid, *refs):
+    refs = list(refs)
+    message_behind, message_ahead = (refs.pop(0), refs.pop(0)) if planes[0] == 0 else (None, None)
+    later, faces_out = refs[0], refs[1:]
+    tiles = size_y // 8
+    walls = walls_of(count)
+    blocks = relax_blocks(entries)
+    for p, x in enumerate(planes):
+        for tile in range(tiles + 1):
+            rows = slice(8 * tile, 8 * tile + 8)
+            h = [
+                streamed(
+                    ends, middle, message_behind, message_ahead, i, x, tile, size_x, size_y, size_z, walls
+                )
+                for i in range(19)
+            ]
+            for part in range(size_z // 128):
+                lanes = slice(128 * part, 128 * part + 128)
+                s = [solid[c, p, rows, lanes] for c in range(4)]
+                out = collide([v[:, lanes] for v in h], *s, blocks)
+                for i in range(19):
+                    store_padded(later, i, p, tile, part, out[i], tiles)
+    if faces_out:
+        faces(later, *faces_out, size_y, size_z, False)
+
+
+def last_kernel(size_x, size_y, size_z, count, ends, middle, advanced, held, done):
+    walls = walls_of(count)
+    copies = []
     for i in range(19):
-        c_x, c_y, c_z = VEC[i]
-        if x - c_x < 0:
-            value = from_behind[FORWARD.index(i), 8 * tile : 8 * tile + 8, :]
-        elif x - c_x >= size_x:
-            value = from_ahead[BACKWARD.index(i), 8 * tile : 8 * tile + 8, :]
-        else:
-            at = 8 + 8 * tile - c_y
-            value = turned(post[i, x - c_x, at : at + 8, :], c_z, size_z)
-        if c_y == 1 and tile == 0:
-            back = post[OPP[i], x, 8:16, :]
-            value = jnp.where((row == 0) & at_low, back, value)
-        if c_y == -1 and tile == tiles - 1:
-            back = post[OPP[i], x, 8 * tiles : 8 + 8 * tiles, :]
-            value = jnp.where((row == 7) & at_high, back, value)
-        out.append(value)
-    return out
-
-
-def second_kernel(
-    size_x, size_y, size_z, count, rates, post, solid, from_behind, from_ahead, later, ahead, behind
+        for x in range(size_x):
+            if not 0 <= x - VEC[i][0] < size_x:
+                continue
+            for tile in range(size_y // 8):
+                held[i, x, 8 * tile : 8 * tile + 8, :] = streamed(
+                    ends, middle, None, None, i, x, tile, size_x, size_y, size_z, walls
+                )
+        low, high = max(0, VEC[i][0]), size_x + min(0, VEC[i][0])
+        copy = pltpu.make_async_copy(
+            held.at[i, low:high], advanced.at[i, low:high], done.at[i]
+        )
+        copy.start()
+        copies.append(copy)
+    for copy in copies:
+        copy.wait()
+
+
+def enter_kernel(
+    size_x, size_y, size_z, count, ends, message_behind, message_ahead, given, advanced, held, done
 ):
-    tiles = size_y // 8
-    here = lax.axis_index("gy")
-    at_low, at_high = here == 0, here == count - 1
-    blocks = relax_blocks(rates)
-    for x in range(size_x):
-        for tile in range(tiles + 1):
-            h = streamed(
-                post, from_behind, from_ahead, x, tile, size_x, size_y, size_z, at_low, at_high
-            )
-            s = [solid[c, x, 8 * tile : 8 * tile + 8, :] for c in range(4)]
-            out = collide(h, *s, blocks)
-            for i in range(19):
-                store_padded(later, i, x, tile, out[i], tiles)
-    faces(later, ahead, behind, size_x, size_z, tiles, tiles)
-
-
-def last_kernel(size_x, size_y, size_z, count, post, from_behind, from_ahead, advanced):
-    here = lax.axis_index("gy")
-    at_low, at_high = here == 0, here == count - 1
-    for x in range(size_x):
-        for tile in range(size_y // 8):
-            h = streamed(
-                post, from_behind, from_ahead, x, tile, size_x, size_y, size_z, at_low, at_high
-            )
-            for i in range(19):
-                advanced[i, x, 8 * tile : 8 * tile + 8, :] = h[i]
+    del given
+    walls = walls_of(count)
+    copies = []
+    for x, numbers in ((0, FORWARD), (size_x - 1, BACKWARD)):
+        for i in numbers:
+            k = len(copies)
+            for tile in range(size_y // 8):
+                held[k, 8 * tile : 8 * tile + 8, :] = streamed(
+                    ends, None, message_behind, message_ahead, i, x, tile, size_x, size_y, size_z, walls
+                )
+            copy = pltpu.make_async_copy(held.at[k], advanced.at[i, x], done.at[k])
+            copy.start()
+            copies.append(copy)
+    for copy in copies:
+        copy.wait()
 
 
 def shape(*sizes):
     return jax.ShapeDtypeStruct(sizes, F32)
 
 
-def call(kernel, out_shape, limit, in_specs=None):
-    extra = {} if in_specs is None else {"in_specs": in_specs}
+VMEM = pl.BlockSpec(memory_space=pltpu.VMEM)
+SMEM = pl.BlockSpec(memory_space=pltpu.SMEM)
+HBM = pl.BlockSpec(memory_space=pltpu.HBM)
+
+
+def call(kernel, out_shape, limit, in_specs, out_specs=None, scratch=(), aliases=None):
     return pl.pallas_call(
         kernel,
         out_shape=out_shape,
+        in_specs=in_specs,
+        out_specs=jax.tree.map(lambda _: VMEM, out_shape) if out_specs is None else out_specs,
+        scratch_shapes=scratch,
+        input_output_aliases={} if aliases is None else aliases,
         compiler_params=pltpu.CompilerParams(vmem_limit_bytes=limit * 2**20),
-        **extra,
     )
 
 
 def around(value, axis, steps):
     count = lax.axis_size(axis)
     return lax.ppermute(value, axis, [(i, (i + steps) % count) for i in range(count)])
+
+
+def paired(value, axis, parity):
+    count = lax.axis_size(axis)
+    pairs = []
+    for i in range(count):
+        other = i + 1 if i % 2 == parity else i - 1
+        pairs.append((i, other if 0 <= other < count else i))
+    return lax.ppermute(value, axis, pairs)
 
 
 def local(populations, relax_rates, velocity, velocity_change, fractions, anchor, destination):
@@ -558,52 +743,97 @@
     count = lax.axis_size("gy")
     rows = anchor.shape[0]
     sizes = (size_x, size_y, size_z)
-    scalars = pl.BlockSpec(memory_space=pltpu.SMEM)
-    blocks = pl.BlockSpec(memory_space=pltpu.VMEM)
-    column_shape = shape(32, 128)
+    part = functools.partial
+    migrants = shape(32, 128)
     table, own, ahead, behind = call(
-        pack_kernel, (shape(32, rows), column_shape, column_shape, column_shape), 8
+        pack_kernel,
+        (shape(32, rows), migrants, migrants, migrants),
+        8,
+        [HBM] * 5,
+        scratch=[
+            pltpu.VMEM((3, rows), F32),
+            pltpu.VMEM((3, rows), F32),
+            pltpu.VMEM((27, rows), F32),
+            pltpu.VMEM((1, rows), I32),
+            pltpu.VMEM((1, rows), I32),
+            pltpu.SemaphoreType.DMA((5,)),
+        ],
     )(velocity, velocity_change, fractions, anchor[None, :], destination[None, :])
-    column = own + around(ahead, "gx", 1) + around(behind, "gx", -1)
-    edge_rows = 23 * 2 * size_x
-    up, down = call(
-        functools.partial(edge_kernel, *sizes), (shape(edge_rows, size_z),) * 2, 8
-    )(populations, table)
-    from_down = around(up, "gy", 1)
-    from_up = around(down, "gy", -1)
-    shifts = [0]
-    for shift in (1, -1, 2, -2):
-        if all((shift - other) % count for other in shifts):
+    from_behind, from_ahead = around(ahead, "gx", 1), around(behind, "gx", -1)
+    first = 23 * 2 * size_x
+    fold = size_z // 128
+    message = shape(first + 32 // fold, size_z)
+    one, two = call(part(edge_kernel, *sizes), (message, message), 8, [VMEM] * 2)(populations, table)
+    column, one, two = call(
+        part(merge_kernel, first, fold),
+        (migrants, message, message),
+        8,
+        [VMEM] * 5,
+        aliases={3: 1, 4: 2},
+    )(own, from_behind, from_ahead, one, two)
+    shifts = []
+    for shift in (2, -2):
+        if shift % count > 1 and all((shift - other) % count for other in shifts):
             shifts.append(shift)
-    columns = [column] + [around(column, "gy", shift) for shift in shifts[1:]]
-    sums, outer = call(
-        functools.partial(stay_kernel, *sizes),
-        (shape(4, size_x, size_y + 8, size_z), shape(19, size_x, 8, size_z)),
+    rest = [around(column, "gy", shift) for shift in shifts]
+    one, two = paired(one, "gy", 0), paired(two, "gy", 1)
+    sums, entries = call(
+        part(stay_kernel, *sizes), (shape(4, *sizes), shape(ENTRIES, 8, 128)), 16, [SMEM, VMEM]
+    )(relax_rates, table)
+    outer_sums, outer = call(
+        part(outer_kernel, size_x, size_z),
+        (shape(4, size_x, 8, size_z), shape(19, size_x, 8, size_z)),
+        8,
+        [VMEM] * 2,
+    )(one, two)
+
+    def padded(planes):
+        return shape(19, planes, size_y + 24, size_z)
+
+    def solids(planes):
+        return shape(4, planes, size_y + 8, size_z)
+
+    outside, inside = (0, size_x - 1), tuple(range(1, size_x - 1))
+    known = (entries, sums, outer_sums, outer, populations, column, one, two, *rest)
+    wide_face = shape((5 * size_y + 10 + 7) // 8 * 8, size_z)
+    face = shape(5 * size_y, size_z)
+    ends, solid_ends, ahead, behind = call(
+        part(first_kernel, *sizes, count, shifts, first, outside),
+        (padded(2), solids(2), wide_face, wide_face),
         16,
-    )(table, from_up, from_down)
-    padded = shape(19, size_x, size_y + 24, size_z)
-    post, solid, ahead, behind = call(
-        functools.partial(first_kernel, *sizes, count, shifts),
-        (
-            padded,
-            shape(4, size_x, size_y + 8, size_z),
-            shape(5, size_y + 8, size_z),
-            shape(5, size_y + 8, size_z),
-        ),
-        24,
-        [scalars] + [blocks] * (3 + len(shifts)),
-    )(relax_rates, sums, outer, populations, *columns)
+        [VMEM] * len(known),
+    )(*known)
     from_behind, from_ahead = around(ahead, "gx", 1), around(behind, "gx", -1)
-    later, ahead, behind = call(
-        functools.partial(second_kernel, *sizes, count),
-        (padded, shape(5, size_y, size_z), shape(5, size_y, size_z)),
-        24,
-        [scalars] + [blocks] * 4,
-    )(relax_rates, post, solid, from_behind, from_ahead)
+    middle, solid_middle = call(
+        part(first_kernel, *sizes, count, shifts, first, inside),
+        (padded(len(inside)), solids(len(inside))),
+        16,
+        [VMEM] * len(known),
+    )(*known)
+    later_middle = call(
+        part(second_kernel, *sizes, count, inside), padded(len(inside)), 16, [VMEM] * 4
+    )(entries, ends, middle, solid_middle)
+    later_ends, ahead, behind = call(
+        part(second_kernel, *sizes, count, outside), (padded(2), face, face), 16, [VMEM] * 6
+    )(entries, ends, middle, solid_ends, from_behind, from_ahead)
     from_behind, from_ahead = around(ahead, "gx", 1), around(behind, "gx", -1)
+    advanced = call(
+        part(last_kernel, *sizes, count),
+        shape(19, *sizes),
+        16,
+        [VMEM] * 2,
+        HBM,
+        [pltpu.VMEM((19, *sizes), F32), pltpu.SemaphoreType.DMA((19,))],
+    )(later_ends, later_middle)
     return call(
-        functools.partial(last_kernel, *sizes, count), shape(19, *sizes), 24, [blocks] * 3
-    )(later, from_behind, from_ahead)
+        part(enter_kernel, *sizes, count),
+        shape(19, *sizes),
+        16,
+        [VMEM] * 3 + [HBM],
+        HBM,
+        [pltpu.VMEM((10, size_y, size_z), F32), pltpu.SemaphoreType.DMA((10,))],
+        {3: 0},
+    )(later_ends, from_behind, from_ahead, advanced)
 
 
 def solution(mesh):

time: 49.1 us -> 40.5 us (0.82)
  the two profiles are of different devices: /device:TPU:0 before, /device:TPU:1 now
where the time goes in v2:
time: 40.5 us; the launch traced here: 40.1 us
  starting transfers between devices  12.5 us (31%)
  Pallas kernels  12.3 us (30%)
  waiting for transfers between devices  9.88 us (24%)
  local copies, waits for them, and re-layouts  5.32 us (13%)
    ppermute x7, starting transfers between devices, around(): lax.ppermute(value, axis, [(i, (i + steps) % count) for i in range(count)])  10.4 us
    ppermute x7, waiting for transfers between devices, around(): lax.ppermute(value, axis, [(i, (i + steps) % count) for i in range(count)])  9.87 us
    unnamed x16, local copies, waits for them, and re-layouts  5.32 us
    pallas_call x1, Pallas kernels, local(): call(part(stay_kernel, *sizes), (shape(4, *sizes), shape(ENTRIES, 8, 128)...  2.04 us
    ppermute x2, starting transfers between devices, paired(): return lax.ppermute(value, axis, pairs)  2.02 us
    pallas_call x1, Pallas kernels, local(): call(part(first_kernel, *sizes, count, shifts, first, outside), (padded(2...  1.72 us
    pallas_call x1, Pallas kernels, local(): call(part(first_kernel, *sizes, count, shifts, first, inside), (padded(le...  1.6 us
    pallas_call x1, Pallas kernels, local(): call(part(last_kernel, *sizes, count), shape(19, *sizes), 16, [VMEM] * 2,...  1.5 us
  transfers between devices with their start and end apart: 9, of which 5 were waited for; matrix products, arithmetic and copies ran while one was open for 0% of the time, Pallas kernels for 19%

profile of v2, /device:TPU:1, one launch (start us, length us, event | category | flops | bytes accessed | tf_op | source)
XLA Modules:
  0.0 40.1 jit_solution(12010299587936794442)
XLA Ops:
  0.0 0.9 %copy-done.2 = f32[27,512]{1,0:T(8,128)S(1)} copy-done((f32[27,512]{1,0:T(8,128)S(1)}, f32[27,512]{1,0:T(8,128)}, u32[]{:S(2)}) %copy-start.2) | copy-done | bytes 55320
  0.9 0.7 %copy-done.3 = f32[3,512]{1,0:T(4,128)S(1)} copy-done((f32[3,512]{1,0:T(4,128)S(1)}, f32[3,512]{1,0:T(4,128)}, u32[]{:S(2)}) %copy-start.3) | copy-done | bytes 6168
  1.6 0.7 %copy-done.4 = f32[3,512]{1,0:T(4,128)S(1)} copy-done((f32[3,512]{1,0:T(4,128)S(1)}, f32[3,512]{1,0:T(4,128)}, u32[]{:S(2)}) %copy-start.4) | copy-done | bytes 6168
  2.3 0.7 %copy-done.5 = s32[512]{0:T(512)S(1)} copy-done((s32[512]{0:T(512)S(1)}, s32[512]{0:T(512)}, u32[]{:S(2)}) %copy-start.5) | copy-done | bytes 2072
  2.9 0.7 %copy-done.6 = s32[512]{0:T(512)S(1)} copy-done((s32[512]{0:T(512)S(1)}, s32[512]{0:T(512)}, u32[]{:S(2)}) %copy-start.6) | copy-done | bytes 2072
  3.6 0.7 %shard_map.73 = (f32[32,512]{1,0:T(8,128)S(1)}, f32[32,128]{1,0:T(8,128)S(1)}, f32[32,128]{1,0:T(8,128)S(1)}, f32[32,128]{1,0:T(8,128)S(1)}) custom-call(f32[3,512]{1,0:T(4,128)S(1)} %copy-done.3, f32[3,512]{1,0:T(4,128)S(1)} %copy-done.4, f32[27,512]{1,0:T(8,128)S(1)} %copy-done.2, s32[1,512]{1,0:T(1,128)S(1)} %bitcast.2, s32[1,512]{1,0:T(1,128)S(1)} %bitcast.3), custom_call_target="tpu_custom_call" | custom-call | tf_op jit(solution)/shard_map/pallas_call | solution.py:748
  4.4 2.7 %collective-permute-start = (f32[32,128]{1,0:T(8,128)S(1)}, f32[32,128]{1,0:T(8,128)S(1)}, u32[]{:S(2)}, u32[]{:S(2)}) collective-permute-start(f32[32,128]{1,0:T(8,128)S(1)} %get-tuple-element.31), channel_id=1, source_target_pairs={{0,4},{4,8},{8,12},{12,16},{16,20},{20,24},{24,28},{28,0},{1,5},{5... | collective-permute-start | bytes 49160 | tf_op jit(solution)/shard_map/ppermute | solution.py:729
  7.0 1.7 %copy-done = f32[19,4,32,256]{3,2,1,0:T(8,128)S(1)} copy-done((f32[19,4,32,256]{3,2,1,0:T(8,128)S(1)}, f32[19,4,32,256]{3,2,1,0:T(8,128)}, u32[]{:S(2)}) %copy-start) | copy-done | bytes 2490392
  8.7 0.8 %shard_map.75 = (f32[200,256]{1,0:T(8,128)S(1)}, f32[200,256]{1,0:T(8,128)S(1)}) custom-call(f32[19,4,32,256]{3,2,1,0:T(8,128)S(1)} %copy-done, f32[32,512]{1,0:T(8,128)S(1)} %get-tuple-element.27.table), custom_call_target="tpu_custom_call" | custom-call | tf_op jit(solution)/shard_map/pallas_call | solution.py:766
  9.5 0.7 %collective-permute-done.1.from_ahead = f32[32,128]{1,0:T(8,128)S(1)} collective-permute-done((f32[32,128]{1,0:T(8,128)S(1)}, f32[32,128]{1,0:T(8,128)S(1)}, u32[]{:S(2)}, u32[]{:S(2)}) %collective-permute-start.1) | collective-permute-done | bytes 16416 | tf_op jit(solution)/shard_map/ppermute | solution.py:729
  10.2 1.4 %collective-permute-start.2 = (f32[200,256]{1,0:T(8,128)S(1)}, f32[200,256]{1,0:T(8,128)S(1)}, u32[]{:S(2)}, u32[]{:S(2)}) collective-permute-start(f32[200,256]{1,0:T(8,128)S(1)} %get-tuple-element.35), channel_id=1, source_target_pairs={{0,1},{1,0},{2,3},{3,2},{4,5},{5,4},{6,7},{7,6},{8,9},{9,8},{10,11... | collective-permute-start | bytes 614408 | tf_op jit(solution)/shard_map/ppermute | solution.py:738
  12.2 3.6 %collective-permute-start.4 = (f32[32,128]{1,0:T(8,128)S(1)}, f32[32,128]{1,0:T(8,128)S(1)}, u32[]{:S(2)}, u32[]{:S(2)}) collective-permute-start(f32[32,128]{1,0:T(8,128)S(1)} %get-tuple-element.39.column), channel_id=1, source_target_pairs={{0,2},{1,3},{2,0},{3,1},{4,6},{5,7},{6,4},{7,5},{8,10},{9,11},{10,... | collective-permute-start | bytes 49160 | tf_op jit(solution)/shard_map/ppermute | solution.py:729
  15.8 2.0 %shard_map.74 = (f32[4,4,32,256]{3,2,1,0:T(8,128)S(1)}, f32[47,8,128]{2,1,0:T(8,128)S(1)}) custom-call(f32[19]{0:T(128)S(1)} %copy-done.7, f32[32,512]{1,0:T(8,128)S(1)} %get-tuple-element.27.table), custom_call_target="tpu_custom_call" | custom-call | tf_op jit(solution)/shard_map/pallas_call | solution.py:780
  18.1 2.0 %collective-permute-done.4.refs_0_ = f32[32,128]{1,0:T(8,128)S(1)} collective-permute-done((f32[32,128]{1,0:T(8,128)S(1)}, f32[32,128]{1,0:T(8,128)S(1)}, u32[]{:S(2)}, u32[]{:S(2)}) %collective-permute-start.4) | collective-permute-done | bytes 16416 | tf_op jit(solution)/shard_map/ppermute | solution.py:729
  20.2 1.7 %shard_map.78 = (f32[19,2,56,256]{3,2,1,0:T(8,128)S(1)}, f32[4,2,40,256]{3,2,1,0:T(8,128)S(1)}, f32[176,256]{1,0:T(8,128)S(1)}, f32[176,256]{1,0:T(8,128)S(1)}) custom-call(f32[47,8,128]{2,1,0:T(8,128)S(1)} %get-tuple-element.28.entries, f32[4,4,32,256]{3,2,1,0:T(8,128)S(1)} %get-tuple-element.29.sums, f32[4,4,8,256]{3,2,1,0:T(8,128)S(1)} %get-tuple-element.37.outer_sums, ...), custom_call_target="tpu_custom_call" | custom-call | tf_op jit(solution)/shard_map/pallas_call | solution.py:800
  21.9 3.6 %collective-permute-start.5 = (f32[176,256]{1,0:T(8,128)S(1)}, f32[176,256]{1,0:T(8,128)S(1)}, u32[]{:S(2)}, u32[]{:S(2)}) collective-permute-start(f32[176,256]{1,0:T(8,128)S(1)} %get-tuple-element.43), channel_id=1, source_target_pairs={{0,4},{4,8},{8,12},{12,16},{16,20},{20,24},{24,28},{28,0},{1,5},{5... | collective-permute-start | bytes 540680 | tf_op jit(solution)/shard_map/ppermute | solution.py:729
  25.5 1.6 %shard_map.79 = (f32[19,2,56,256]{3,2,1,0:T(8,128)S(1)}, f32[4,2,40,256]{3,2,1,0:T(8,128)S(1)}) custom-call(f32[47,8,128]{2,1,0:T(8,128)S(1)} %get-tuple-element.28.entries, f32[4,4,32,256]{3,2,1,0:T(8,128)S(1)} %get-tuple-element.29.sums, f32[4,4,8,256]{3,2,1,0:T(8,128)S(1)} %get-tuple-element.37.outer_sums, f32[19,4,8,256]{3,2,1,0:T(8,128)S(1)} %get-tuple-element.38.outer, ...), custom_call_target="tpu_custom_call" | custom-call | tf_op jit(solution)/shard_map/pallas_call | solution.py:807
  27.1 1.1 %collective-permute-done.5.refs_0_ = f32[176,256]{1,0:T(8,128)S(1)} collective-permute-done((f32[176,256]{1,0:T(8,128)S(1)}, f32[176,256]{1,0:T(8,128)S(1)}, u32[]{:S(2)}, u32[]{:S(2)}) %collective-permute-start.5) | collective-permute-done | bytes 180256 | tf_op jit(solution)/shard_map/ppermute | solution.py:729
  28.2 3.2 %collective-permute-done.6.refs_1_ = f32[176,256]{1,0:T(8,128)S(1)} collective-permute-done((f32[176,256]{1,0:T(8,128)S(1)}, f32[176,256]{1,0:T(8,128)S(1)}, u32[]{:S(2)}, u32[]{:S(2)}) %collective-permute-start.6) | collective-permute-done | bytes 180256 | tf_op jit(solution)/shard_map/ppermute | solution.py:729
  31.4 1.4 %shard_map.80 = (f32[19,2,56,256]{3,2,1,0:T(8,128)S(1)}, f32[160,256]{1,0:T(8,128)S(1)}, f32[160,256]{1,0:T(8,128)S(1)}) custom-call(f32[47,8,128]{2,1,0:T(8,128)S(1)} %get-tuple-element.28.entries, f32[19,2,56,256]{3,2,1,0:T(8,128)S(1)} %get-tuple-element.40.ends, f32[19,2,56,256]{3,2,1,0:T(8,128)S(1)} %get-tuple-element.41.middle, ...), custom_call_target="tpu_custom_call" | custom-call | tf_op jit(solution)/shard_map/pallas_call | solution.py:816
  33.4 1.5 %shard_map.81.middle = f32[19,2,56,256]{3,2,1,0:T(8,128)S(1)} custom-call(f32[47,8,128]{2,1,0:T(8,128)S(1)} %get-tuple-element.28.entries, f32[19,2,56,256]{3,2,1,0:T(8,128)S(1)} %get-tuple-element.40.ends, f32[19,2,56,256]{3,2,1,0:T(8,128)S(1)} %get-tuple-element.41.middle, f32[4,2,40,256]{3,2,1,0:T(8,128)S(1)} %get-tuple-element.48.solid), custom_call_target="tpu_custom_call" | custom-call | tf_op jit(solution)/shard_map/pallas_call | solution.py:813
  34.9 1.5 %shard_map.82.given = f32[19,4,32,256]{3,2,1,0:T(8,128)} custom-call(f32[19,2,56,256]{3,2,1,0:T(8,128)S(1)} %get-tuple-element.45.ends, f32[19,2,56,256]{3,2,1,0:T(8,128)S(1)} %shard_map.81.middle), custom_call_target="tpu_custom_call" | custom-call | tf_op jit(solution)/shard_map/pallas_call | solution.py:820
  36.4 2.9 %collective-permute-done.8.message_ahead = f32[160,256]{1,0:T(8,128)S(1)} collective-permute-done((f32[160,256]{1,0:T(8,128)S(1)}, f32[160,256]{1,0:T(8,128)S(1)}, u32[]{:S(2)}, u32[]{:S(2)}) %collective-permute-start.8) | collective-permute-done | bytes 163872 | tf_op jit(solution)/shard_map/ppermute | solution.py:729
  39.3 0.8 %shard_map.83 = f32[19,4,32,256]{3,2,1,0:T(8,128)} custom-call(f32[19,2,56,256]{3,2,1,0:T(8,128)S(1)} %get-tuple-element.45.ends, f32[160,256]{1,0:T(8,128)S(1)} %collective-permute-done.7.message_behind, f32[160,256]{1,0:T(8,128)S(1)} %collective-permute-done.8.message_ahead, f32[19,4,32,256]{3,2,1,0:T(8,128)} %shard_map.82.given), custom_call_target="tpu_custom_call", output_to_operand_aliasing={{}: (3, {})} | custom-call | tf_op jit(solution)/shard_map/pallas_call | solution.py:828
  (21 shorter events, 1.5 us)
Async XLA Ops:
  0.0 15.8 %copy-start.7 = (f32[19]{0:T(128)S(1)}, f32[19]{0:T(128)}, u32[]{:S(2)}) copy-start(f32[19]{0:T(128)} %rates.1) | copy-start | bytes 232
  0.0 0.9 %copy-start.2 = (f32[27,512]{1,0:T(8,128)S(1)}, f32[27,512]{1,0:T(8,128)}, u32[]{:S(2)}) copy-start(f32[27,512]{1,0:T(8,128)} %fractions_in.1) | copy-start | bytes 165892
  0.9 0.7 %copy-start.3 = (f32[3,512]{1,0:T(4,128)S(1)}, f32[3,512]{1,0:T(4,128)}, u32[]{:S(2)}) copy-start(f32[3,512]{1,0:T(4,128)} %velocity_in.1) | copy-start | bytes 18436
  1.6 0.7 %copy-start.4 = (f32[3,512]{1,0:T(4,128)S(1)}, f32[3,512]{1,0:T(4,128)}, u32[]{:S(2)}) copy-start(f32[3,512]{1,0:T(4,128)} %change_in.1) | copy-start | bytes 18436
  2.3 0.7 %copy-start.5 = (s32[512]{0:T(512)S(1)}, s32[512]{0:T(512)}, u32[]{:S(2)}) copy-start(s32[512]{0:T(512)} %param.12) | copy-start | bytes 6148
  2.9 0.7 %copy-start.6 = (s32[512]{0:T(512)S(1)}, s32[512]{0:T(512)}, u32[]{:S(2)}) copy-start(s32[512]{0:T(512)} %param.13) | copy-start | bytes 6148
  4.4 5.1 %collective-permute-start = (f32[32,128]{1,0:T(8,128)S(1)}, f32[32,128]{1,0:T(8,128)S(1)}, u32[]{:S(2)}, u32[]{:S(2)}) collective-permute-start(f32[32,128]{1,0:T(8,128)S(1)} %get-tuple-element.31), channel_id=1, source_target_pairs={{0,4},{4,8},{8,12},{12,16},{16,20},{20,24},{24,28},{28,0},{1,5},{5... | collective-permute-start | bytes 49160 | tf_op jit(solution)/shard_map/ppermute | solution.py:729
  7.0 3.2 %collective-permute-start.1 = (f32[32,128]{1,0:T(8,128)S(1)}, f32[32,128]{1,0:T(8,128)S(1)}, u32[]{:S(2)}, u32[]{:S(2)}) collective-permute-start(f32[32,128]{1,0:T(8,128)S(1)} %get-tuple-element.32), channel_id=1, source_target_pairs={{0,28},{4,0},{8,4},{12,8},{16,12},{20,16},{24,20},{28,24},{1,29},{... | collective-permute-start | bytes 49160 | tf_op jit(solution)/shard_map/ppermute | solution.py:729
  7.0 1.7 %copy-start = (f32[19,4,32,256]{3,2,1,0:T(8,128)S(1)}, f32[19,4,32,256]{3,2,1,0:T(8,128)}, u32[]{:S(2)}) copy-start(f32[19,4,32,256]{3,2,1,0:T(8,128)} %populations.5) | copy-start | bytes 7471108
  8.7 11.5 %copy-start.1 = (f32[19,4,32,256]{3,2,1,0:T(8,128)S(1)}, f32[19,4,32,256]{3,2,1,0:T(8,128)}, u32[]{:S(2)}) copy-start(f32[19,4,32,256]{3,2,1,0:T(8,128)} %populations.5) | copy-start | bytes 7471108
  10.2 7.7 %collective-permute-start.2 = (f32[200,256]{1,0:T(8,128)S(1)}, f32[200,256]{1,0:T(8,128)S(1)}, u32[]{:S(2)}, u32[]{:S(2)}) collective-permute-start(f32[200,256]{1,0:T(8,128)S(1)} %get-tuple-element.35), channel_id=1, source_target_pairs={{0,1},{1,0},{2,3},{3,2},{4,5},{5,4},{6,7},{7,6},{8,9},{9,8},{10,11... | collective-permute-start | bytes 614408 | tf_op jit(solution)/shard_map/ppermute | solution.py:738
  11.5 6.4 %collective-permute-start.3 = (f32[200,256]{1,0:T(8,128)S(1)}, f32[200,256]{1,0:T(8,128)S(1)}, u32[]{:S(2)}, u32[]{:S(2)}) collective-permute-start(f32[200,256]{1,0:T(8,128)S(1)} %get-tuple-element.36), channel_id=1, source_target_pairs={{0,0},{1,2},{2,1},{3,3},{4,4},{5,6},{6,5},{7,7},{8,8},{9,10},{10,9... | collective-permute-start | bytes 614408 | tf_op jit(solution)/shard_map/ppermute | solution.py:738
  12.2 8.0 %collective-permute-start.4 = (f32[32,128]{1,0:T(8,128)S(1)}, f32[32,128]{1,0:T(8,128)S(1)}, u32[]{:S(2)}, u32[]{:S(2)}) collective-permute-start(f32[32,128]{1,0:T(8,128)S(1)} %get-tuple-element.39.column), channel_id=1, source_target_pairs={{0,2},{1,3},{2,0},{3,1},{4,6},{5,7},{6,4},{7,5},{8,10},{9,11},{10,... | collective-permute-start | bytes 49160 | tf_op jit(solution)/shard_map/ppermute | solution.py:729
  21.9 6.3 %collective-permute-start.5 = (f32[176,256]{1,0:T(8,128)S(1)}, f32[176,256]{1,0:T(8,128)S(1)}, u32[]{:S(2)}, u32[]{:S(2)}) collective-permute-start(f32[176,256]{1,0:T(8,128)S(1)} %get-tuple-element.43), channel_id=1, source_target_pairs={{0,4},{4,8},{8,12},{12,16},{16,20},{20,24},{24,28},{28,0},{1,5},{5... | collective-permute-start | bytes 540680 | tf_op jit(solution)/shard_map/ppermute | solution.py:729
  25.5 5.9 %collective-permute-start.6 = (f32[176,256]{1,0:T(8,128)S(1)}, f32[176,256]{1,0:T(8,128)S(1)}, u32[]{:S(2)}, u32[]{:S(2)}) collective-permute-start(f32[176,256]{1,0:T(8,128)S(1)} %get-tuple-element.44), channel_id=1, source_target_pairs={{0,28},{4,0},{8,4},{12,8},{16,12},{20,16},{24,20},{28,24},{1,29},{... | collective-permute-start | bytes 540680 | tf_op jit(solution)/shard_map/ppermute | solution.py:729
  32.8 3.6 %collective-permute-start.7 = (f32[160,256]{1,0:T(8,128)S(1)}, f32[160,256]{1,0:T(8,128)S(1)}, u32[]{:S(2)}, u32[]{:S(2)}) collective-permute-start(f32[160,256]{1,0:T(8,128)S(1)} %get-tuple-element.46), channel_id=1, source_target_pairs={{0,4},{4,8},{8,12},{12,16},{16,20},{20,24},{24,28},{28,0},{1,5},{5... | collective-permute-start | bytes 491528 | tf_op jit(solution)/shard_map/ppermute | solution.py:729
  32.9 6.4 %collective-permute-start.8 = (f32[160,256]{1,0:T(8,128)S(1)}, f32[160,256]{1,0:T(8,128)S(1)}, u32[]{:S(2)}, u32[]{:S(2)}) collective-permute-start(f32[160,256]{1,0:T(8,128)S(1)} %get-tuple-element.47), channel_id=1, source_target_pairs={{0,28},{4,0},{8,4},{12,8},{16,12},{20,16},{24,20},{28,24},{1,29},{... | collective-permute-start | bytes 491528 | tf_op jit(solution)/shard_map/ppermute | solution.py:729

commit v3 on v2

--- a/solution.py
+++ b/solution.py
@@ -380,7 +380,13 @@
     table[...] = jnp.where((iota((32, rows), 0) < 27) & (dest != 4), 0.0, payload)
 
 
-def edge_kernel(size_x, size_y, size_z, populations, table, one, two):
+def edge_kernel(size_x, size_y, size_z, populations, table, one, two, bottom, top, done):
+    copies = (
+        pltpu.make_async_copy(populations.at[:, :, 0:8, :], bottom, done.at[0]),
+        pltpu.make_async_copy(populations.at[:, :, size_y - 8 : size_y, :], top, done.at[1]),
+    )
+    for copy in copies:
+        copy.start()
     a_x, a_y, a_z = cells_of(table[30:31, :].astype(I32), size_y, size_z)
     rows = 2 * size_x
     index = iota((rows, 1), 0)
@@ -396,13 +402,15 @@
         8 * size_y,
     )
     first = 19 * rows
+    for copy in copies:
+        copy.wait()
 
     def write(down, up):
         for i in range(19):
             for x in range(size_x):
                 at = i * rows + 2 * x
-                down[at : at + 2, :] = populations[i, x, 0:2, :]
-                up[at : at + 2, :] = populations[i, x, size_y - 2 : size_y, :]
+                down[at : at + 2, :] = bottom[i, x, 0:2, :]
+                up[at : at + 2, :] = top[i, x, 6:8, :]
         down[first : first + 4 * rows, :] = sums[: 4 * rows]
         up[first : first + 4 * rows, :] = sums[4 * rows :]
 
@@ -449,7 +457,9 @@
             sums[c, x, :, :] = totals[at : at + size_y]
 
 
-def outer_kernel(size_x, size_z, one, two, sums, outer):
+def outer_kernel(size_x, size_y, size_z, count, shifts, column, one, two, *refs):
+    rest, (sums, outer, migrants) = refs[: len(shifts)], refs[len(shifts) :]
+    arrivals(size_x, size_y, size_z, count, shifts, column, one, two, rest, migrants)
     blank = jnp.zeros((8, size_z), F32)
     ones = jnp.ones((8, size_z), F32)
     rows = 2 * size_x
@@ -484,7 +494,8 @@
     return jnp.where((other >= 0) & (other < count), other, here + 2 * count)
 
 
-def arrivals(size_y, size_z, count, shifts, first, column, one, two, rest):
+def arrivals(size_x, size_y, size_z, count, shifts, column, one, two, rest, migrants):
+    first = 23 * 2 * size_x
     here = lax.axis_index("gy")
     fold = size_z // 128
     deep = 32 // fold
@@ -516,7 +527,10 @@
         offsets.append((offset + across) * size_y)
     table = jnp.concatenate(tables, axis=1)
     a_x, a_y, a_z = cells_of(table[30:31, :].astype(I32), size_y, size_z)
-    return table, a_x, a_y + jnp.concatenate(offsets, axis=1), a_z
+    migrants[0:32, :] = table
+    migrants[32:33, :] = a_x.astype(F32)
+    migrants[33:34, :] = (a_y + jnp.concatenate(offsets, axis=1)).astype(F32)
+    migrants[34:35, :] = a_z.astype(F32)
 
 
 def store_padded(target, i, x, tile, part, value, tiles):
@@ -535,12 +549,11 @@
 
 
 def first_kernel(
-    size_x, size_y, size_z, count, shifts, first, planes, entries, sums, outer_sums, outer,
-    populations, column, one, two, *refs
+    size_x, size_y, size_z, count, planes, entries, sums, outer_sums, outer, populations, migrants,
+    post, solid, *faces_out
 ):
-    rest, (post, solid), faces_out = refs[: len(shifts)], refs[len(shifts) : len(shifts) + 2], refs[len(shifts) + 2 :]
     tiles = size_y // 8
-    table, a_x, a_y, a_z = arrivals(size_y, size_z, count, shifts, first, column, one, two, rest)
+    a_x, a_y, a_z = (migrants[k : k + 1, :].astype(I32) for k in (32, 33, 34))
     wide = size_y + 8
     index = iota((len(planes) * wide, 1), 0)
     number = lax.div(index, jnp.int32(wide))
@@ -549,7 +562,7 @@
     rows_y = jnp.where(row < size_y + 2, row, jnp.where(row >= size_y + 6, row - wide, -3 * size_y))
     big = 4 * size_y * (count + 2)
     totals = deposited(
-        [(rows_x, rows_y)], table[0:27, :], table[27:30, :], a_x, a_y, a_z, size_z, big
+        [(rows_x, rows_y)], migrants[0:27, :], migrants[27:30, :], a_x, a_y, a_z, size_z, big
     )
     blocks = relax_blocks(entries)
     cells = len(planes) * wide
@@ -724,6 +737,10 @@
     )
 
 
+def in_hbm(value):
+    return pltpu.with_memory_space_constraint(value, pltpu.HBM)
+
+
 def around(value, axis, steps):
     count = lax.axis_size(axis)
     return lax.ppermute(value, axis, [(i, (i + steps) % count) for i in range(count)])
@@ -744,10 +761,10 @@
     rows = anchor.shape[0]
     sizes = (size_x, size_y, size_z)
     part = functools.partial
-    migrants = shape(32, 128)
+    packed = shape(32, 128)
     table, own, ahead, behind = call(
         pack_kernel,
-        (shape(32, rows), migrants, migrants, migrants),
+        (shape(32, rows), packed, packed, packed),
         8,
         [HBM] * 5,
         scratch=[
@@ -758,15 +775,21 @@
             pltpu.VMEM((1, rows), I32),
             pltpu.SemaphoreType.DMA((5,)),
         ],
-    )(velocity, velocity_change, fractions, anchor[None, :], destination[None, :])
+    )(*map(in_hbm, (velocity, velocity_change, fractions, anchor[None, :], destination[None, :])))
     from_behind, from_ahead = around(ahead, "gx", 1), around(behind, "gx", -1)
     first = 23 * 2 * size_x
     fold = size_z // 128
     message = shape(first + 32 // fold, size_z)
-    one, two = call(part(edge_kernel, *sizes), (message, message), 8, [VMEM] * 2)(populations, table)
+    one, two = call(
+        part(edge_kernel, *sizes),
+        (message, message),
+        8,
+        [HBM, VMEM],
+        scratch=[pltpu.VMEM((19, size_x, 8, size_z), F32)] * 2 + [pltpu.SemaphoreType.DMA((2,))],
+    )(in_hbm(populations), table)
     column, one, two = call(
         part(merge_kernel, first, fold),
-        (migrants, message, message),
+        (packed, message, message),
         8,
         [VMEM] * 5,
         aliases={3: 1, 4: 2},
@@ -780,12 +803,13 @@
     sums, entries = call(
         part(stay_kernel, *sizes), (shape(4, *sizes), shape(ENTRIES, 8, 128)), 16, [SMEM, VMEM]
     )(relax_rates, table)
-    outer_sums, outer = call(
-        part(outer_kernel, size_x, size_z),
-        (shape(4, size_x, 8, size_z), shape(19, size_x, 8, size_z)),
+    width = -(-(3 + len(shifts)) * LANES // 128) * 128
+    outer_sums, outer, migrants = call(
+        part(outer_kernel, *sizes, count, shifts),
+        (shape(4, size_x, 8, size_z), shape(19, size_x, 8, size_z), shape(40, width)),
         8,
-        [VMEM] * 2,
-    )(one, two)
+        [VMEM] * (3 + len(shifts)),
+    )(column, one, two, *rest)
 
     def padded(planes):
         return shape(19, planes, size_y + 24, size_z)
@@ -794,18 +818,18 @@
         return shape(4, planes, size_y + 8, size_z)
 
     outside, inside = (0, size_x - 1), tuple(range(1, size_x - 1))
-    known = (entries, sums, outer_sums, outer, populations, column, one, two, *rest)
+    known = (entries, sums, outer_sums, outer, populations, migrants)
     wide_face = shape((5 * size_y + 10 + 7) // 8 * 8, size_z)
     face = shape(5 * size_y, size_z)
     ends, solid_ends, ahead, behind = call(
-        part(first_kernel, *sizes, count, shifts, first, outside),
+        part(first_kernel, *sizes, count, outside),
         (padded(2), solids(2), wide_face, wide_face),
         16,
         [VMEM] * len(known),
     )(*known)
     from_behind, from_ahead = around(ahead, "gx", 1), around(behind, "gx", -1)
     middle, solid_middle = call(
-        part(first_kernel, *sizes, count, shifts, first, inside),
+        part(first_kernel, *sizes, count, inside),
         (padded(len(inside)), solids(len(inside))),
         16,
         [VMEM] * len(known),

time: 40.5 us -> 37.3 us (0.921)
  the two profiles are of different devices: /device:TPU:1 before, /device:TPU:3 now
where the time goes in v3:
time: 37.3 us; the launch traced here: 37.1 us
  Pallas kernels  13.9 us (37%)
  waiting for transfers between devices  12.1 us (32%)
  starting transfers between devices  11 us (29%)
    ppermute x7, waiting for transfers between devices, around(): lax.ppermute(value, axis, [(i, (i + steps) % count) for i in range(count)])  12.1 us
    ppermute x7, starting transfers between devices, around(): lax.ppermute(value, axis, [(i, (i + steps) % count) for i in range(count)])  8.96 us
    pallas_call x1, Pallas kernels, local(): call(part(stay_kernel, *sizes), (shape(4, *sizes), shape(ENTRIES, 8, 128)...  2.04 us
    ppermute x2, starting transfers between devices, paired(): return lax.ppermute(value, axis, pairs)  2.02 us
    pallas_call x1, Pallas kernels, local(): call(part(edge_kernel, *sizes), (message, message), 8, [HBM, VMEM], scrat...  1.78 us
    pallas_call x1, Pallas kernels, local(): call(pack_kernel, (shape(32, rows), packed, packed, packed), 8, [HBM] * 5...  1.69 us
    pallas_call x1, Pallas kernels, local(): call(part(first_kernel, *sizes, count, outside), (padded(2), solids(2), w...  1.53 us
    pallas_call x1, Pallas kernels, local(): call(part(last_kernel, *sizes, count), shape(19, *sizes), 16, [VMEM] * 2,...  1.5 us
  transfers between devices with their start and end apart: 9, of which 6 were waited for; matrix products, arithmetic and copies ran while one was open for 0% of the time, Pallas kernels for 22%

profile of v3, /device:TPU:3, one launch (start us, length us, event | category | flops | bytes accessed | tf_op | source)
XLA Modules:
  0.0 37.1 jit_solution(9222640885010123281)
XLA Ops:
  0.0 1.7 %shard_map.73 = (f32[32,512]{1,0:T(8,128)S(1)}, f32[32,128]{1,0:T(8,128)S(1)}, f32[32,128]{1,0:T(8,128)S(1)}, f32[32,128]{1,0:T(8,128)S(1)}) custom-call(f32[3,512]{1,0:T(4,128)} %velocity_in.1, f32[3,512]{1,0:T(4,128)} %change_in.1, f32[27,512]{1,0:T(8,128)} %fractions_in.1, s32[1,512]{1,0:T(1,128)} %bitcast.2, s32[1,512]{1,0:T(1,128)} %bitcast.3), custom_call_target="tpu_custom_call" | custom-call | tf_op jit(solution)/shard_map/pallas_call | solution.py:765
  1.7 1.8 %collective-permute-start = (f32[32,128]{1,0:T(8,128)S(1)}, f32[32,128]{1,0:T(8,128)S(1)}, u32[]{:S(2)}, u32[]{:S(2)}) collective-permute-start(f32[32,128]{1,0:T(8,128)S(1)} %get-tuple-element.32), channel_id=1, source_target_pairs={{0,4},{4,8},{8,12},{12,16},{16,20},{20,24},{24,28},{28,0},{1,5},{5... | collective-permute-start | bytes 49160 | tf_op jit(solution)/shard_map/ppermute | solution.py:746
  3.5 0.0 collective-permute-start.1
  3.5 1.8 %shard_map.75 = (f32[200,256]{1,0:T(8,128)S(1)}, f32[200,256]{1,0:T(8,128)S(1)}) custom-call(f32[19,4,32,256]{3,2,1,0:T(8,128)} %populations.5, f32[32,512]{1,0:T(8,128)S(1)} %get-tuple-element.28.table), custom_call_target="tpu_custom_call" | custom-call | tf_op jit(solution)/shard_map/pallas_call | solution.py:783
  5.3 2.3 %collective-permute-done.1.from_ahead = f32[32,128]{1,0:T(8,128)S(1)} collective-permute-done((f32[32,128]{1,0:T(8,128)S(1)}, f32[32,128]{1,0:T(8,128)S(1)}, u32[]{:S(2)}, u32[]{:S(2)}) %collective-permute-start.1) | collective-permute-done | bytes 16416 | tf_op jit(solution)/shard_map/ppermute | solution.py:746
  7.6 1.4 %collective-permute-start.2 = (f32[200,256]{1,0:T(8,128)S(1)}, f32[200,256]{1,0:T(8,128)S(1)}, u32[]{:S(2)}, u32[]{:S(2)}) collective-permute-start(f32[200,256]{1,0:T(8,128)S(1)} %get-tuple-element.37), channel_id=1, source_target_pairs={{0,1},{1,0},{2,3},{3,2},{4,5},{5,4},{6,7},{7,6},{8,9},{9,8},{10,11... | collective-permute-start | bytes 614408 | tf_op jit(solution)/shard_map/ppermute | solution.py:755
  9.0 0.7 %collective-permute-start.3 = (f32[200,256]{1,0:T(8,128)S(1)}, f32[200,256]{1,0:T(8,128)S(1)}, u32[]{:S(2)}, u32[]{:S(2)}) collective-permute-start(f32[200,256]{1,0:T(8,128)S(1)} %get-tuple-element.38), channel_id=1, source_target_pairs={{0,0},{1,2},{2,1},{3,3},{4,4},{5,6},{6,5},{7,7},{8,8},{9,10},{10,9... | collective-permute-start | bytes 614408 | tf_op jit(solution)/shard_map/ppermute | solution.py:755
  9.6 3.6 %collective-permute-start.4 = (f32[32,128]{1,0:T(8,128)S(1)}, f32[32,128]{1,0:T(8,128)S(1)}, u32[]{:S(2)}, u32[]{:S(2)}) collective-permute-start(f32[32,128]{1,0:T(8,128)S(1)} %get-tuple-element.36.column), channel_id=1, source_target_pairs={{0,2},{1,3},{2,0},{3,1},{4,6},{5,7},{6,4},{7,5},{8,10},{9,11},{10,... | collective-permute-start | bytes 49160 | tf_op jit(solution)/shard_map/ppermute | solution.py:746
  13.3 2.0 %shard_map.74 = (f32[4,4,32,256]{3,2,1,0:T(8,128)S(1)}, f32[47,8,128]{2,1,0:T(8,128)S(1)}) custom-call(f32[19]{0:T(128)S(1)} %copy-done.1, f32[32,512]{1,0:T(8,128)S(1)} %get-tuple-element.28.table), custom_call_target="tpu_custom_call" | custom-call | tf_op jit(solution)/shard_map/pallas_call | solution.py:803
  15.3 2.8 %collective-permute-done.4.refs_0_ = f32[32,128]{1,0:T(8,128)S(1)} collective-permute-done((f32[32,128]{1,0:T(8,128)S(1)}, f32[32,128]{1,0:T(8,128)S(1)}, u32[]{:S(2)}, u32[]{:S(2)}) %collective-permute-start.4) | collective-permute-done | bytes 16416 | tf_op jit(solution)/shard_map/ppermute | solution.py:746
  18.1 0.0 collective-permute-done.2.one
  18.1 0.3 shard_map.77
  18.4 1.5 %shard_map.78 = (f32[19,2,56,256]{3,2,1,0:T(8,128)S(1)}, f32[4,2,40,256]{3,2,1,0:T(8,128)S(1)}, f32[176,256]{1,0:T(8,128)S(1)}, f32[176,256]{1,0:T(8,128)S(1)}) custom-call(f32[47,8,128]{2,1,0:T(8,128)S(1)} %get-tuple-element.29.entries, f32[4,4,32,256]{3,2,1,0:T(8,128)S(1)} %get-tuple-element.30.sums, f32[4,4,8,256]{3,2,1,0:T(8,128)S(1)} %get-tuple-element.39.outer_sums, ...), custom_call_target="tpu_custom_call" | custom-call | tf_op jit(solution)/shard_map/pallas_call | solution.py:824
  19.9 2.1 %collective-permute-start.5 = (f32[176,256]{1,0:T(8,128)S(1)}, f32[176,256]{1,0:T(8,128)S(1)}, u32[]{:S(2)}, u32[]{:S(2)}) collective-permute-start(f32[176,256]{1,0:T(8,128)S(1)} %get-tuple-element.45), channel_id=1, source_target_pairs={{0,4},{4,8},{8,12},{12,16},{16,20},{20,24},{24,28},{28,0},{1,5},{5... | collective-permute-start | bytes 540680 | tf_op jit(solution)/shard_map/ppermute | solution.py:746
  22.0 1.4 %shard_map.79 = (f32[19,2,56,256]{3,2,1,0:T(8,128)S(1)}, f32[4,2,40,256]{3,2,1,0:T(8,128)S(1)}) custom-call(f32[47,8,128]{2,1,0:T(8,128)S(1)} %get-tuple-element.29.entries, f32[4,4,32,256]{3,2,1,0:T(8,128)S(1)} %get-tuple-element.30.sums, f32[4,4,8,256]{3,2,1,0:T(8,128)S(1)} %get-tuple-element.39.outer_sums, f32[19,4,8,256]{3,2,1,0:T(8,128)S(1)} %get-tuple-element.40.outer, ...), custom_call_target="tpu_custom_call" | custom-call | tf_op jit(solution)/shard_map/pallas_call | solution.py:831
  23.4 2.4 %collective-permute-done.5.refs_0_ = f32[176,256]{1,0:T(8,128)S(1)} collective-permute-done((f32[176,256]{1,0:T(8,128)S(1)}, f32[176,256]{1,0:T(8,128)S(1)}, u32[]{:S(2)}, u32[]{:S(2)}) %collective-permute-start.5) | collective-permute-done | bytes 180256 | tf_op jit(solution)/shard_map/ppermute | solution.py:746
  25.8 2.0 %collective-permute-done.6.refs_1_ = f32[176,256]{1,0:T(8,128)S(1)} collective-permute-done((f32[176,256]{1,0:T(8,128)S(1)}, f32[176,256]{1,0:T(8,128)S(1)}, u32[]{:S(2)}, u32[]{:S(2)}) %collective-permute-start.6) | collective-permute-done | bytes 180256 | tf_op jit(solution)/shard_map/ppermute | solution.py:746
  27.8 1.4 %shard_map.80 = (f32[19,2,56,256]{3,2,1,0:T(8,128)S(1)}, f32[160,256]{1,0:T(8,128)S(1)}, f32[160,256]{1,0:T(8,128)S(1)}) custom-call(f32[47,8,128]{2,1,0:T(8,128)S(1)} %get-tuple-element.29.entries, f32[19,2,56,256]{3,2,1,0:T(8,128)S(1)} %get-tuple-element.42.ends, f32[19,2,56,256]{3,2,1,0:T(8,128)S(1)} %get-tuple-element.43.middle, ...), custom_call_target="tpu_custom_call" | custom-call | tf_op jit(solution)/shard_map/pallas_call | solution.py:840
  29.2 1.4 %collective-permute-start.7 = (f32[160,256]{1,0:T(8,128)S(1)}, f32[160,256]{1,0:T(8,128)S(1)}, u32[]{:S(2)}, u32[]{:S(2)}) collective-permute-start(f32[160,256]{1,0:T(8,128)S(1)} %get-tuple-element.48), channel_id=1, source_target_pairs={{0,4},{4,8},{8,12},{12,16},{16,20},{20,24},{24,28},{28,0},{1,5},{5... | collective-permute-start | bytes 491528 | tf_op jit(solution)/shard_map/ppermute | solution.py:746
  30.7 1.5 %shard_map.81.middle = f32[19,2,56,256]{3,2,1,0:T(8,128)S(1)} custom-call(f32[47,8,128]{2,1,0:T(8,128)S(1)} %get-tuple-element.29.entries, f32[19,2,56,256]{3,2,1,0:T(8,128)S(1)} %get-tuple-element.42.ends, f32[19,2,56,256]{3,2,1,0:T(8,128)S(1)} %get-tuple-element.43.middle, f32[4,2,40,256]{3,2,1,0:T(8,128)S(1)} %get-tuple-element.50.solid), custom_call_target="tpu_custom_call" | custom-call | tf_op jit(solution)/shard_map/pallas_call | solution.py:837
  32.1 1.5 %shard_map.82.given = f32[19,4,32,256]{3,2,1,0:T(8,128)} custom-call(f32[19,2,56,256]{3,2,1,0:T(8,128)S(1)} %get-tuple-element.47.ends, f32[19,2,56,256]{3,2,1,0:T(8,128)S(1)} %shard_map.81.middle), custom_call_target="tpu_custom_call" | custom-call | tf_op jit(solution)/shard_map/pallas_call | solution.py:844
  33.7 0.3 collective-permute-done.7.message_behind
  34.0 2.3 %collective-permute-done.8.message_ahead = f32[160,256]{1,0:T(8,128)S(1)} collective-permute-done((f32[160,256]{1,0:T(8,128)S(1)}, f32[160,256]{1,0:T(8,128)S(1)}, u32[]{:S(2)}, u32[]{:S(2)}) %collective-permute-start.8) | collective-permute-done | bytes 163872 | tf_op jit(solution)/shard_map/ppermute | solution.py:746
  36.3 0.8 %shard_map.83 = f32[19,4,32,256]{3,2,1,0:T(8,128)} custom-call(f32[19,2,56,256]{3,2,1,0:T(8,128)S(1)} %get-tuple-element.47.ends, f32[160,256]{1,0:T(8,128)S(1)} %collective-permute-done.7.message_behind, f32[160,256]{1,0:T(8,128)S(1)} %collective-permute-done.8.message_ahead, f32[19,4,32,256]{3,2,1,0:T(8,128)} %shard_map.82.given), custom_call_target="tpu_custom_call", output_to_operand_aliasing={{}: (3, {})} | custom-call | tf_op jit(solution)/shard_map/pallas_call | solution.py:852
  (9 shorter events, 0.0 us)
Async XLA Ops:
  0.0 18.3 %copy-start = (f32[19,4,32,256]{3,2,1,0:T(8,128)S(1)}, f32[19,4,32,256]{3,2,1,0:T(8,128)}, u32[]{:S(2)}) copy-start(f32[19,4,32,256]{3,2,1,0:T(8,128)} %populations.5) | copy-start | bytes 7471108
  0.0 13.2 %copy-start.1 = (f32[19]{0:T(128)S(1)}, f32[19]{0:T(128)}, u32[]{:S(2)}) copy-start(f32[19]{0:T(128)} %rates.1) | copy-start | bytes 232
  1.7 3.6 %collective-permute-start = (f32[32,128]{1,0:T(8,128)S(1)}, f32[32,128]{1,0:T(8,128)S(1)}, u32[]{:S(2)}, u32[]{:S(2)}) collective-permute-start(f32[32,128]{1,0:T(8,128)S(1)} %get-tuple-element.32), channel_id=1, source_target_pairs={{0,4},{4,8},{8,12},{12,16},{16,20},{20,24},{24,28},{28,0},{1,5},{5... | collective-permute-start | bytes 49160 | tf_op jit(solution)/shard_map/ppermute | solution.py:746
  3.5 4.1 %collective-permute-start.1 = (f32[32,128]{1,0:T(8,128)S(1)}, f32[32,128]{1,0:T(8,128)S(1)}, u32[]{:S(2)}, u32[]{:S(2)}) collective-permute-start(f32[32,128]{1,0:T(8,128)S(1)} %get-tuple-element.33), channel_id=1, source_target_pairs={{0,28},{4,0},{8,4},{12,8},{16,12},{20,16},{24,20},{28,24},{1,29},{... | collective-permute-start | bytes 49160 | tf_op jit(solution)/shard_map/ppermute | solution.py:746
  7.6 10.5 %collective-permute-start.2 = (f32[200,256]{1,0:T(8,128)S(1)}, f32[200,256]{1,0:T(8,128)S(1)}, u32[]{:S(2)}, u32[]{:S(2)}) collective-permute-start(f32[200,256]{1,0:T(8,128)S(1)} %get-tuple-element.37), channel_id=1, source_target_pairs={{0,1},{1,0},{2,3},{3,2},{4,5},{5,4},{6,7},{7,6},{8,9},{9,8},{10,11... | collective-permute-start | bytes 614408 | tf_op jit(solution)/shard_map/ppermute | solution.py:755
  9.0 9.1 %collective-permute-start.3 = (f32[200,256]{1,0:T(8,128)S(1)}, f32[200,256]{1,0:T(8,128)S(1)}, u32[]{:S(2)}, u32[]{:S(2)}) collective-permute-start(f32[200,256]{1,0:T(8,128)S(1)} %get-tuple-element.38), channel_id=1, source_target_pairs={{0,0},{1,2},{2,1},{3,3},{4,4},{5,6},{6,5},{7,7},{8,8},{9,10},{10,9... | collective-permute-start | bytes 614408 | tf_op jit(solution)/shard_map/ppermute | solution.py:755
  9.6 8.4 %collective-permute-start.4 = (f32[32,128]{1,0:T(8,128)S(1)}, f32[32,128]{1,0:T(8,128)S(1)}, u32[]{:S(2)}, u32[]{:S(2)}) collective-permute-start(f32[32,128]{1,0:T(8,128)S(1)} %get-tuple-element.36.column), channel_id=1, source_target_pairs={{0,2},{1,3},{2,0},{3,1},{4,6},{5,7},{6,4},{7,5},{8,10},{9,11},{10,... | collective-permute-start | bytes 49160 | tf_op jit(solution)/shard_map/ppermute | solution.py:746
  19.9 5.9 %collective-permute-start.5 = (f32[176,256]{1,0:T(8,128)S(1)}, f32[176,256]{1,0:T(8,128)S(1)}, u32[]{:S(2)}, u32[]{:S(2)}) collective-permute-start(f32[176,256]{1,0:T(8,128)S(1)} %get-tuple-element.45), channel_id=1, source_target_pairs={{0,4},{4,8},{8,12},{12,16},{16,20},{20,24},{24,28},{28,0},{1,5},{5... | collective-permute-start | bytes 540680 | tf_op jit(solution)/shard_map/ppermute | solution.py:746
  22.0 5.8 %collective-permute-start.6 = (f32[176,256]{1,0:T(8,128)S(1)}, f32[176,256]{1,0:T(8,128)S(1)}, u32[]{:S(2)}, u32[]{:S(2)}) collective-permute-start(f32[176,256]{1,0:T(8,128)S(1)} %get-tuple-element.46), channel_id=1, source_target_pairs={{0,28},{4,0},{8,4},{12,8},{16,12},{20,16},{24,20},{28,24},{1,29},{... | collective-permute-start | bytes 540680 | tf_op jit(solution)/shard_map/ppermute | solution.py:746
  29.2 4.8 %collective-permute-start.7 = (f32[160,256]{1,0:T(8,128)S(1)}, f32[160,256]{1,0:T(8,128)S(1)}, u32[]{:S(2)}, u32[]{:S(2)}) collective-permute-start(f32[160,256]{1,0:T(8,128)S(1)} %get-tuple-element.48), channel_id=1, source_target_pairs={{0,4},{4,8},{8,12},{12,16},{16,20},{20,24},{24,28},{28,0},{1,5},{5... | collective-permute-start | bytes 491528 | tf_op jit(solution)/shard_map/ppermute | solution.py:746
  30.7 5.6 %collective-permute-start.8 = (f32[160,256]{1,0:T(8,128)S(1)}, f32[160,256]{1,0:T(8,128)S(1)}, u32[]{:S(2)}, u32[]{:S(2)}) collective-permute-start(f32[160,256]{1,0:T(8,128)S(1)} %get-tuple-element.49), channel_id=1, source_target_pairs={{0,28},{4,0},{8,4},{12,8},{16,12},{20,16},{24,20},{28,24},{1,29},{... | collective-permute-start | bytes 491528 | tf_op jit(solution)/shard_map/ppermute | solution.py:746

commit v4 on v3

--- a/solution.py
+++ b/solution.py
@@ -68,6 +68,8 @@
 VEC, WEIGHTS, OPP, BASIS = lattice()
 FORWARD = [i for i in range(19) if VEC[i][0] == 1]
 BACKWARD = [i for i in range(19) if VEC[i][0] == -1]
+DOWNWARD = [i for i in range(19) if VEC[i][1] == -1]
+UPWARD = [OPP[i] for i in DOWNWARD]
 
 
 def symmetric_blocks():
@@ -138,12 +140,14 @@
                 at += 1
 
 
-def relax_blocks(table):
+def relax_blocks(table, lanes=128):
     blocks, at = [], 0
     for block in RELAX:
         rows = []
         for row in block:
-            rows.append([table[at + k] for k in range(len(row))])
+            rows.append(
+                [jnp.concatenate([table[at + k]] * (lanes // 128), axis=1) for k in range(len(row))]
+            )
             at += len(row)
         blocks.append(rows)
     return blocks
@@ -266,6 +270,47 @@
     return out
 
 
+def equilibrium(density, flow, numbers):
+    v_x, v_y, v_z = flow
+    rest = 1.0 - 1.5 * (v_x * v_x + v_y * v_y + v_z * v_z)
+    out = {}
+    for i in numbers:
+        if i in out:
+            continue
+        along = None
+        for sign, v in zip(VEC[i], flow):
+            if sign:
+                part = v if sign == 1 else -v
+                along = part if along is None else along + part
+        if along is None:
+            out[i] = rest
+        else:
+            along = 3.0 * along
+            even = rest + 0.5 * along * along
+            out[i], out[OPP[i]] = even + along, even - along
+    return out
+
+
+def fluid_parts(h, blocks, numbers):
+    zero = jnp.zeros_like(h[0])
+    relaxed = collide(h, zero, zero, zero, zero, blocks)
+    density, flow = zero, [zero, zero, zero]
+    for i in range(19):
+        part = np.float32(WEIGHTS[i]) * h[i]
+        density = density + part
+        for k in range(3):
+            if VEC[i][k]:
+                flow[k] = flow[k] + part if VEC[i][k] == 1 else flow[k] - part
+    inverse = 1.0 / density
+    still = equilibrium(density, [f * inverse for f in flow], numbers)
+    bounced = [h[OPP[i]] - density * still[OPP[i]] for i in numbers]
+    return [relaxed[i] for i in numbers], bounced, density
+
+
+def blended(relaxed, bounced, density, share, still):
+    return relaxed + share * ((bounced + density * still) - relaxed)
+
+
 def iota(shape, dim):
     return lax.broadcasted_iota(I32, shape, dim)
 
@@ -310,16 +355,23 @@
     return totals
 
 
+def even_x():
+    return lax.rem(lax.axis_index("gx"), 2) == 0
+
+
 def pack_kernel(
     velocity_in,
     change_in,
     fractions_in,
     anchor_in,
     destination_in,
+    populations,
     table,
     own,
-    ahead,
-    behind,
+    near,
+    far,
+    bottom,
+    top,
     velocity,
     change,
     fractions,
@@ -333,13 +385,15 @@
         (change_in, change),
         (fractions_in, fractions),
         (anchor_in, anchor),
+        (populations.at[:, :, 0:8, :], bottom),
+        (populations.at[:, :, populations.shape[2] - 8 :, :], top),
     )
     copies = [pltpu.make_async_copy(a, b, done.at[k]) for k, (a, b) in enumerate(pairs)]
     for copy in copies:
         copy.start()
     rows = destination.shape[1]
     order = jnp.where(iota((128, 128), 0) <= iota((128, 128), 1), 1.0, 0.0).astype(BF16)
-    for copy in copies:
+    for copy in copies[:5]:
         copy.wait()
     dest = destination[...]
     kinds = iota((16, rows), 0)
@@ -375,18 +429,24 @@
     packed = dot_t(high, chosen) + dot_t(middle, chosen) + dot_t(low, chosen)
     lane = iota((32, 128), 1)
     own[...] = jnp.where(lane < 2 * CAP, packed, 0.0)
-    ahead[...] = jnp.where((lane >= 2 * CAP) & (lane < 5 * CAP), packed, 0.0)
-    behind[...] = jnp.where(lane >= 5 * CAP, packed, 0.0)
+    ahead = jnp.where((lane >= 2 * CAP) & (lane < 5 * CAP), packed, 0.0)
+    behind = jnp.where(lane >= 5 * CAP, packed, 0.0)
+    even = even_x()
+    near[...] = jnp.where(even, ahead, behind)
+    far[...] = jnp.where(even, behind, ahead)
     table[...] = jnp.where((iota((32, rows), 0) < 27) & (dest != 4), 0.0, payload)
-
-
-def edge_kernel(size_x, size_y, size_z, populations, table, one, two, bottom, top, done):
-    copies = (
-        pltpu.make_async_copy(populations.at[:, :, 0:8, :], bottom, done.at[0]),
-        pltpu.make_async_copy(populations.at[:, :, size_y - 8 : size_y, :], top, done.at[1]),
-    )
-    for copy in copies:
-        copy.start()
+    for copy in copies[5:]:
+        copy.wait()
+
+
+def edge_rows(size_x):
+    starts = [0]
+    for rows in (19 * size_x, 4 * 2 * size_x, 11 * size_x):
+        starts.append(starts[-1] + rows)
+    return starts
+
+
+def edge_kernel(size_x, size_y, size_z, bottom, top, table, entries, one, two, held):
     a_x, a_y, a_z = cells_of(table[30:31, :].astype(I32), size_y, size_z)
     rows = 2 * size_x
     index = iota((rows, 1), 0)
@@ -401,18 +461,27 @@
         size_z,
         8 * size_y,
     )
-    first = 19 * rows
-    for copy in copies:
-        copy.wait()
+    _, at_sums, at_second, _ = edge_rows(size_x)
+    for i in range(19):
+        for x in range(size_x):
+            held[i, x : x + 1, :] = bottom[i, x, 1:2, :]
+            held[i, size_x + x : size_x + x + 1, :] = top[i, x, 6:7, :]
+    second = fluid_parts([held[i] for i in range(19)], relax_blocks(entries, size_z), DOWNWARD + UPWARD)
+    relaxed, bounced, density = second
 
     def write(down, up):
         for i in range(19):
             for x in range(size_x):
-                at = i * rows + 2 * x
-                down[at : at + 2, :] = bottom[i, x, 0:2, :]
-                up[at : at + 2, :] = top[i, x, 6:8, :]
-        down[first : first + 4 * rows, :] = sums[: 4 * rows]
-        up[first : first + 4 * rows, :] = sums[4 * rows :]
+                at = i * size_x + x
+                down[at : at + 1, :] = bottom[i, x, 0:1, :]
+                up[at : at + 1, :] = top[i, x, 7:8, :]
+        down[at_sums : at_sums + 4 * rows, :] = sums[: 4 * rows]
+        up[at_sums : at_sums + 4 * rows, :] = sums[4 * rows :]
+        for target, own, at_row in ((down, 0, 0), (up, 5, size_x)):
+            parts = relaxed[own : own + 5] + bounced[own : own + 5] + [density]
+            for k, value in enumerate(parts):
+                at = at_second + k * size_x
+                target[at : at + size_x, :] = value[at_row : at_row + size_x]
 
     even = lax.rem(lax.axis_index("gy"), 2) == 0
 
@@ -425,18 +494,42 @@
         write(one, two)
 
 
-def merge_kernel(first, fold, own, from_behind, from_ahead, one_in, two_in, column, one, two):
+def folded(table):
+    return sum(
+        table[8 * k : 8 * k + 8] if k == 0 else pltpu.roll(table[8 * k : 8 * k + 8], LANES * k, 1)
+        for k in range(4)
+    )
+
+
+def merge_kernel(first, fold, own, far, near, one_in, two_in, column, one, two):
     del one_in, two_in
-    merged = own[...] + from_behind[...] + from_ahead[...]
+    merged = folded(own[...] + near[...] + far[...])
     column[...] = merged
-    deep = 32 // fold
+    deep = 8 // fold
     for k in range(fold):
         for target in (one, two):
             target[first : first + deep, 128 * k : 128 * k + 128] = merged[deep * k : deep * k + deep]
 
 
-def stay_kernel(size_x, size_y, size_z, rates, table, sums, entries):
+def relax_kernel(rates, entries):
     relax_rows(rates, entries)
+
+
+def fluid_kernel(size_x, size_y, size_z, entries, populations, relaxed, bounced, density):
+    blocks = relax_blocks(entries)
+    for p, x in enumerate((0, size_x - 1)):
+        for tile in range(size_y // 8):
+            rows = slice(8 * tile, 8 * tile + 8)
+            for part in range(size_z // 128):
+                lanes = slice(128 * part, 128 * part + 128)
+                f, b, d = fluid_parts([populations[i, x, rows, lanes] for i in range(19)], blocks, range(19))
+                for i in range(19):
+                    relaxed[i, p, rows, lanes] = f[i]
+                    bounced[i, p, rows, lanes] = b[i]
+                density[p, rows, lanes] = d
+
+
+def stay_kernel(size_x, size_y, size_z, table, sums):
     a_x, a_y, a_z = cells_of(table[30:31, :].astype(I32), size_y, size_z)
     index = iota((size_x * size_y, 1), 0)
     rows_x = lax.div(index, jnp.int32(size_y))
@@ -457,26 +550,32 @@
             sums[c, x, :, :] = totals[at : at + size_y]
 
 
-def outer_kernel(size_x, size_y, size_z, count, shifts, column, one, two, *refs):
-    rest, (sums, outer, migrants) = refs[: len(shifts)], refs[len(shifts) :]
+def outer_kernel(size_x, size_y, size_z, count, shifts, column, *refs):
+    rest, (two, one, sums, outer, second, migrants) = refs[: len(shifts)], refs[len(shifts) :]
     arrivals(size_x, size_y, size_z, count, shifts, column, one, two, rest, migrants)
     blank = jnp.zeros((8, size_z), F32)
     ones = jnp.ones((8, size_z), F32)
-    rows = 2 * size_x
+    _, at_sums, at_second, _ = edge_rows(size_x)
 
     def write(above, below):
         for c in range(4):
             for x in range(size_x):
-                at = (19 + c) * rows + 2 * x
+                at = at_sums + c * 2 * size_x + 2 * x
                 sums[c, x, :, :] = blank
                 sums[c, x, 0:2, :] = above[at : at + 2, :]
                 sums[c, x, 6:8, :] = below[at : at + 2, :]
         for i in range(19):
             for x in range(size_x):
-                at = i * rows + 2 * x
+                at = i * size_x + x
                 outer[i, x, :, :] = ones
-                outer[i, x, 0:2, :] = above[at : at + 2, :]
-                outer[i, x, 6:8, :] = below[at : at + 2, :]
+                outer[i, x, 0:1, :] = above[at : at + 1, :]
+                outer[i, x, 7:8, :] = below[at : at + 1, :]
+        for k in range(11):
+            for x in range(size_x):
+                at = at_second + k * size_x + x
+                second[k, x, :, :] = ones
+                second[k, x, 1:2, :] = above[at : at + 1, :]
+                second[k, x, 6:7, :] = below[at : at + 1, :]
 
     even = lax.rem(lax.axis_index("gy"), 2) == 0
 
@@ -495,17 +594,17 @@
 
 
 def arrivals(size_x, size_y, size_z, count, shifts, column, one, two, rest, migrants):
-    first = 23 * 2 * size_x
+    first = edge_rows(size_x)[-1]
     here = lax.axis_index("gy")
     fold = size_z // 128
-    deep = 32 // fold
-
-    def unfolded(message):
+    deep = 8 // fold
+
+    def gathered(message):
         return jnp.concatenate(
             [message[first : first + deep, 128 * k : 128 * k + 128] for k in range(fold)], axis=0
         )
 
-    parts = [column[...], unfolded(one), unfolded(two)] + [r[...] for r in rest]
+    parts = [column[...], gathered(one), gathered(two)] + [r[...] for r in rest]
     sources = [here, pair_source(here, 0, count), pair_source(here, 1, count)]
     sources += [lax.rem(here - shift + 2 * count, count) for shift in shifts]
     lane = iota((1, 128), 1)
@@ -517,13 +616,15 @@
     per_group = 128 // LANES
     tables, offsets = [], []
     for start in range(0, len(parts), per_group):
-        table = None
+        blocks = [jnp.zeros((8, 128), F32)] * 4
         offset = jnp.full((1, 128), 2 * count, I32)
         for k, part in enumerate(parts[start : start + per_group]):
-            part = part if k == 0 else pltpu.roll(part, k * LANES, 1)
-            table = part if table is None else table + part
+            place = lax.div(lane, jnp.int32(LANES)) == k
+            for q in range(4):
+                turn = LANES * (k - q) % 128
+                blocks[q] = jnp.where(place, part if turn == 0 else pltpu.roll(part, turn, 1), blocks[q])
             offset = jnp.where(lax.div(lane, jnp.int32(LANES)) == k, sources[start + k] - here, offset)
-        tables.append(table)
+        tables.append(jnp.concatenate(blocks, axis=0))
         offsets.append((offset + across) * size_y)
     table = jnp.concatenate(tables, axis=1)
     a_x, a_y, a_z = cells_of(table[30:31, :].astype(I32), size_y, size_z)
@@ -549,9 +650,10 @@
 
 
 def first_kernel(
-    size_x, size_y, size_z, count, planes, entries, sums, outer_sums, outer, populations, migrants,
-    post, solid, *faces_out
+    size_x, size_y, size_z, count, planes, entries, sums, outer_sums, outer, second, migrants, *refs
 ):
+    prepared = planes[0] == 0
+    given, (post, solid, *faces_out) = (refs[:3], refs[3:]) if prepared else (refs[:1], refs[1:])
     tiles = size_y // 8
     a_x, a_y, a_z = (migrants[k : k + 1, :].astype(I32) for k in (32, 33, 34))
     wide = size_y + 8
@@ -583,13 +685,43 @@
                     solid[c, p, rows, lanes] = value
                 if tile == tiles:
                     h = [outer[i, x, :, lanes] for i in range(19)]
+                    out = collide(h, share, *flow, blocks)
+                    line = iota((8, 128), 0)
+                    away = jnp.where(line < 4, 1.0, -1.0)
+                    still = equilibrium(None, [away * v for v in flow], DOWNWARD)
+                    density = second[10, x, :, lanes]
+                    for k, (i, j) in enumerate(zip(DOWNWARD, UPWARD)):
+                        parts = (second[k, x, :, lanes], second[5 + k, x, :, lanes], density)
+                        value = blended(*parts, share, still[i])
+                        out[i] = jnp.where(line == 1, value, out[i])
+                        out[j] = jnp.where(line == 6, value, out[j])
+                elif prepared:
+                    relaxed, bounced, dense = given
+                    still = equilibrium(None, flow, range(19))
+                    density = dense[p, rows, lanes]
+                    out = [
+                        blended(relaxed[i, p, rows, lanes], bounced[i, p, rows, lanes], density, share, still[i])
+                        for i in range(19)
+                    ]
                 else:
-                    h = [populations[i, x, rows, lanes] for i in range(19)]
-                out = collide(h, share, *flow, blocks)
+                    h = [given[0][i, x, rows, lanes] for i in range(19)]
+                    out = collide(h, share, *flow, blocks)
                 for i in range(19):
                     store_padded(post, i, p, tile, part, out[i], tiles)
     if faces_out:
-        faces(post, *faces_out, size_y, size_z, True)
+        send_faces(post, *faces_out, size_y, size_z, True)
+
+
+def send_faces(post, near, far, size_y, size_z, outer):
+    even = even_x()
+
+    @pl.when(even)
+    def _():
+        faces(post, near, far, size_y, size_z, outer)
+
+    @pl.when(jnp.logical_not(even))
+    def _():
+        faces(post, far, near, size_y, size_z, outer)
 
 
 def faces(post, ahead, behind, size_y, size_z, outer):
@@ -609,7 +741,7 @@
                 target[to + 1 : to + 2, :] = value[7:8]
 
 
-def streamed(ends, middle, message_behind, message_ahead, i, x, tile, size_x, size_y, size_z, walls):
+def streamed(ends, middle, messages, i, x, tile, size_x, size_y, size_z, walls):
     tiles = size_y // 8
     row = iota((8, size_z), 0)
     c_x, c_y, c_z = VEC[i]
@@ -627,14 +759,18 @@
         at = 8 + 8 * tile - c_y
         value = turned(source[i, p, at : at + 8, :], c_z, size_z)
     else:
-        message, numbers = (message_behind, FORWARD) if from_x < 0 else (message_ahead, BACKWARD)
+        near, far, even = messages
+        from_near, numbers = (jnp.logical_not(even), FORWARD) if from_x < 0 else (even, BACKWARD)
         k = numbers.index(i)
+
+        def received(at, rows):
+            return jnp.where(from_near, near[at : at + rows, :], far[at : at + rows, :])
+
         if tile < tiles:
-            at = k * size_y + 8 * tile
-            value = message[at : at + 8, :]
+            value = received(k * size_y + 8 * tile, 8)
         else:
             at = 5 * size_y + 2 * k
-            value = jnp.where(row < 4, message[at : at + 1, :], message[at + 1 : at + 2, :])
+            value = jnp.where(row < 4, received(at, 1), received(at + 1, 1))
     source, p = plane(x)
     if c_y == 1 and tile == 0:
         value = jnp.where((row == 0) & walls[0], source[OPP[i], p, 8:16, :], value)
@@ -651,7 +787,7 @@
 
 def second_kernel(size_x, size_y, size_z, count, planes, entries, ends, middle, solid, *refs):
     refs = list(refs)
-    message_behind, message_ahead = (refs.pop(0), refs.pop(0)) if planes[0] == 0 else (None, None)
+    messages = (refs.pop(1), refs.pop(0), even_x()) if planes[0] == 0 else None
     later, faces_out = refs[0], refs[1:]
     tiles = size_y // 8
     walls = walls_of(count)
@@ -661,7 +797,7 @@
             rows = slice(8 * tile, 8 * tile + 8)
             h = [
                 streamed(
-                    ends, middle, message_behind, message_ahead, i, x, tile, size_x, size_y, size_z, walls
+                    ends, middle, messages, i, x, tile, size_x, size_y, size_z, walls
                 )
                 for i in range(19)
             ]
@@ -672,7 +808,7 @@
                 for i in range(19):
                     store_padded(later, i, p, tile, part, out[i], tiles)
     if faces_out:
-        faces(later, *faces_out, size_y, size_z, False)
+        send_faces(later, *faces_out, size_y, size_z, False)
 
 
 def last_kernel(size_x, size_y, size_z, count, ends, middle, advanced, held, done):
@@ -684,7 +820,7 @@
                 continue
             for tile in range(size_y // 8):
                 held[i, x, 8 * tile : 8 * tile + 8, :] = streamed(
-                    ends, middle, None, None, i, x, tile, size_x, size_y, size_z, walls
+                    ends, middle, None, i, x, tile, size_x, size_y, size_z, walls
                 )
         low, high = max(0, VEC[i][0]), size_x + min(0, VEC[i][0])
         copy = pltpu.make_async_copy(
@@ -697,9 +833,10 @@
 
 
 def enter_kernel(
-    size_x, size_y, size_z, count, ends, message_behind, message_ahead, given, advanced, held, done
+    size_x, size_y, size_z, count, ends, far, near, given, advanced, held, done
 ):
     del given
+    messages = (near, far, even_x())
     walls = walls_of(count)
     copies = []
     for x, numbers in ((0, FORWARD), (size_x - 1, BACKWARD)):
@@ -707,7 +844,7 @@
             k = len(copies)
             for tile in range(size_y // 8):
                 held[k, 8 * tile : 8 * tile + 8, :] = streamed(
-                    ends, None, message_behind, message_ahead, i, x, tile, size_x, size_y, size_z, walls
+                    ends, None, messages, i, x, tile, size_x, size_y, size_z, walls
                 )
             copy = pltpu.make_async_copy(held.at[k], advanced.at[i, x], done.at[k])
             copy.start()
@@ -746,13 +883,21 @@
     return lax.ppermute(value, axis, [(i, (i + steps) % count) for i in range(count)])
 
 
-def paired(value, axis, parity):
+def paired(value, axis, parity, wrap=False):
     count = lax.axis_size(axis)
+    if wrap and count % 2:
+        raise ValueError("odd ring")
     pairs = []
     for i in range(count):
         other = i + 1 if i % 2 == parity else i - 1
+        other = other % count if wrap else other
         pairs.append((i, other if 0 <= other < count else i))
     return lax.ppermute(value, axis, pairs)
+
+
+def exchanged(near, far):
+    far = paired(far, "gx", 1, True)
+    return paired(near, "gx", 0, True), far
 
 
 def local(populations, relax_rates, velocity, velocity_change, fractions, anchor, destination):
@@ -762,54 +907,63 @@
     sizes = (size_x, size_y, size_z)
     part = functools.partial
     packed = shape(32, 128)
-    table, own, ahead, behind = call(
+    band = shape(19, size_x, 8, size_z)
+    table, own, near, far, bottom, top = call(
         pack_kernel,
-        (shape(32, rows), packed, packed, packed),
+        (shape(32, rows), packed, packed, packed, band, band),
         8,
-        [HBM] * 5,
+        [HBM] * 6,
         scratch=[
             pltpu.VMEM((3, rows), F32),
             pltpu.VMEM((3, rows), F32),
             pltpu.VMEM((27, rows), F32),
             pltpu.VMEM((1, rows), I32),
             pltpu.VMEM((1, rows), I32),
-            pltpu.SemaphoreType.DMA((5,)),
+            pltpu.SemaphoreType.DMA((7,)),
         ],
-    )(*map(in_hbm, (velocity, velocity_change, fractions, anchor[None, :], destination[None, :])))
-    from_behind, from_ahead = around(ahead, "gx", 1), around(behind, "gx", -1)
-    first = 23 * 2 * size_x
+    )(*map(in_hbm, (velocity, velocity_change, fractions, anchor[None, :], destination[None, :], populations)))
+    near, far = exchanged(near, far)
+    first = edge_rows(size_x)[-1]
     fold = size_z // 128
-    message = shape(first + 32 // fold, size_z)
+    message = shape(-(-(first + 8 // fold) // 8) * 8, size_z)
+    entries = call(relax_kernel, shape(ENTRIES, 8, 128), 8, [SMEM])(relax_rates)
     one, two = call(
         part(edge_kernel, *sizes),
         (message, message),
         8,
-        [HBM, VMEM],
-        scratch=[pltpu.VMEM((19, size_x, 8, size_z), F32)] * 2 + [pltpu.SemaphoreType.DMA((2,))],
-    )(in_hbm(populations), table)
+        [VMEM] * 4,
+        scratch=[pltpu.VMEM((19, 2 * size_x, size_z), F32)],
+    )(bottom, top, table, entries)
     column, one, two = call(
         part(merge_kernel, first, fold),
-        (packed, message, message),
+        (shape(8, 128), message, message),
         8,
         [VMEM] * 5,
         aliases={3: 1, 4: 2},
-    )(own, from_behind, from_ahead, one, two)
+    )(own, far, near, one, two)
     shifts = []
     for shift in (2, -2):
         if shift % count > 1 and all((shift - other) % count for other in shifts):
             shifts.append(shift)
     rest = [around(column, "gy", shift) for shift in shifts]
     one, two = paired(one, "gy", 0), paired(two, "gy", 1)
-    sums, entries = call(
-        part(stay_kernel, *sizes), (shape(4, *sizes), shape(ENTRIES, 8, 128)), 16, [SMEM, VMEM]
-    )(relax_rates, table)
+    sums = call(part(stay_kernel, *sizes), shape(4, *sizes), 16, [VMEM])(table)
+    plane_pair = shape(19, 2, size_y, size_z)
+    parts = call(
+        part(fluid_kernel, *sizes), (plane_pair, plane_pair, shape(2, size_y, size_z)), 16, [VMEM] * 2
+    )(entries, populations)
     width = -(-(3 + len(shifts)) * LANES // 128) * 128
-    outer_sums, outer, migrants = call(
+    outer_sums, outer, second, migrants = call(
         part(outer_kernel, *sizes, count, shifts),
-        (shape(4, size_x, 8, size_z), shape(19, size_x, 8, size_z), shape(40, width)),
+        (
+            shape(4, size_x, 8, size_z),
+            shape(19, size_x, 8, size_z),
+            shape(11, size_x, 8, size_z),
+            shape(40, width),
+        ),
         8,
         [VMEM] * (3 + len(shifts)),
-    )(column, one, two, *rest)
+    )(column, *rest, two, one)
 
     def padded(planes):
         return shape(19, planes, size_y + 24, size_z)
@@ -818,29 +972,29 @@
         return shape(4, planes, size_y + 8, size_z)
 
     outside, inside = (0, size_x - 1), tuple(range(1, size_x - 1))
-    known = (entries, sums, outer_sums, outer, populations, migrants)
+    known = (entries, sums, outer_sums, outer, second, migrants)
     wide_face = shape((5 * size_y + 10 + 7) // 8 * 8, size_z)
     face = shape(5 * size_y, size_z)
-    ends, solid_ends, ahead, behind = call(
+    ends, solid_ends, near, far = call(
         part(first_kernel, *sizes, count, outside),
         (padded(2), solids(2), wide_face, wide_face),
         16,
-        [VMEM] * len(known),
-    )(*known)
-    from_behind, from_ahead = around(ahead, "gx", 1), around(behind, "gx", -1)
+        [VMEM] * (len(known) + 3),
+    )(*known, *parts)
+    near, far = exchanged(near, far)
     middle, solid_middle = call(
         part(first_kernel, *sizes, count, inside),
         (padded(len(inside)), solids(len(inside))),
         16,
-        [VMEM] * len(known),
-    )(*known)
+        [VMEM] * (len(known) + 1),
+    )(*known, populations)
     later_middle = call(
         part(second_kernel, *sizes, count, inside), padded(len(inside)), 16, [VMEM] * 4
     )(entries, ends, middle, solid_middle)
-    later_ends, ahead, behind = call(
+    later_ends, near, far = call(
         part(second_kernel, *sizes, count, outside), (padded(2), face, face), 16, [VMEM] * 6
-    )(entries, ends, middle, solid_ends, from_behind, from_ahead)
-    from_behind, from_ahead = around(ahead, "gx", 1), around(behind, "gx", -1)
+    )(entries, ends, middle, solid_ends, far, near)
+    near, far = exchanged(near, far)
     advanced = call(
         part(last_kernel, *sizes, count),
         shape(19, *sizes),
@@ -857,7 +1011,7 @@
         HBM,
         [pltpu.VMEM((10, size_y, size_z), F32), pltpu.SemaphoreType.DMA((10,))],
         {3: 0},
-    )(later_ends, from_behind, from_ahead, advanced)
+    )(later_ends, far, near, advanced)
 
 
 def solution(mesh):

time: 37.3 us -> 34.8 us (0.933)
  the two profiles are of different devices: /device:TPU:3 before, /device:TPU:0 now
where the time goes in v4:
time: 34.8 us; the launch traced here: 34.7 us
  Pallas kernels  14.1 us (41%)
  starting transfers between devices  11.6 us (33%)
  waiting for transfers between devices  8.87 us (25%)
    ppermute x8, starting transfers between devices, paired(): return lax.ppermute(value, axis, pairs)  11.5 us
    ppermute x8, waiting for transfers between devices, paired(): return lax.ppermute(value, axis, pairs)  7.02 us
    ppermute x1, waiting for transfers between devices, around(): lax.ppermute(value, axis, [(i, (i + steps) % count) for i in range(count)])  1.86 us
    pallas_call x1, Pallas kernels, local(): call(pack_kernel, (shape(32, rows), packed, packed, packed, band, band),...  1.7 us
    pallas_call x1, Pallas kernels, local(): sums = call(part(stay_kernel, *sizes), shape(4, *sizes), 16, [VMEM])(table)  1.5 us
    pallas_call x1, Pallas kernels, local(): call(part(last_kernel, *sizes, count), shape(19, *sizes), 16, [VMEM] * 2,...  1.5 us
    pallas_call x1, Pallas kernels, local(): call(part(second_kernel, *sizes, count, outside), (padded(2), face, face)...  1.5 us
    pallas_call x1, Pallas kernels, local(): call(part(second_kernel, *sizes, count, inside), padded(len(inside)), 16,...  1.47 us
  transfers between devices with their start and end apart: 9, of which 3 were waited for; matrix products, arithmetic and copies ran while one was open for 0% of the time, Pallas kernels for 25%

profile of v4, /device:TPU:0, one launch (start us, length us, event | category | flops | bytes accessed | tf_op | source)
XLA Modules:
  0.0 34.7 jit_solution(17073757558801400860)
XLA Ops:
  0.0 1.7 %shard_map.74 = (f32[32,512]{1,0:T(8,128)S(1)}, f32[32,128]{1,0:T(8,128)S(1)}, f32[32,128]{1,0:T(8,128)S(1)}, f32[32,128]{1,0:T(8,128)S(1)}, f32[19,4,8,256]{3,2...) custom-call(f32[3,512]{1,0:T(4,128)} %velocity_in.1, f32[3,512]{1,0:T(4,128)} %change_in.1, f32[27,512]{1,0:T(8,128)} %fractions_in.1, ...), custom_call_target="tpu_custom_call" | custom-call | tf_op jit(solution)/shard_map/pallas_call | solution.py:911
  1.7 3.4 %collective-permute-start = (f32[32,128]{1,0:T(8,128)S(1)}, f32[32,128]{1,0:T(8,128)S(1)}, u32[]{:S(2)}, u32[]{:S(2)}) collective-permute-start(f32[32,128]{1,0:T(8,128)S(1)} %get-tuple-element.34), channel_id=1, source_target_pairs={{0,28},{4,8},{8,4},{12,16},{16,12},{20,24},{24,20},{28,0},{1,29},{... | collective-permute-start | bytes 49160 | tf_op jit(solution)/shard_map/ppermute | solution.py:895
  5.1 0.0 collective-permute-start.1
  5.1 0.6 %shard_map.73.entries = f32[47,8,128]{2,1,0:T(8,128)S(1)} custom-call(f32[19]{0:T(128)S(1)} %copy-done.1), custom_call_target="tpu_custom_call" | custom-call | tf_op jit(solution)/shard_map/pallas_call | solution.py:929
  5.7 0.9 %shard_map.76 = (f32[160,256]{1,0:T(8,128)S(1)}, f32[160,256]{1,0:T(8,128)S(1)}) custom-call(f32[19,4,8,256]{3,2,1,0:T(8,128)S(1)} %get-tuple-element.36.bottom, f32[19,4,8,256]{3,2,1,0:T(8,128)S(1)} %get-tuple-element.37.top, f32[32,512]{1,0:T(8,128)S(1)} %get-tuple-element.32.table, f32[47,8,128]{2,1,0:T(8,128)S(1)} %shard_map.73.entries), custom_call_target="tpu_custom_call" | custom-call | tf_op jit(solution)/shard_map/pallas_call | solution.py:930
  6.7 0.0 collective-permute-done.far
  6.7 0.0 collective-permute-done.1.near
  6.7 0.1 shard_map.77
  6.8 0.7 %collective-permute-start.3 = (f32[160,256]{1,0:T(8,128)S(1)}, f32[160,256]{1,0:T(8,128)S(1)}, u32[]{:S(2)}, u32[]{:S(2)}) collective-permute-start(f32[160,256]{1,0:T(8,128)S(1)} %get-tuple-element.41), channel_id=1, source_target_pairs={{0,0},{1,2},{2,1},{3,3},{4,4},{5,6},{6,5},{7,7},{8,8},{9,10},{10,9... | collective-permute-start | bytes 491528 | tf_op jit(solution)/shard_map/ppermute | solution.py:895
  7.4 5.1 %collective-permute-start.4 = (f32[160,256]{1,0:T(8,128)S(1)}, f32[160,256]{1,0:T(8,128)S(1)}, u32[]{:S(2)}, u32[]{:S(2)}) collective-permute-start(f32[160,256]{1,0:T(8,128)S(1)} %get-tuple-element.42), channel_id=1, source_target_pairs={{0,1},{1,0},{2,3},{3,2},{4,5},{5,4},{6,7},{7,6},{8,9},{9,8},{10,11... | collective-permute-start | bytes 491528 | tf_op jit(solution)/shard_map/ppermute | solution.py:895
  12.6 1.5 %shard_map.75.sums = f32[4,4,32,256]{3,2,1,0:T(8,128)S(1)} custom-call(f32[32,512]{1,0:T(8,128)S(1)} %get-tuple-element.32.table), custom_call_target="tpu_custom_call" | custom-call | tf_op jit(solution)/shard_map/pallas_call | solution.py:950
  14.1 1.1 %shard_map.79 = (f32[19,2,32,256]{3,2,1,0:T(8,128)S(1)}, f32[19,2,32,256]{3,2,1,0:T(8,128)S(1)}, f32[2,32,256]{2,1,0:T(8,128)S(1)}) custom-call(f32[47,8,128]{2,1,0:T(8,128)S(1)} %shard_map.73.entries, f32[19,4,32,256]{3,2,1,0:T(8,128)S(1)} %copy-done), custom_call_target="tpu_custom_call" | custom-call | tf_op jit(solution)/shard_map/pallas_call | solution.py:952
  15.2 1.9 %collective-permute-done.2.refs_0_ = f32[8,128]{1,0:T(8,128)S(1)} collective-permute-done((f32[8,128]{1,0:T(8,128)S(1)}, f32[8,128]{1,0:T(8,128)S(1)}, u32[]{:S(2)}, u32[]{:S(2)}) %collective-permute-start.2) | collective-permute-done | bytes 4128 | tf_op jit(solution)/shard_map/ppermute | solution.py:883
  17.1 0.3 shard_map.78
  17.4 1.1 %shard_map.80 = (f32[19,2,56,256]{3,2,1,0:T(8,128)S(1)}, f32[4,2,40,256]{3,2,1,0:T(8,128)S(1)}, f32[176,256]{1,0:T(8,128)S(1)}, f32[176,256]{1,0:T(8,128)S(1)}) custom-call(f32[47,8,128]{2,1,0:T(8,128)S(1)} %shard_map.73.entries, f32[4,4,32,256]{3,2,1,0:T(8,128)S(1)} %shard_map.75.sums, f32[4,4,8,256]{3,2,1,0:T(8,128)S(1)} %get-tuple-element.43.outer_sums, ...), custom_call_target="tpu_custom_call" | custom-call | tf_op jit(solution)/shard_map/pallas_call | solution.py:978
  18.5 1.3 %collective-permute-start.5 = (f32[176,256]{1,0:T(8,128)S(1)}, f32[176,256]{1,0:T(8,128)S(1)}, u32[]{:S(2)}, u32[]{:S(2)}) collective-permute-start(f32[176,256]{1,0:T(8,128)S(1)} %get-tuple-element.53), channel_id=1, source_target_pairs={{0,28},{4,8},{8,4},{12,16},{16,12},{20,24},{24,20},{28,0},{1,29},{... | collective-permute-start | bytes 540680 | tf_op jit(solution)/shard_map/ppermute | solution.py:895
  19.9 1.5 %shard_map.81 = (f32[19,2,56,256]{3,2,1,0:T(8,128)S(1)}, f32[4,2,40,256]{3,2,1,0:T(8,128)S(1)}) custom-call(f32[47,8,128]{2,1,0:T(8,128)S(1)} %shard_map.73.entries, f32[4,4,32,256]{3,2,1,0:T(8,128)S(1)} %shard_map.75.sums, f32[4,4,8,256]{3,2,1,0:T(8,128)S(1)} %get-tuple-element.43.outer_sums, f32[19,4,8,256]{3,2,1,0:T(8,128)S(1)} %get-tuple-element.44.outer, ...), custom_call_target="tpu_custom_call" | custom-call | tf_op jit(solution)/shard_map/pallas_call | solution.py:985
  21.3 4.5 %collective-permute-done.5.refs_0_ = f32[176,256]{1,0:T(8,128)S(1)} collective-permute-done((f32[176,256]{1,0:T(8,128)S(1)}, f32[176,256]{1,0:T(8,128)S(1)}, u32[]{:S(2)}, u32[]{:S(2)}) %collective-permute-start.5) | collective-permute-done | bytes 180256 | tf_op jit(solution)/shard_map/ppermute | solution.py:895
  25.9 1.5 %shard_map.82 = (f32[19,2,56,256]{3,2,1,0:T(8,128)S(1)}, f32[160,256]{1,0:T(8,128)S(1)}, f32[160,256]{1,0:T(8,128)S(1)}) custom-call(f32[47,8,128]{2,1,0:T(8,128)S(1)} %shard_map.73.entries, f32[19,2,56,256]{3,2,1,0:T(8,128)S(1)} %get-tuple-element.50.ends, f32[19,2,56,256]{3,2,1,0:T(8,128)S(1)} %get-tuple-element.51.middle, ...), custom_call_target="tpu_custom_call" | custom-call | tf_op jit(solution)/shard_map/pallas_call | solution.py:994
  27.4 1.0 %collective-permute-start.7 = (f32[160,256]{1,0:T(8,128)S(1)}, f32[160,256]{1,0:T(8,128)S(1)}, u32[]{:S(2)}, u32[]{:S(2)}) collective-permute-start(f32[160,256]{1,0:T(8,128)S(1)} %get-tuple-element.56), channel_id=1, source_target_pairs={{0,28},{4,8},{8,4},{12,16},{16,12},{20,24},{24,20},{28,0},{1,29},{... | collective-permute-start | bytes 491528 | tf_op jit(solution)/shard_map/ppermute | solution.py:895
  28.4 1.5 %shard_map.83.middle = f32[19,2,56,256]{3,2,1,0:T(8,128)S(1)} custom-call(f32[47,8,128]{2,1,0:T(8,128)S(1)} %shard_map.73.entries, f32[19,2,56,256]{3,2,1,0:T(8,128)S(1)} %get-tuple-element.50.ends, f32[19,2,56,256]{3,2,1,0:T(8,128)S(1)} %get-tuple-element.51.middle, f32[4,2,40,256]{3,2,1,0:T(8,128)S(1)} %get-tuple-element.58.solid), custom_call_target="tpu_custom_call" | custom-call | tf_op jit(solution)/shard_map/pallas_call | solution.py:991
  29.9 1.5 %shard_map.84.given = f32[19,4,32,256]{3,2,1,0:T(8,128)} custom-call(f32[19,2,56,256]{3,2,1,0:T(8,128)S(1)} %get-tuple-element.55.ends, f32[19,2,56,256]{3,2,1,0:T(8,128)S(1)} %shard_map.83.middle), custom_call_target="tpu_custom_call" | custom-call | tf_op jit(solution)/shard_map/pallas_call | solution.py:998
  31.4 2.5 %collective-permute-done.7.far = f32[160,256]{1,0:T(8,128)S(1)} collective-permute-done((f32[160,256]{1,0:T(8,128)S(1)}, f32[160,256]{1,0:T(8,128)S(1)}, u32[]{:S(2)}, u32[]{:S(2)}) %collective-permute-start.7) | collective-permute-done | bytes 163872 | tf_op jit(solution)/shard_map/ppermute | solution.py:895
  33.8 0.8 %shard_map.85 = f32[19,4,32,256]{3,2,1,0:T(8,128)} custom-call(f32[19,2,56,256]{3,2,1,0:T(8,128)S(1)} %get-tuple-element.55.ends, f32[160,256]{1,0:T(8,128)S(1)} %collective-permute-done.7.far, f32[160,256]{1,0:T(8,128)S(1)} %collective-permute-done.8.near, f32[19,4,32,256]{3,2,1,0:T(8,128)} %shard_map.84.given), custom_call_target="tpu_custom_call", output_to_operand_aliasing={{}: (3, {})} | custom-call | tf_op jit(solution)/shard_map/pallas_call | solution.py:1006
  (11 shorter events, 0.0 us)
Async XLA Ops:
  0.0 5.1 %copy-start.1 = (f32[19]{0:T(128)S(1)}, f32[19]{0:T(128)}, u32[]{:S(2)}) copy-start(f32[19]{0:T(128)} %rates.1) | copy-start | bytes 232
  0.0 14.1 %copy-start = (f32[19,4,32,256]{3,2,1,0:T(8,128)S(1)}, f32[19,4,32,256]{3,2,1,0:T(8,128)}, u32[]{:S(2)}) copy-start(f32[19,4,32,256]{3,2,1,0:T(8,128)} %refs_0_.1) | copy-start | bytes 7471108
  1.7 4.9 %collective-permute-start = (f32[32,128]{1,0:T(8,128)S(1)}, f32[32,128]{1,0:T(8,128)S(1)}, u32[]{:S(2)}, u32[]{:S(2)}) collective-permute-start(f32[32,128]{1,0:T(8,128)S(1)} %get-tuple-element.34), channel_id=1, source_target_pairs={{0,28},{4,8},{8,4},{12,16},{16,12},{20,24},{24,20},{28,0},{1,29},{... | collective-permute-start | bytes 49160 | tf_op jit(solution)/shard_map/ppermute | solution.py:895
  5.1 1.6 %collective-permute-start.1 = (f32[32,128]{1,0:T(8,128)S(1)}, f32[32,128]{1,0:T(8,128)S(1)}, u32[]{:S(2)}, u32[]{:S(2)}) collective-permute-start(f32[32,128]{1,0:T(8,128)S(1)} %get-tuple-element.35), channel_id=1, source_target_pairs={{0,4},{4,0},{8,12},{12,8},{16,20},{20,16},{24,28},{28,24},{1,5},{5... | collective-permute-start | bytes 49160 | tf_op jit(solution)/shard_map/ppermute | solution.py:895
  6.8 10.3 %collective-permute-start.3 = (f32[160,256]{1,0:T(8,128)S(1)}, f32[160,256]{1,0:T(8,128)S(1)}, u32[]{:S(2)}, u32[]{:S(2)}) collective-permute-start(f32[160,256]{1,0:T(8,128)S(1)} %get-tuple-element.41), channel_id=1, source_target_pairs={{0,0},{1,2},{2,1},{3,3},{4,4},{5,6},{6,5},{7,7},{8,8},{9,10},{10,9... | collective-permute-start | bytes 491528 | tf_op jit(solution)/shard_map/ppermute | solution.py:895
  7.4 9.7 %collective-permute-start.4 = (f32[160,256]{1,0:T(8,128)S(1)}, f32[160,256]{1,0:T(8,128)S(1)}, u32[]{:S(2)}, u32[]{:S(2)}) collective-permute-start(f32[160,256]{1,0:T(8,128)S(1)} %get-tuple-element.42), channel_id=1, source_target_pairs={{0,1},{1,0},{2,3},{3,2},{4,5},{5,4},{6,7},{7,6},{8,9},{9,8},{10,11... | collective-permute-start | bytes 491528 | tf_op jit(solution)/shard_map/ppermute | solution.py:895
  12.6 4.5 %collective-permute-start.2 = (f32[8,128]{1,0:T(8,128)S(1)}, f32[8,128]{1,0:T(8,128)S(1)}, u32[]{:S(2)}, u32[]{:S(2)}) collective-permute-start(f32[8,128]{1,0:T(8,128)S(1)} %get-tuple-element.40.column), channel_id=1, source_target_pairs={{0,2},{1,3},{2,0},{3,1},{4,6},{5,7},{6,4},{7,5},{8,10},{9,11},{10,... | collective-permute-start | bytes 12296 | tf_op jit(solution)/shard_map/ppermute | solution.py:883
  18.5 7.3 %collective-permute-start.5 = (f32[176,256]{1,0:T(8,128)S(1)}, f32[176,256]{1,0:T(8,128)S(1)}, u32[]{:S(2)}, u32[]{:S(2)}) collective-permute-start(f32[176,256]{1,0:T(8,128)S(1)} %get-tuple-element.53), channel_id=1, source_target_pairs={{0,28},{4,8},{8,4},{12,16},{16,12},{20,24},{24,20},{28,0},{1,29},{... | collective-permute-start | bytes 540680 | tf_op jit(solution)/shard_map/ppermute | solution.py:895
  19.9 6.0 %collective-permute-start.6 = (f32[176,256]{1,0:T(8,128)S(1)}, f32[176,256]{1,0:T(8,128)S(1)}, u32[]{:S(2)}, u32[]{:S(2)}) collective-permute-start(f32[176,256]{1,0:T(8,128)S(1)} %get-tuple-element.54), channel_id=1, source_target_pairs={{0,4},{4,0},{8,12},{12,8},{16,20},{20,16},{24,28},{28,24},{1,5},{5... | collective-permute-start | bytes 540680 | tf_op jit(solution)/shard_map/ppermute | solution.py:895
  27.4 6.5 %collective-permute-start.7 = (f32[160,256]{1,0:T(8,128)S(1)}, f32[160,256]{1,0:T(8,128)S(1)}, u32[]{:S(2)}, u32[]{:S(2)}) collective-permute-start(f32[160,256]{1,0:T(8,128)S(1)} %get-tuple-element.56), channel_id=1, source_target_pairs={{0,28},{4,8},{8,4},{12,16},{16,12},{20,24},{24,20},{28,0},{1,29},{... | collective-permute-start | bytes 491528 | tf_op jit(solution)/shard_map/ppermute | solution.py:895
  28.4 5.5 %collective-permute-start.8 = (f32[160,256]{1,0:T(8,128)S(1)}, f32[160,256]{1,0:T(8,128)S(1)}, u32[]{:S(2)}, u32[]{:S(2)}) collective-permute-start(f32[160,256]{1,0:T(8,128)S(1)} %get-tuple-element.57), channel_id=1, source_target_pairs={{0,4},{4,0},{8,12},{12,8},{16,20},{20,16},{24,28},{28,24},{1,5},{5... | collective-permute-start | bytes 491528 | tf_op jit(solution)/shard_map/ppermute | solution.py:895

commit v5 on v4

--- a/solution.py
+++ b/solution.py
@@ -427,7 +427,8 @@
     high = payload.astype(BF16)
     middle, low = halves(payload - high.astype(F32))
     packed = dot_t(high, chosen) + dot_t(middle, chosen) + dot_t(low, chosen)
-    lane = iota((32, 128), 1)
+    packed = folded(packed)
+    lane = lax.rem(iota((8, 128), 1), jnp.int32(LANES))
     own[...] = jnp.where(lane < 2 * CAP, packed, 0.0)
     ahead = jnp.where((lane >= 2 * CAP) & (lane < 5 * CAP), packed, 0.0)
     behind = jnp.where(lane >= 5 * CAP, packed, 0.0)
@@ -503,7 +504,7 @@
 
 def merge_kernel(first, fold, own, far, near, one_in, two_in, column, one, two):
     del one_in, two_in
-    merged = folded(own[...] + near[...] + far[...])
+    merged = own[...] + near[...] + far[...]
     column[...] = merged
     deep = 8 // fold
     for k in range(fold):
@@ -649,12 +650,7 @@
     return value if shift == 0 else pltpu.roll(value, shift % size_z, 1)
 
 
-def first_kernel(
-    size_x, size_y, size_z, count, planes, entries, sums, outer_sums, outer, second, migrants, *refs
-):
-    prepared = planes[0] == 0
-    given, (post, solid, *faces_out) = (refs[:3], refs[3:]) if prepared else (refs[:1], refs[1:])
-    tiles = size_y // 8
+def solids(size_x, size_y, size_z, planes, sums, outer_sums, migrants, solid):
     a_x, a_y, a_z = (migrants[k : k + 1, :].astype(I32) for k in (32, 33, 34))
     wide = size_y + 8
     index = iota((len(planes) * wide, 1), 0)
@@ -662,54 +658,105 @@
     row = index - number * wide
     rows_x = number + planes[0] if len(planes) == planes[-1] - planes[0] + 1 else number * (size_x - 1)
     rows_y = jnp.where(row < size_y + 2, row, jnp.where(row >= size_y + 6, row - wide, -3 * size_y))
-    big = 4 * size_y * (count + 2)
+    big = 4 * size_y * (lax.axis_size("gy") + 2)
     totals = deposited(
         [(rows_x, rows_y)], migrants[0:27, :], migrants[27:30, :], a_x, a_y, a_z, size_z, big
     )
-    blocks = relax_blocks(entries)
     cells = len(planes) * wide
     for p, x in enumerate(planes):
-        for tile in range(tiles + 1):
-            rows = slice(8 * tile, 8 * tile + 8)
-            for part in range(size_z // 128):
-                lanes = slice(128 * part, 128 * part + 128)
-                parts = []
-                for c in range(4):
-                    at = c * cells + p * wide + 8 * tile
-                    staying = outer_sums[c, x, :, lanes] if tile == tiles else sums[c, x, rows, lanes]
-                    parts.append(totals[at : at + 8, lanes] + staying)
-                scale = 1.0 / (parts[0] + 1e-06)
-                share = jnp.minimum(parts[0], 1.0)
-                flow = [parts[k] * scale for k in (1, 2, 3)]
-                for c, value in enumerate([share] + flow):
-                    solid[c, p, rows, lanes] = value
-                if tile == tiles:
-                    h = [outer[i, x, :, lanes] for i in range(19)]
-                    out = collide(h, share, *flow, blocks)
-                    line = iota((8, 128), 0)
-                    away = jnp.where(line < 4, 1.0, -1.0)
-                    still = equilibrium(None, [away * v for v in flow], DOWNWARD)
-                    density = second[10, x, :, lanes]
-                    for k, (i, j) in enumerate(zip(DOWNWARD, UPWARD)):
-                        parts = (second[k, x, :, lanes], second[5 + k, x, :, lanes], density)
-                        value = blended(*parts, share, still[i])
-                        out[i] = jnp.where(line == 1, value, out[i])
-                        out[j] = jnp.where(line == 6, value, out[j])
-                elif prepared:
-                    relaxed, bounced, dense = given
-                    still = equilibrium(None, flow, range(19))
-                    density = dense[p, rows, lanes]
-                    out = [
-                        blended(relaxed[i, p, rows, lanes], bounced[i, p, rows, lanes], density, share, still[i])
-                        for i in range(19)
-                    ]
-                else:
-                    h = [given[0][i, x, rows, lanes] for i in range(19)]
-                    out = collide(h, share, *flow, blocks)
-                for i in range(19):
-                    store_padded(post, i, p, tile, part, out[i], tiles)
-    if faces_out:
-        send_faces(post, *faces_out, size_y, size_z, True)
+        parts = []
+        for c in range(4):
+            at = c * cells + p * wide
+            solid_sum = jnp.concatenate([sums[c, x, :, :], outer_sums[c, x, :, :]], axis=0)
+            parts.append(totals[at : at + wide] + solid_sum)
+        scale = 1.0 / (parts[0] + 1e-06)
+        solid[0, p, :, :] = jnp.minimum(parts[0], 1.0)
+        for c in (1, 2, 3):
+            solid[c, p, :, :] = parts[c] * scale
+
+
+def outer_collision(solid, outer, second, blocks, p, x, lanes, rows):
+    share, *flow = (solid[c, p, rows, lanes] for c in range(4))
+    out = collide([outer[i, x, :, lanes] for i in range(19)], share, *flow, blocks)
+    line = iota((8, 128), 0)
+    away = jnp.where(line < 4, 1.0, -1.0)
+    still = equilibrium(None, [away * v for v in flow], DOWNWARD)
+    density = second[10, x, :, lanes]
+    for k, (i, j) in enumerate(zip(DOWNWARD, UPWARD)):
+        value = blended(second[k, x, :, lanes], second[5 + k, x, :, lanes], density, share, still[i])
+        out[i] = jnp.where(line == 1, value, out[i])
+        out[j] = jnp.where(line == 6, value, out[j])
+    return out
+
+
+def prepared_collision(solid, relaxed, bounced, dense, p, rows, lanes, numbers):
+    share, *flow = (solid[c, p, rows, lanes] for c in range(4))
+    still = equilibrium(None, flow, numbers)
+    density = dense[p, rows, lanes]
+    return {
+        i: blended(relaxed[i, p, rows, lanes], bounced[i, p, rows, lanes], density, share, still[i])
+        for i in numbers
+    }
+
+
+def tile_parts(size_y, size_z):
+    for tile in range(size_y // 8 + 1):
+        for part in range(size_z // 128):
+            yield tile, slice(8 * tile, 8 * tile + 8), part, slice(128 * part, 128 * part + 128)
+
+
+def leaving_kernel(
+    size_x, size_y, size_z, entries, sums, outer_sums, outer, second, migrants, relaxed, bounced, dense,
+    solid, near, far, leaving
+):
+    tiles = size_y // 8
+    planes = (0, size_x - 1)
+    solids(size_x, size_y, size_z, planes, sums, outer_sums, migrants, solid)
+    blocks = relax_blocks(entries)
+    for p, x in enumerate(planes):
+        numbers = FORWARD if p else BACKWARD
+        for tile, rows, part, lanes in tile_parts(size_y, size_z):
+            if tile == tiles:
+                out = outer_collision(solid, outer, second, blocks, p, x, lanes, rows)
+            else:
+                out = prepared_collision(solid, relaxed, bounced, dense, p, rows, lanes, numbers)
+            for k, i in enumerate(numbers):
+                store_padded(leaving, k, p, tile, part, out[i], tiles)
+    send_faces(leaving, near, far, size_y, size_z, True)
+
+
+def ends_kernel(
+    size_x, size_y, size_z, entries, outer, second, relaxed, bounced, dense, solid, post
+):
+    tiles = size_y // 8
+    blocks = relax_blocks(entries)
+    for p, x in enumerate((0, size_x - 1)):
+        for tile, rows, part, lanes in tile_parts(size_y, size_z):
+            if tile == tiles:
+                out = outer_collision(solid, outer, second, blocks, p, x, lanes, rows)
+            else:
+                out = prepared_collision(solid, relaxed, bounced, dense, p, rows, lanes, range(19))
+            for i in range(19):
+                store_padded(post, i, p, tile, part, out[i], tiles)
+
+
+def middle_kernel(
+    size_x, size_y, size_z, planes, entries, sums, outer_sums, outer, second, migrants, populations,
+    post, solid
+):
+    tiles = size_y // 8
+    solids(size_x, size_y, size_z, planes, sums, outer_sums, migrants, solid)
+    blocks = relax_blocks(entries)
+    for p, x in enumerate(planes):
+        for tile, rows, part, lanes in tile_parts(size_y, size_z):
+            if tile == tiles:
+                out = outer_collision(solid, outer, second, blocks, p, x, lanes, rows)
+            else:
+                share, *flow = (solid[c, p, rows, lanes] for c in range(4))
+                h = [populations[i, x, rows, lanes] for i in range(19)]
+                out = collide(h, share, *flow, blocks)
+            for i in range(19):
+                store_padded(post, i, p, tile, part, out[i], tiles)
 
 
 def send_faces(post, near, far, size_y, size_z, outer):
@@ -732,10 +779,10 @@
             for tile in range(tiles):
                 at = 8 + 8 * tile - c_y
                 to = k * size_y + 8 * tile
-                target[to : to + 8, :] = turned(post[i, p, at : at + 8, :], c_z, size_z)
+                target[to : to + 8, :] = turned(post[k, p, at : at + 8, :], c_z, size_z)
             if outer:
                 at = 8 + size_y - c_y
-                value = turned(post[i, p, at : at + 8, :], c_z, size_z)
+                value = turned(post[k, p, at : at + 8, :], c_z, size_z)
                 to = 5 * size_y + 2 * k
                 target[to : to + 1, :] = value[0:1]
                 target[to + 1 : to + 2, :] = value[7:8]
@@ -787,28 +834,30 @@
 
 def second_kernel(size_x, size_y, size_z, count, planes, entries, ends, middle, solid, *refs):
     refs = list(refs)
-    messages = (refs.pop(1), refs.pop(0), even_x()) if planes[0] == 0 else None
-    later, faces_out = refs[0], refs[1:]
+    outside = planes[0] == 0
+    messages = (refs.pop(1), refs.pop(0), even_x()) if outside else None
+    leaving = len(refs) > 1
+    if leaving:
+        del refs[0]
     tiles = size_y // 8
     walls = walls_of(count)
     blocks = relax_blocks(entries)
     for p, x in enumerate(planes):
+        numbers = (FORWARD if p else BACKWARD) if leaving else range(19)
         for tile in range(tiles + 1):
             rows = slice(8 * tile, 8 * tile + 8)
             h = [
-                streamed(
-                    ends, middle, messages, i, x, tile, size_x, size_y, size_z, walls
-                )
+                streamed(ends, middle, messages, i, x, tile, size_x, size_y, size_z, walls)
                 for i in range(19)
             ]
             for part in range(size_z // 128):
                 lanes = slice(128 * part, 128 * part + 128)
                 s = [solid[c, p, rows, lanes] for c in range(4)]
                 out = collide([v[:, lanes] for v in h], *s, blocks)
-                for i in range(19):
-                    store_padded(later, i, p, tile, part, out[i], tiles)
-    if faces_out:
-        send_faces(later, *faces_out, size_y, size_z, False)
+                for k, i in enumerate(numbers):
+                    store_padded(refs[-1], k, p, tile, part, out[i], tiles)
+    if leaving:
+        send_faces(refs[-1], refs[0], refs[1], size_y, size_z, False)
 
 
 def last_kernel(size_x, size_y, size_z, count, ends, middle, advanced, held, done):
@@ -906,7 +955,7 @@
     rows = anchor.shape[0]
     sizes = (size_x, size_y, size_z)
     part = functools.partial
-    packed = shape(32, 128)
+    packed = shape(8, 128)
     band = shape(19, size_x, 8, size_z)
     table, own, near, far, bottom, top = call(
         pack_kernel,
@@ -968,32 +1017,39 @@
     def padded(planes):
         return shape(19, planes, size_y + 24, size_z)
 
-    def solids(planes):
+    def solid_shape(planes):
         return shape(4, planes, size_y + 8, size_z)
 
     outside, inside = (0, size_x - 1), tuple(range(1, size_x - 1))
-    known = (entries, sums, outer_sums, outer, second, migrants)
+    sent = pltpu.VMEM((5, 2, size_y + 24, size_z), F32)
     wide_face = shape((5 * size_y + 10 + 7) // 8 * 8, size_z)
     face = shape(5 * size_y, size_z)
-    ends, solid_ends, near, far = call(
-        part(first_kernel, *sizes, count, outside),
-        (padded(2), solids(2), wide_face, wide_face),
-        16,
-        [VMEM] * (len(known) + 3),
+    known = (entries, sums, outer_sums, outer, second, migrants)
+    solid_ends, near, far = call(
+        part(leaving_kernel, *sizes), (solid_shape(2), wide_face, wide_face), 16, [VMEM] * 9, scratch=[sent]
     )(*known, *parts)
     near, far = exchanged(near, far)
     middle, solid_middle = call(
-        part(first_kernel, *sizes, count, inside),
-        (padded(len(inside)), solids(len(inside))),
+        part(middle_kernel, *sizes, inside),
+        (padded(len(inside)), solid_shape(len(inside))),
         16,
-        [VMEM] * (len(known) + 1),
+        [VMEM] * 7,
     )(*known, populations)
+    ends = call(part(ends_kernel, *sizes), padded(2), 16, [VMEM] * 7)(
+        entries, outer, second, *parts, solid_ends
+    )
     later_middle = call(
         part(second_kernel, *sizes, count, inside), padded(len(inside)), 16, [VMEM] * 4
     )(entries, ends, middle, solid_middle)
-    later_ends, near, far = call(
-        part(second_kernel, *sizes, count, outside), (padded(2), face, face), 16, [VMEM] * 6
-    )(entries, ends, middle, solid_ends, far, near)
+    given = (entries, ends, middle, solid_ends, far, near)
+    near, far = call(
+        part(second_kernel, *sizes, count, outside),
+        (face, face),
+        16,
+        [VMEM] * 6 + [pl.BlockSpec(memory_space=pl.ANY)],
+        scratch=[sent],
+    )(*given, later_middle)
+    later_ends = call(part(second_kernel, *sizes, count, outside), padded(2), 16, [VMEM] * 6)(*given)
     near, far = exchanged(near, far)
     advanced = call(
         part(last_kernel, *sizes, count),

time: 34.8 us -> 34.1 us (0.980)
  waiting for transfers between devices: 8.87 us -> 7.02 us
  Pallas kernels: 14.1 us -> 15.4 us
    ppermute x8, waiting for transfers between devices: 7.02 us -> 5.15 us  [paired(): return lax.ppermute(value, axis, pairs)]
    pallas_call x3 -> x5, Pallas kernels: 4.1 us -> 5.44 us  [the longest x1 1.43 us: local(): call(part(middle_kernel, *sizes, inside), (padded(len(inside)), solid_sha...]
  transfers between devices with their start and end apart: 9 -> 9, of which waited for: 3 -> 3; matrix products, arithmetic and copies ran while one was open for 0% -> 0% of each run, Pallas kernels for 25% -> 31%
where the time goes in v5:
time: 34.1 us; the launch traced here: 33.9 us
  Pallas kernels  15.4 us (45%)
  starting transfers between devices  11.3 us (33%)
  waiting for transfers between devices  7.02 us (21%)
    ppermute x8, starting transfers between devices, paired(): return lax.ppermute(value, axis, pairs)  11.3 us
    ppermute x8, waiting for transfers between devices, paired(): return lax.ppermute(value, axis, pairs)  5.15 us
    ppermute x1, waiting for transfers between devices, around(): lax.ppermute(value, axis, [(i, (i + steps) % count) for i in range(count)])  1.86 us
    pallas_call x1, Pallas kernels, local(): call(pack_kernel, (shape(32, rows), packed, packed, packed, band, band),...  1.77 us
    pallas_call x1, Pallas kernels, local(): call(part(last_kernel, *sizes, count), shape(19, *sizes), 16, [VMEM] * 2,...  1.5 us
    pallas_call x1, Pallas kernels, local(): sums = call(part(stay_kernel, *sizes), shape(4, *sizes), 16, [VMEM])(table)  1.5 us
    pallas_call x1, Pallas kernels, local(): call(part(second_kernel, *sizes, count, inside), padded(len(inside)), 16,...  1.49 us
    pallas_call x1, Pallas kernels, local(): call(part(middle_kernel, *sizes, inside), (padded(len(inside)), solid_sha...  1.43 us
  transfers between devices with their start and end apart: 9, of which 3 were waited for; matrix products, arithmetic and copies ran while one was open for 0% of the time, Pallas kernels for 31%

profile of v5, /device:TPU:0, one launch (start us, length us, event | category | flops | bytes accessed | tf_op | source)
XLA Modules:
  0.0 33.9 jit_solution(8061165737919236766)
XLA Ops:
  0.0 1.8 %shard_map.74 = (f32[32,512]{1,0:T(8,128)S(1)}, f32[8,128]{1,0:T(8,128)S(1)}, f32[8,128]{1,0:T(8,128)S(1)}, f32[8,128]{1,0:T(8,128)S(1)}, f32[19,4,8,256]{3,2,1,0:T(8,128)S(1)}, /*index=5*/f32[19,4,8,256]{3,2,1,0:T(8,128)S(1)}) custom-call(f32[3,512]{1,0:T(4,128)} %velocity_in.1, f32[3,512]{1,0:T(4,128)} %change_in.1, f32[27,512]{1,0:T(8,128)} %fractions_in.1, ...), custom_call_target="tpu_custom_call" | custom-call | tf_op jit(solution)/shard_map/pallas_call | solution.py:960
  1.8 3.4 %collective-permute-start = (f32[8,128]{1,0:T(8,128)S(1)}, f32[8,128]{1,0:T(8,128)S(1)}, u32[]{:S(2)}, u32[]{:S(2)}) collective-permute-start(f32[8,128]{1,0:T(8,128)S(1)} %get-tuple-element.31), channel_id=1, source_target_pairs={{0,28},{4,8},{8,4},{12,16},{16,12},{20,24},{24,20},{28,0},{1,29},{... | collective-permute-start | bytes 12296 | tf_op jit(solution)/shard_map/ppermute | solution.py:944
  5.2 0.0 collective-permute-start.1
  5.2 0.6 %shard_map.73.entries = f32[47,8,128]{2,1,0:T(8,128)S(1)} custom-call(f32[19]{0:T(128)S(1)} %copy-done.1), custom_call_target="tpu_custom_call" | custom-call | tf_op jit(solution)/shard_map/pallas_call | solution.py:978
  5.8 0.9 %shard_map.75 = (f32[160,256]{1,0:T(8,128)S(1)}, f32[160,256]{1,0:T(8,128)S(1)}) custom-call(f32[19,4,8,256]{3,2,1,0:T(8,128)S(1)} %get-tuple-element.33.bottom, f32[19,4,8,256]{3,2,1,0:T(8,128)S(1)} %get-tuple-element.34.top, f32[32,512]{1,0:T(8,128)S(1)} %get-tuple-element.35.table, f32[47,8,128]{2,1,0:T(8,128)S(1)} %shard_map.73.entries), custom_call_target="tpu_custom_call" | custom-call | tf_op jit(solution)/shard_map/pallas_call | solution.py:979
  6.8 0.7 %collective-permute-start.3 = (f32[160,256]{1,0:T(8,128)S(1)}, f32[160,256]{1,0:T(8,128)S(1)}, u32[]{:S(2)}, u32[]{:S(2)}) collective-permute-start(f32[160,256]{1,0:T(8,128)S(1)} %get-tuple-element.39), channel_id=1, source_target_pairs={{0,0},{1,2},{2,1},{3,3},{4,4},{5,6},{6,5},{7,7},{8,8},{9,10},{10,9... | collective-permute-start | bytes 491528 | tf_op jit(solution)/shard_map/ppermute | solution.py:944
  7.4 4.9 %collective-permute-start.4 = (f32[160,256]{1,0:T(8,128)S(1)}, f32[160,256]{1,0:T(8,128)S(1)}, u32[]{:S(2)}, u32[]{:S(2)}) collective-permute-start(f32[160,256]{1,0:T(8,128)S(1)} %get-tuple-element.40), channel_id=1, source_target_pairs={{0,1},{1,0},{2,3},{3,2},{4,5},{5,4},{6,7},{7,6},{8,9},{9,8},{10,11... | collective-permute-start | bytes 491528 | tf_op jit(solution)/shard_map/ppermute | solution.py:944
  12.4 0.0 collective-permute-start.2
  12.4 1.5 %shard_map.79.sums = f32[4,4,32,256]{3,2,1,0:T(8,128)S(1)} custom-call(f32[32,512]{1,0:T(8,128)S(1)} %get-tuple-element.35.table), custom_call_target="tpu_custom_call" | custom-call | tf_op jit(solution)/shard_map/pallas_call | solution.py:999
  13.9 1.1 %shard_map.78 = (f32[19,2,32,256]{3,2,1,0:T(8,128)S(1)}, f32[19,2,32,256]{3,2,1,0:T(8,128)S(1)}, f32[2,32,256]{2,1,0:T(8,128)S(1)}) custom-call(f32[47,8,128]{2,1,0:T(8,128)S(1)} %shard_map.73.entries, f32[19,4,32,256]{3,2,1,0:T(8,128)S(1)} %copy-done), custom_call_target="tpu_custom_call" | custom-call | tf_op jit(solution)/shard_map/pallas_call | solution.py:1001
  15.0 1.9 %collective-permute-done.2.refs_0_ = f32[8,128]{1,0:T(8,128)S(1)} collective-permute-done((f32[8,128]{1,0:T(8,128)S(1)}, f32[8,128]{1,0:T(8,128)S(1)}, u32[]{:S(2)}, u32[]{:S(2)}) %collective-permute-start.2) | collective-permute-done | bytes 4128 | tf_op jit(solution)/shard_map/ppermute | solution.py:932
  16.9 0.3 shard_map.77
  17.2 0.9 %shard_map.80 = (f32[4,2,40,256]{3,2,1,0:T(8,128)S(1)}, f32[176,256]{1,0:T(8,128)S(1)}, f32[176,256]{1,0:T(8,128)S(1)}) custom-call(f32[47,8,128]{2,1,0:T(8,128)S(1)} %shard_map.73.entries, f32[4,4,32,256]{3,2,1,0:T(8,128)S(1)} %shard_map.79.sums, f32[4,4,8,256]{3,2,1,0:T(8,128)S(1)} %get-tuple-element.46.outer_sums, ...), custom_call_target="tpu_custom_call" | custom-call | tf_op jit(solution)/shard_map/pallas_call | solution.py:1028
  18.0 1.4 %collective-permute-start.5 = (f32[176,256]{1,0:T(8,128)S(1)}, f32[176,256]{1,0:T(8,128)S(1)}, u32[]{:S(2)}, u32[]{:S(2)}) collective-permute-start(f32[176,256]{1,0:T(8,128)S(1)} %get-tuple-element.50), channel_id=1, source_target_pairs={{0,28},{4,8},{8,4},{12,16},{16,12},{20,24},{24,20},{28,0},{1,29},{... | collective-permute-start | bytes 540680 | tf_op jit(solution)/shard_map/ppermute | solution.py:944
  19.5 1.4 %shard_map.82 = (f32[19,2,56,256]{3,2,1,0:T(8,128)S(1)}, f32[4,2,40,256]{3,2,1,0:T(8,128)S(1)}) custom-call(f32[47,8,128]{2,1,0:T(8,128)S(1)} %shard_map.73.entries, f32[4,4,32,256]{3,2,1,0:T(8,128)S(1)} %shard_map.79.sums, f32[4,4,8,256]{3,2,1,0:T(8,128)S(1)} %get-tuple-element.46.outer_sums, f32[19,4,8,256]{3,2,1,0:T(8,128)S(1)} %get-tuple-element.41.outer, ...), custom_call_target="tpu_custom_call" | custom-call | tf_op jit(solution)/shard_map/pallas_call | solution.py:1032
  20.9 0.6 %shard_map.81.ends = f32[19,2,56,256]{3,2,1,0:T(8,128)S(1)} custom-call(f32[47,8,128]{2,1,0:T(8,128)S(1)} %shard_map.73.entries, f32[19,4,8,256]{3,2,1,0:T(8,128)S(1)} %get-tuple-element.41.outer, f32[11,4,8,256]{3,2,1,0:T(8,128)S(1)} %get-tuple-element.42.second, f32[19,2,32,256]{3,2,1,0:T(8,128)S(1)} %get-tuple-element.43.relaxed, ...), custom_call_target="tpu_custom_call" | custom-call | tf_op jit(solution)/shard_map/pallas_call | solution.py:1038
  21.5 1.5 %shard_map.84.refs_2_.middle = f32[19,2,56,256]{3,2,1,0:T(8,128)S(1)} custom-call(f32[47,8,128]{2,1,0:T(8,128)S(1)} %shard_map.73.entries, f32[19,2,56,256]{3,2,1,0:T(8,128)S(1)} %shard_map.81.ends, f32[19,2,56,256]{3,2,1,0:T(8,128)S(1)} %get-tuple-element.49.middle, f32[4,2,40,256]{3,2,1,0:T(8,128)S(1)} %get-tuple-element.52.solid), custom_call_target="tpu_custom_call" | custom-call | tf_op jit(solution)/shard_map/pallas_call | solution.py:1041
  23.0 2.4 %collective-permute-done.5.refs_0_ = f32[176,256]{1,0:T(8,128)S(1)} collective-permute-done((f32[176,256]{1,0:T(8,128)S(1)}, f32[176,256]{1,0:T(8,128)S(1)}, u32[]{:S(2)}, u32[]{:S(2)}) %collective-permute-start.5) | collective-permute-done | bytes 180256 | tf_op jit(solution)/shard_map/ppermute | solution.py:944
  25.4 1.1 %shard_map.85 = (f32[160,256]{1,0:T(8,128)S(1)}, f32[160,256]{1,0:T(8,128)S(1)}) custom-call(f32[47,8,128]{2,1,0:T(8,128)S(1)} %shard_map.73.entries, f32[19,2,56,256]{3,2,1,0:T(8,128)S(1)} %shard_map.81.ends, f32[19,2,56,256]{3,2,1,0:T(8,128)S(1)} %get-tuple-element.49.middle, f32[4,2,40,256]{3,2,1,0:T(8,128)S(1)} %get-tuple-element.48.solid, ...), custom_call_target="tpu_custom_call" | custom-call | tf_op jit(solution)/shard_map/pallas_call | solution.py:1045
  26.6 0.9 %collective-permute-start.7 = (f32[160,256]{1,0:T(8,128)S(1)}, f32[160,256]{1,0:T(8,128)S(1)}, u32[]{:S(2)}, u32[]{:S(2)}) collective-permute-start(f32[160,256]{1,0:T(8,128)S(1)} %get-tuple-element.53), channel_id=1, source_target_pairs={{0,28},{4,8},{8,4},{12,16},{16,12},{20,24},{24,20},{28,0},{1,29},{... | collective-permute-start | bytes 491528 | tf_op jit(solution)/shard_map/ppermute | solution.py:944
  27.5 1.4 %shard_map.83.ends = f32[19,2,56,256]{3,2,1,0:T(8,128)S(1)} custom-call(f32[47,8,128]{2,1,0:T(8,128)S(1)} %shard_map.73.entries, f32[19,2,56,256]{3,2,1,0:T(8,128)S(1)} %shard_map.81.ends, f32[19,2,56,256]{3,2,1,0:T(8,128)S(1)} %get-tuple-element.49.middle, f32[4,2,40,256]{3,2,1,0:T(8,128)S(1)} %get-tuple-element.48.solid, ...), custom_call_target="tpu_custom_call" | custom-call | tf_op jit(solution)/shard_map/pallas_call | solution.py:1052
  28.9 1.5 %shard_map.86.given = f32[19,4,32,256]{3,2,1,0:T(8,128)} custom-call(f32[19,2,56,256]{3,2,1,0:T(8,128)S(1)} %shard_map.83.ends, f32[19,2,56,256]{3,2,1,0:T(8,128)S(1)} %shard_map.84.refs_2_.middle), custom_call_target="tpu_custom_call" | custom-call | tf_op jit(solution)/shard_map/pallas_call | solution.py:1054
  30.4 2.7 %collective-permute-done.7.far = f32[160,256]{1,0:T(8,128)S(1)} collective-permute-done((f32[160,256]{1,0:T(8,128)S(1)}, f32[160,256]{1,0:T(8,128)S(1)}, u32[]{:S(2)}, u32[]{:S(2)}) %collective-permute-start.7) | collective-permute-done | bytes 163872 | tf_op jit(solution)/shard_map/ppermute | solution.py:944
  33.1 0.8 %shard_map.87 = f32[19,4,32,256]{3,2,1,0:T(8,128)} custom-call(f32[19,2,56,256]{3,2,1,0:T(8,128)S(1)} %shard_map.83.ends, f32[160,256]{1,0:T(8,128)S(1)} %collective-permute-done.7.far, f32[160,256]{1,0:T(8,128)S(1)} %collective-permute-done.8.near, f32[19,4,32,256]{3,2,1,0:T(8,128)} %shard_map.86.given), custom_call_target="tpu_custom_call", output_to_operand_aliasing={{}: (3, {})} | custom-call | tf_op jit(solution)/shard_map/pallas_call | solution.py:1062
  (13 shorter events, 0.0 us)
Async XLA Ops:
  0.0 5.2 %copy-start.1 = (f32[19]{0:T(128)S(1)}, f32[19]{0:T(128)}, u32[]{:S(2)}) copy-start(f32[19]{0:T(128)} %rates.1) | copy-start | bytes 232
  0.0 13.9 %copy-start = (f32[19,4,32,256]{3,2,1,0:T(8,128)S(1)}, f32[19,4,32,256]{3,2,1,0:T(8,128)}, u32[]{:S(2)}) copy-start(f32[19,4,32,256]{3,2,1,0:T(8,128)} %populations.5) | copy-start | bytes 7471108
  1.8 4.9 %collective-permute-start = (f32[8,128]{1,0:T(8,128)S(1)}, f32[8,128]{1,0:T(8,128)S(1)}, u32[]{:S(2)}, u32[]{:S(2)}) collective-permute-start(f32[8,128]{1,0:T(8,128)S(1)} %get-tuple-element.31), channel_id=1, source_target_pairs={{0,28},{4,8},{8,4},{12,16},{16,12},{20,24},{24,20},{28,0},{1,29},{... | collective-permute-start | bytes 12296 | tf_op jit(solution)/shard_map/ppermute | solution.py:944
  5.2 1.6 %collective-permute-start.1 = (f32[8,128]{1,0:T(8,128)S(1)}, f32[8,128]{1,0:T(8,128)S(1)}, u32[]{:S(2)}, u32[]{:S(2)}) collective-permute-start(f32[8,128]{1,0:T(8,128)S(1)} %get-tuple-element.32), channel_id=1, source_target_pairs={{0,4},{4,0},{8,12},{12,8},{16,20},{20,16},{24,28},{28,24},{1,5},{5... | collective-permute-start | bytes 12296 | tf_op jit(solution)/shard_map/ppermute | solution.py:944
  6.8 10.1 %collective-permute-start.3 = (f32[160,256]{1,0:T(8,128)S(1)}, f32[160,256]{1,0:T(8,128)S(1)}, u32[]{:S(2)}, u32[]{:S(2)}) collective-permute-start(f32[160,256]{1,0:T(8,128)S(1)} %get-tuple-element.39), channel_id=1, source_target_pairs={{0,0},{1,2},{2,1},{3,3},{4,4},{5,6},{6,5},{7,7},{8,8},{9,10},{10,9... | collective-permute-start | bytes 491528 | tf_op jit(solution)/shard_map/ppermute | solution.py:944
  7.4 9.4 %collective-permute-start.4 = (f32[160,256]{1,0:T(8,128)S(1)}, f32[160,256]{1,0:T(8,128)S(1)}, u32[]{:S(2)}, u32[]{:S(2)}) collective-permute-start(f32[160,256]{1,0:T(8,128)S(1)} %get-tuple-element.40), channel_id=1, source_target_pairs={{0,1},{1,0},{2,3},{3,2},{4,5},{5,4},{6,7},{7,6},{8,9},{9,8},{10,11... | collective-permute-start | bytes 491528 | tf_op jit(solution)/shard_map/ppermute | solution.py:944
  12.4 4.5 %collective-permute-start.2 = (f32[8,128]{1,0:T(8,128)S(1)}, f32[8,128]{1,0:T(8,128)S(1)}, u32[]{:S(2)}, u32[]{:S(2)}) collective-permute-start(f32[8,128]{1,0:T(8,128)S(1)} %get-tuple-element.38.column), channel_id=1, source_target_pairs={{0,2},{1,3},{2,0},{3,1},{4,6},{5,7},{6,4},{7,5},{8,10},{9,11},{10,... | collective-permute-start | bytes 12296 | tf_op jit(solution)/shard_map/ppermute | solution.py:932
  18.0 7.4 %collective-permute-start.5 = (f32[176,256]{1,0:T(8,128)S(1)}, f32[176,256]{1,0:T(8,128)S(1)}, u32[]{:S(2)}, u32[]{:S(2)}) collective-permute-start(f32[176,256]{1,0:T(8,128)S(1)} %get-tuple-element.50), channel_id=1, source_target_pairs={{0,28},{4,8},{8,4},{12,16},{16,12},{20,24},{24,20},{28,0},{1,29},{... | collective-permute-start | bytes 540680 | tf_op jit(solution)/shard_map/ppermute | solution.py:944
  19.5 6.0 %collective-permute-start.6 = (f32[176,256]{1,0:T(8,128)S(1)}, f32[176,256]{1,0:T(8,128)S(1)}, u32[]{:S(2)}, u32[]{:S(2)}) collective-permute-start(f32[176,256]{1,0:T(8,128)S(1)} %get-tuple-element.51), channel_id=1, source_target_pairs={{0,4},{4,0},{8,12},{12,8},{16,20},{20,16},{24,28},{28,24},{1,5},{5... | collective-permute-start | bytes 540680 | tf_op jit(solution)/shard_map/ppermute | solution.py:944
  26.6 6.5 %collective-permute-start.7 = (f32[160,256]{1,0:T(8,128)S(1)}, f32[160,256]{1,0:T(8,128)S(1)}, u32[]{:S(2)}, u32[]{:S(2)}) collective-permute-start(f32[160,256]{1,0:T(8,128)S(1)} %get-tuple-element.53), channel_id=1, source_target_pairs={{0,28},{4,8},{8,4},{12,16},{16,12},{20,24},{24,20},{28,0},{1,29},{... | collective-permute-start | bytes 491528 | tf_op jit(solution)/shard_map/ppermute | solution.py:944
  27.5 5.7 %collective-permute-start.8 = (f32[160,256]{1,0:T(8,128)S(1)}, f32[160,256]{1,0:T(8,128)S(1)}, u32[]{:S(2)}, u32[]{:S(2)}) collective-permute-start(f32[160,256]{1,0:T(8,128)S(1)} %get-tuple-element.54), channel_id=1, source_target_pairs={{0,4},{4,0},{8,12},{12,8},{16,20},{20,16},{24,28},{28,24},{1,5},{5... | collective-permute-start | bytes 491528 | tf_op jit(solution)/shard_map/ppermute | solution.py:944

commit v6 on v5

--- a/solution.py
+++ b/solution.py
@@ -551,32 +551,34 @@
             sums[c, x, :, :] = totals[at : at + size_y]
 
 
-def outer_kernel(size_x, size_y, size_z, count, shifts, column, *refs):
-    rest, (two, one, sums, outer, second, migrants) = refs[: len(shifts)], refs[len(shifts) :]
-    arrivals(size_x, size_y, size_z, count, shifts, column, one, two, rest, migrants)
+def outer_kernel(size_x, size_y, size_z, count, shifts, planes, *refs):
+    if planes[0] == 0:
+        column, *rest = refs[: 1 + len(shifts)]
+        two, one, sums, outer, second, migrants = refs[1 + len(shifts) :]
+        arrivals(size_x, size_y, size_z, count, shifts, column, one, two, rest, migrants)
+    else:
+        two, one, sums, outer, second = refs
     blank = jnp.zeros((8, size_z), F32)
     ones = jnp.ones((8, size_z), F32)
     _, at_sums, at_second, _ = edge_rows(size_x)
 
     def write(above, below):
-        for c in range(4):
-            for x in range(size_x):
+        for p, x in enumerate(planes):
+            for c in range(4):
                 at = at_sums + c * 2 * size_x + 2 * x
-                sums[c, x, :, :] = blank
-                sums[c, x, 0:2, :] = above[at : at + 2, :]
-                sums[c, x, 6:8, :] = below[at : at + 2, :]
-        for i in range(19):
-            for x in range(size_x):
+                sums[c, p, :, :] = blank
+                sums[c, p, 0:2, :] = above[at : at + 2, :]
+                sums[c, p, 6:8, :] = below[at : at + 2, :]
+            for i in range(19):
                 at = i * size_x + x
-                outer[i, x, :, :] = ones
-                outer[i, x, 0:1, :] = above[at : at + 1, :]
-                outer[i, x, 7:8, :] = below[at : at + 1, :]
-        for k in range(11):
-            for x in range(size_x):
+                outer[i, p, :, :] = ones
+                outer[i, p, 0:1, :] = above[at : at + 1, :]
+                outer[i, p, 7:8, :] = below[at : at + 1, :]
+            for k in range(11):
                 at = at_second + k * size_x + x
-                second[k, x, :, :] = ones
-                second[k, x, 1:2, :] = above[at : at + 1, :]
-                second[k, x, 6:7, :] = below[at : at + 1, :]
+                second[k, p, :, :] = ones
+                second[k, p, 1:2, :] = above[at : at + 1, :]
+                second[k, p, 6:7, :] = below[at : at + 1, :]
 
     even = lax.rem(lax.axis_index("gy"), 2) == 0
 
@@ -650,24 +652,23 @@
     return value if shift == 0 else pltpu.roll(value, shift % size_z, 1)
 
 
-def solids(size_x, size_y, size_z, planes, sums, outer_sums, migrants, solid):
+def solids(size_x, size_y, size_z, planes, first, sums, outer_sums, migrants, solid):
     a_x, a_y, a_z = (migrants[k : k + 1, :].astype(I32) for k in (32, 33, 34))
     wide = size_y + 8
     index = iota((len(planes) * wide, 1), 0)
     number = lax.div(index, jnp.int32(wide))
     row = index - number * wide
-    rows_x = number + planes[0] if len(planes) == planes[-1] - planes[0] + 1 else number * (size_x - 1)
     rows_y = jnp.where(row < size_y + 2, row, jnp.where(row >= size_y + 6, row - wide, -3 * size_y))
     big = 4 * size_y * (lax.axis_size("gy") + 2)
     totals = deposited(
-        [(rows_x, rows_y)], migrants[0:27, :], migrants[27:30, :], a_x, a_y, a_z, size_z, big
+        [(number + planes[0], rows_y)], migrants[0:27, :], migrants[27:30, :], a_x, a_y, a_z, size_z, big
     )
     cells = len(planes) * wide
     for p, x in enumerate(planes):
         parts = []
         for c in range(4):
             at = c * cells + p * wide
-            solid_sum = jnp.concatenate([sums[c, x, :, :], outer_sums[c, x, :, :]], axis=0)
+            solid_sum = jnp.concatenate([sums[c, x, :, :], outer_sums[c, first + p, :, :]], axis=0)
             parts.append(totals[at : at + wide] + solid_sum)
         scale = 1.0 / (parts[0] + 1e-06)
         solid[0, p, :, :] = jnp.minimum(parts[0], 1.0)
@@ -675,22 +676,22 @@
             solid[c, p, :, :] = parts[c] * scale
 
 
-def outer_collision(solid, outer, second, blocks, p, x, lanes, rows):
-    share, *flow = (solid[c, p, rows, lanes] for c in range(4))
-    out = collide([outer[i, x, :, lanes] for i in range(19)], share, *flow, blocks)
+def outer_collision(solid, outer, second, blocks, p, lanes):
+    share, *flow = solid
+    out = collide([outer[i, p, :, lanes] for i in range(19)], share, *flow, blocks)
     line = iota((8, 128), 0)
     away = jnp.where(line < 4, 1.0, -1.0)
     still = equilibrium(None, [away * v for v in flow], DOWNWARD)
-    density = second[10, x, :, lanes]
+    density = second[10, p, :, lanes]
     for k, (i, j) in enumerate(zip(DOWNWARD, UPWARD)):
-        value = blended(second[k, x, :, lanes], second[5 + k, x, :, lanes], density, share, still[i])
+        value = blended(second[k, p, :, lanes], second[5 + k, p, :, lanes], density, share, still[i])
         out[i] = jnp.where(line == 1, value, out[i])
         out[j] = jnp.where(line == 6, value, out[j])
     return out
 
 
 def prepared_collision(solid, relaxed, bounced, dense, p, rows, lanes, numbers):
-    share, *flow = (solid[c, p, rows, lanes] for c in range(4))
+    share, *flow = solid
     still = equilibrium(None, flow, numbers)
     density = dense[p, rows, lanes]
     return {
@@ -705,37 +706,59 @@
             yield tile, slice(8 * tile, 8 * tile + 8), part, slice(128 * part, 128 * part + 128)
 
 
+def by_plane(work, far):
+    even = even_x()
+
+    @pl.when(even if far else jnp.logical_not(even))
+    def _():
+        work(0, BACKWARD)
+
+    @pl.when(jnp.logical_not(even) if far else even)
+    def _():
+        work(1, FORWARD)
+
+
 def leaving_kernel(
-    size_x, size_y, size_z, entries, sums, outer_sums, outer, second, migrants, relaxed, bounced, dense,
-    solid, near, far, leaving
+    size_x, size_y, size_z, far, entries, sums, outer_sums, outer, second, migrants, relaxed, bounced,
+    dense, *refs
 ):
+    solid, message, leaving = refs[-3:]
     tiles = size_y // 8
-    planes = (0, size_x - 1)
-    solids(size_x, size_y, size_z, planes, sums, outer_sums, migrants, solid)
-    blocks = relax_blocks(entries)
-    for p, x in enumerate(planes):
-        numbers = FORWARD if p else BACKWARD
+
+    def work(place, numbers):
+        plane = place * (size_x - 1)
+        solids(size_x, size_y, size_z, (plane,), place, sums, outer_sums, migrants, solid)
+        blocks = relax_blocks(entries)
         for tile, rows, part, lanes in tile_parts(size_y, size_z):
+            s = [solid[c, 0, rows, lanes] for c in range(4)]
             if tile == tiles:
-                out = outer_collision(solid, outer, second, blocks, p, x, lanes, rows)
+                out = outer_collision(s, outer, second, blocks, place, lanes)
             else:
-                out = prepared_collision(solid, relaxed, bounced, dense, p, rows, lanes, numbers)
+                out = prepared_collision(s, relaxed, bounced, dense, place, rows, lanes, numbers)
             for k, i in enumerate(numbers):
-                store_padded(leaving, k, p, tile, part, out[i], tiles)
-    send_faces(leaving, near, far, size_y, size_z, True)
+                store_padded(leaving, k, 0, tile, part, out[i], tiles)
+        write_face(leaving, message, numbers, size_y, size_z, True)
+
+    by_plane(work, far)
+
+
+def plane_solid(far, near, place, rows, lanes):
+    in_far = even_x() if place == 0 else jnp.logical_not(even_x())
+    return [jnp.where(in_far, far[c, 0, rows, lanes], near[c, 0, rows, lanes]) for c in range(4)]
 
 
 def ends_kernel(
-    size_x, size_y, size_z, entries, outer, second, relaxed, bounced, dense, solid, post
+    size_x, size_y, size_z, entries, outer, second, relaxed, bounced, dense, solid_far, solid_near, post
 ):
     tiles = size_y // 8
     blocks = relax_blocks(entries)
-    for p, x in enumerate((0, size_x - 1)):
+    for p in range(2):
         for tile, rows, part, lanes in tile_parts(size_y, size_z):
+            s = plane_solid(solid_far, solid_near, p, rows, lanes)
             if tile == tiles:
-                out = outer_collision(solid, outer, second, blocks, p, x, lanes, rows)
+                out = outer_collision(s, outer, second, blocks, p, lanes)
             else:
-                out = prepared_collision(solid, relaxed, bounced, dense, p, rows, lanes, range(19))
+                out = prepared_collision(s, relaxed, bounced, dense, p, rows, lanes, range(19))
             for i in range(19):
                 store_padded(post, i, p, tile, part, out[i], tiles)
 
@@ -745,47 +768,34 @@
     post, solid
 ):
     tiles = size_y // 8
-    solids(size_x, size_y, size_z, planes, sums, outer_sums, migrants, solid)
+    solids(size_x, size_y, size_z, planes, 0, sums, outer_sums, migrants, solid)
     blocks = relax_blocks(entries)
     for p, x in enumerate(planes):
         for tile, rows, part, lanes in tile_parts(size_y, size_z):
+            share, *flow = (solid[c, p, rows, lanes] for c in range(4))
             if tile == tiles:
-                out = outer_collision(solid, outer, second, blocks, p, x, lanes, rows)
+                out = outer_collision((share, *flow), outer, second, blocks, p, lanes)
             else:
-                share, *flow = (solid[c, p, rows, lanes] for c in range(4))
                 h = [populations[i, x, rows, lanes] for i in range(19)]
                 out = collide(h, share, *flow, blocks)
             for i in range(19):
                 store_padded(post, i, p, tile, part, out[i], tiles)
 
 
-def send_faces(post, near, far, size_y, size_z, outer):
-    even = even_x()
-
-    @pl.when(even)
-    def _():
-        faces(post, near, far, size_y, size_z, outer)
-
-    @pl.when(jnp.logical_not(even))
-    def _():
-        faces(post, far, near, size_y, size_z, outer)
-
-
-def faces(post, ahead, behind, size_y, size_z, outer):
+def write_face(post, message, numbers, size_y, size_z, outer):
     tiles = size_y // 8
-    for target, numbers, p in ((ahead, FORWARD, 1), (behind, BACKWARD, 0)):
-        for k, i in enumerate(numbers):
-            _, c_y, c_z = VEC[i]
-            for tile in range(tiles):
-                at = 8 + 8 * tile - c_y
-                to = k * size_y + 8 * tile
-                target[to : to + 8, :] = turned(post[k, p, at : at + 8, :], c_z, size_z)
-            if outer:
-                at = 8 + size_y - c_y
-                value = turned(post[k, p, at : at + 8, :], c_z, size_z)
-                to = 5 * size_y + 2 * k
-                target[to : to + 1, :] = value[0:1]
-                target[to + 1 : to + 2, :] = value[7:8]
+    for k, i in enumerate(numbers):
+        _, c_y, c_z = VEC[i]
+        for tile in range(tiles):
+            at = 8 + 8 * tile - c_y
+            to = k * size_y + 8 * tile
+            message[to : to + 8, :] = turned(post[k, 0, at : at + 8, :], c_z, size_z)
+        if outer:
+            at = 8 + size_y - c_y
+            value = turned(post[k, 0, at : at + 8, :], c_z, size_z)
+            to = 5 * size_y + 2 * k
+            message[to : to + 1, :] = value[0:1]
+            message[to + 1 : to + 2, :] = value[7:8]
 
 
 def streamed(ends, middle, messages, i, x, tile, size_x, size_y, size_z, walls):
@@ -806,11 +816,14 @@
         at = 8 + 8 * tile - c_y
         value = turned(source[i, p, at : at + 8, :], c_z, size_z)
     else:
-        near, far, even = messages
-        from_near, numbers = (jnp.logical_not(even), FORWARD) if from_x < 0 else (even, BACKWARD)
+        numbers = FORWARD if from_x < 0 else BACKWARD
         k = numbers.index(i)
 
         def received(at, rows):
+            if len(messages) == 1:
+                return messages[0][at : at + rows, :]
+            near, far = messages
+            from_near = jnp.logical_not(even_x()) if from_x < 0 else even_x()
             return jnp.where(from_near, near[at : at + rows, :], far[at : at + rows, :])
 
         if tile < tiles:
@@ -832,32 +845,86 @@
     return here == 0, here == count - 1
 
 
-def second_kernel(size_x, size_y, size_z, count, planes, entries, ends, middle, solid, *refs):
-    refs = list(refs)
-    outside = planes[0] == 0
-    messages = (refs.pop(1), refs.pop(0), even_x()) if outside else None
-    leaving = len(refs) > 1
-    if leaving:
-        del refs[0]
-    tiles = size_y // 8
+def second_kernel(size_x, size_y, size_z, count, entries, ends, middle, solid, later):
     walls = walls_of(count)
     blocks = relax_blocks(entries)
-    for p, x in enumerate(planes):
-        numbers = (FORWARD if p else BACKWARD) if leaving else range(19)
-        for tile in range(tiles + 1):
+    for p in range(size_x - 2):
+        for tile in range(size_y // 8 + 1):
             rows = slice(8 * tile, 8 * tile + 8)
             h = [
-                streamed(ends, middle, messages, i, x, tile, size_x, size_y, size_z, walls)
+                streamed(ends, middle, None, i, p + 1, tile, size_x, size_y, size_z, walls)
                 for i in range(19)
             ]
             for part in range(size_z // 128):
                 lanes = slice(128 * part, 128 * part + 128)
                 s = [solid[c, p, rows, lanes] for c in range(4)]
                 out = collide([v[:, lanes] for v in h], *s, blocks)
-                for k, i in enumerate(numbers):
-                    store_padded(refs[-1], k, p, tile, part, out[i], tiles)
-    if leaving:
-        send_faces(refs[-1], refs[0], refs[1], size_y, size_z, False)
+                for i in range(19):
+                    store_padded(later, i, p, tile, part, out[i], size_y // 8)
+
+
+def second_ends(
+    size_x, size_y, size_z, count, entries, ends, middle, solid, messages, place, numbers, later, p
+):
+    walls = walls_of(count)
+    blocks = relax_blocks(entries)
+    x = place * (size_x - 1)
+    for tile in range(size_y // 8 + 1):
+        rows = slice(8 * tile, 8 * tile + 8)
+        h = [
+            streamed(ends, middle, messages, i, x, tile, size_x, size_y, size_z, walls) for i in range(19)
+        ]
+        for part in range(size_z // 128):
+            lanes = slice(128 * part, 128 * part + 128)
+            s = solid(rows, lanes)
+            out = collide([v[:, lanes] for v in h], *s, blocks)
+            for k, i in enumerate(numbers):
+                store_padded(later, k, p, tile, part, out[i], size_y // 8)
+
+
+def second_leaving_kernel(size_x, size_y, size_z, count, far, entries, ends, middle, solid, received, *refs):
+    message, leaving = refs[-2:]
+
+    def work(place, numbers):
+        second_ends(
+            size_x,
+            size_y,
+            size_z,
+            count,
+            entries,
+            ends,
+            middle,
+            lambda rows, lanes: [solid[c, 0, rows, lanes] for c in range(4)],
+            (received,),
+            place,
+            numbers,
+            leaving,
+            0,
+        )
+        write_face(leaving, message, numbers, size_y, size_z, False)
+
+    by_plane(work, far)
+
+
+def second_ends_kernel(
+    size_x, size_y, size_z, count, entries, ends, middle, solid_far, solid_near, far, near, later
+):
+    for place in range(2):
+        second_ends(
+            size_x,
+            size_y,
+            size_z,
+            count,
+            entries,
+            ends,
+            middle,
+            lambda rows, lanes: plane_solid(solid_far, solid_near, place, rows, lanes),
+            (near, far),
+            place,
+            range(19),
+            later,
+            place,
+        )
 
 
 def last_kernel(size_x, size_y, size_z, count, ends, middle, advanced, held, done):
@@ -881,25 +948,44 @@
         copy.wait()
 
 
-def enter_kernel(
-    size_x, size_y, size_z, count, ends, far, near, given, advanced, held, done
-):
+def entering(size_x, size_y, size_z, count, ends, received, place, k, target):
+    numbers = BACKWARD if place else FORWARD
+    walls = walls_of(count)
+    for tile in range(size_y // 8):
+        target[k, 8 * tile : 8 * tile + 8, :] = streamed(
+            ends, None, (received,), numbers[k], place * (size_x - 1), tile, size_x, size_y, size_z, walls
+        )
+
+
+def far_kernel(size_x, size_y, size_z, count, ends, received, held):
+    def work(place, numbers):
+        del numbers
+        for k in range(5):
+            entering(size_x, size_y, size_z, count, ends, received, place, k, held)
+
+    by_plane(work, True)
+
+
+def enter_kernel(size_x, size_y, size_z, count, ends, received, far, given, advanced, near, done):
     del given
-    messages = (near, far, even_x())
-    walls = walls_of(count)
-    copies = []
-    for x, numbers in ((0, FORWARD), (size_x - 1, BACKWARD)):
-        for i in numbers:
-            k = len(copies)
-            for tile in range(size_y // 8):
-                held[k, 8 * tile : 8 * tile + 8, :] = streamed(
-                    ends, None, messages, i, x, tile, size_x, size_y, size_z, walls
-                )
-            copy = pltpu.make_async_copy(held.at[k], advanced.at[i, x], done.at[k])
+
+    def write(place, held, base):
+        numbers = BACKWARD if place else FORWARD
+        for k, i in enumerate(numbers):
+            copy = pltpu.make_async_copy(held.at[k], advanced.at[i, place * (size_x - 1)], done.at[base + k])
             copy.start()
-            copies.append(copy)
-    for copy in copies:
-        copy.wait()
+
+    def work(place, numbers):
+        del numbers
+        write(1 - place, far, 0)
+        for k in range(5):
+            entering(size_x, size_y, size_z, count, ends, received, place, k, near)
+        write(place, near, 5)
+
+    by_plane(work, False)
+    for k in range(5):
+        pltpu.make_async_copy(far.at[k], advanced.at[FORWARD[k], 0], done.at[k]).wait()
+        pltpu.make_async_copy(near.at[k], advanced.at[FORWARD[k], 0], done.at[5 + k]).wait()
 
 
 def shape(*sizes):
@@ -1002,14 +1088,14 @@
         part(fluid_kernel, *sizes), (plane_pair, plane_pair, shape(2, size_y, size_z)), 16, [VMEM] * 2
     )(entries, populations)
     width = -(-(3 + len(shifts)) * LANES // 128) * 128
+    outside, inside = (0, size_x - 1), tuple(range(1, size_x - 1))
+
+    def outer_shapes(planes):
+        return tuple(shape(k, len(planes), 8, size_z) for k in (4, 19, 11))
+
     outer_sums, outer, second, migrants = call(
-        part(outer_kernel, *sizes, count, shifts),
-        (
-            shape(4, size_x, 8, size_z),
-            shape(19, size_x, 8, size_z),
-            shape(11, size_x, 8, size_z),
-            shape(40, width),
-        ),
+        part(outer_kernel, *sizes, count, shifts, outside),
+        outer_shapes(outside) + (shape(40, width),),
         8,
         [VMEM] * (3 + len(shifts)),
     )(column, *rest, two, one)
@@ -1020,37 +1106,56 @@
     def solid_shape(planes):
         return shape(4, planes, size_y + 8, size_z)
 
-    outside, inside = (0, size_x - 1), tuple(range(1, size_x - 1))
-    sent = pltpu.VMEM((5, 2, size_y + 24, size_z), F32)
+    unused = pl.BlockSpec(memory_space=pl.ANY)
+    sent = pltpu.VMEM((5, 1, size_y + 24, size_z), F32)
     wide_face = shape((5 * size_y + 10 + 7) // 8 * 8, size_z)
     face = shape(5 * size_y, size_z)
-    known = (entries, sums, outer_sums, outer, second, migrants)
-    solid_ends, near, far = call(
-        part(leaving_kernel, *sizes), (solid_shape(2), wide_face, wide_face), 16, [VMEM] * 9, scratch=[sent]
-    )(*known, *parts)
+
+    def leaving(far, *given):
+        return call(
+            part(leaving_kernel, *sizes, far),
+            (solid_shape(1), wide_face),
+            16,
+            [VMEM] * 9 + [unused] * (len(given) - 9),
+            scratch=[sent],
+        )(*given)
+
+    known = (entries, sums, outer_sums, outer, second, migrants, *parts)
+    solid_far, far = leaving(True, *known)
+    solid_near, near = leaving(False, *known, solid_far)
     near, far = exchanged(near, far)
+    inner = call(part(outer_kernel, *sizes, count, shifts, inside), outer_shapes(inside), 8, [VMEM] * 2)(
+        two, one
+    )
     middle, solid_middle = call(
         part(middle_kernel, *sizes, inside),
         (padded(len(inside)), solid_shape(len(inside))),
         16,
         [VMEM] * 7,
-    )(*known, populations)
-    ends = call(part(ends_kernel, *sizes), padded(2), 16, [VMEM] * 7)(
-        entries, outer, second, *parts, solid_ends
-    )
-    later_middle = call(
-        part(second_kernel, *sizes, count, inside), padded(len(inside)), 16, [VMEM] * 4
-    )(entries, ends, middle, solid_middle)
-    given = (entries, ends, middle, solid_ends, far, near)
-    near, far = call(
-        part(second_kernel, *sizes, count, outside),
-        (face, face),
-        16,
-        [VMEM] * 6 + [pl.BlockSpec(memory_space=pl.ANY)],
-        scratch=[sent],
-    )(*given, later_middle)
-    later_ends = call(part(second_kernel, *sizes, count, outside), padded(2), 16, [VMEM] * 6)(*given)
+    )(entries, sums, *inner, migrants, populations)
+    ends = call(part(ends_kernel, *sizes), padded(2), 16, [VMEM] * 8)(
+        entries, outer, second, *parts, solid_far, solid_near
+    )
+    later_middle = call(part(second_kernel, *sizes, count), padded(len(inside)), 16, [VMEM] * 4)(
+        entries, ends, middle, solid_middle
+    )
+
+    def second_leaving(far, *given):
+        return call(
+            part(second_leaving_kernel, *sizes, count, far),
+            face,
+            16,
+            [VMEM] * 5 + [unused] * (len(given) - 5),
+            scratch=[sent],
+        )(*given)
+
+    received = (far, near)
+    far = second_leaving(True, entries, ends, middle, solid_far, far, later_middle)
+    near = second_leaving(False, entries, ends, middle, solid_near, near, far)
     near, far = exchanged(near, far)
+    later_ends = call(part(second_ends_kernel, *sizes, count), padded(2), 16, [VMEM] * 7)(
+        entries, ends, middle, solid_far, solid_near, *received
+    )
     advanced = call(
         part(last_kernel, *sizes, count),
         shape(19, *sizes),
@@ -1059,15 +1164,17 @@
         HBM,
         [pltpu.VMEM((19, *sizes), F32), pltpu.SemaphoreType.DMA((19,))],
     )(later_ends, later_middle)
+    slabs = (5, size_y, size_z)
+    far = call(part(far_kernel, *sizes, count), shape(*slabs), 16, [VMEM] * 2)(later_ends, far)
     return call(
         part(enter_kernel, *sizes, count),
         shape(19, *sizes),
         16,
         [VMEM] * 3 + [HBM],
         HBM,
-        [pltpu.VMEM((10, size_y, size_z), F32), pltpu.SemaphoreType.DMA((10,))],
+        [pltpu.VMEM(slabs, F32), pltpu.SemaphoreType.DMA((10,))],
         {3: 0},
-    )(later_ends, far, near, advanced)
+    )(later_ends, near, far, advanced)
 
 
 def solution(mesh):

time: 34.1 us -> 33.3 us (0.977)
  waiting for transfers between devices: 7.02 us -> 5.58 us
  Pallas kernels: 15.4 us -> 15.8 us
    ppermute x8, waiting for transfers between devices: 5.15 us -> 3.73 us  [paired(): return lax.ppermute(value, axis, pairs)]
    pallas_call x6 -> x10, Pallas kernels: 5.78 us -> 6.05 us  [the longest x1 1.49 us: local(): call(part(second_kernel, *sizes, count), padded(len(inside)), 16, [VMEM]...]
  transfers between devices with their start and end apart: 9 -> 9, of which waited for: 3 -> 3; matrix products, arithmetic and copies ran while one was open for 0% -> 0% of each run, Pallas kernels for 31% -> 37%
where the time goes in v6:
time: 33.3 us; the launch traced here: 33.2 us
  Pallas kernels  15.8 us (47%)
  starting transfers between devices  11.5 us (35%)
  waiting for transfers between devices  5.58 us (17%)
  between operations  0.34 us (1%)
    ppermute x8, starting transfers between devices, paired(): return lax.ppermute(value, axis, pairs)  11.5 us
    ppermute x8, waiting for transfers between devices, paired(): return lax.ppermute(value, axis, pairs)  3.73 us
    ppermute x1, waiting for transfers between devices, around(): lax.ppermute(value, axis, [(i, (i + steps) % count) for i in range(count)])  1.85 us
    pallas_call x1, Pallas kernels, local(): call(pack_kernel, (shape(32, rows), packed, packed, packed, band, band),...  1.77 us
    pallas_call x1, Pallas kernels, local(): call(part(last_kernel, *sizes, count), shape(19, *sizes), 16, [VMEM] * 2,...  1.5 us
    pallas_call x1, Pallas kernels, local(): sums = call(part(stay_kernel, *sizes), shape(4, *sizes), 16, [VMEM])(table)  1.5 us
    pallas_call x1, Pallas kernels, local(): call(part(second_kernel, *sizes, count), padded(len(inside)), 16, [VMEM]...  1.49 us
    pallas_call x1, Pallas kernels, local(): call(part(middle_kernel, *sizes, inside), (padded(len(inside)), solid_sha...  1.47 us
  transfers between devices with their start and end apart: 9, of which 3 were waited for; matrix products, arithmetic and copies ran while one was open for 0% of the time, Pallas kernels for 37%

profile of v6, /device:TPU:0, one launch (start us, length us, event | category | flops | bytes accessed | tf_op | source)
XLA Modules:
  0.0 33.2 jit_solution(11834331198057957429)
XLA Ops:
  0.0 1.8 %shard_map.74 = (f32[32,512]{1,0:T(8,128)S(1)}, f32[8,128]{1,0:T(8,128)S(1)}, f32[8,128]{1,0:T(8,128)S(1)}, f32[8,128]{1,0:T(8,128)S(1)}, f32[19,4,8,256]{3,2,1,0:T(8,128)S(1)}, /*index=5*/f32[19,4,8,256]{3,2,1,0:T(8,128)S(1)}) custom-call(f32[3,512]{1,0:T(4,128)} %velocity_in.1, f32[3,512]{1,0:T(4,128)} %change_in.1, f32[27,512]{1,0:T(8,128)} %fractions_in.1, ...), custom_call_target="tpu_custom_call" | custom-call | tf_op jit(solution)/shard_map/pallas_call | solution.py:1046
  1.8 3.4 %collective-permute-start = (f32[8,128]{1,0:T(8,128)S(1)}, f32[8,128]{1,0:T(8,128)S(1)}, u32[]{:S(2)}, u32[]{:S(2)}) collective-permute-start(f32[8,128]{1,0:T(8,128)S(1)} %get-tuple-element.33), channel_id=1, source_target_pairs={{0,28},{4,8},{8,4},{12,16},{16,12},{20,24},{24,20},{28,0},{1,29},{... | collective-permute-start | bytes 12296 | tf_op jit(solution)/shard_map/ppermute | solution.py:1030
  5.2 0.6 %shard_map.73.entries = f32[47,8,128]{2,1,0:T(8,128)S(1)} custom-call(f32[19]{0:T(128)S(1)} %copy-done.1), custom_call_target="tpu_custom_call" | custom-call | tf_op jit(solution)/shard_map/pallas_call | solution.py:1064
  5.8 0.9 %shard_map.75 = (f32[160,256]{1,0:T(8,128)S(1)}, f32[160,256]{1,0:T(8,128)S(1)}) custom-call(f32[19,4,8,256]{3,2,1,0:T(8,128)S(1)} %get-tuple-element.35.bottom, f32[19,4,8,256]{3,2,1,0:T(8,128)S(1)} %get-tuple-element.36.top, f32[32,512]{1,0:T(8,128)S(1)} %get-tuple-element.37.table, f32[47,8,128]{2,1,0:T(8,128)S(1)} %shard_map.73.entries), custom_call_target="tpu_custom_call" | custom-call | tf_op jit(solution)/shard_map/pallas_call | solution.py:1065
  6.8 0.7 %collective-permute-start.3 = (f32[160,256]{1,0:T(8,128)S(1)}, f32[160,256]{1,0:T(8,128)S(1)}, u32[]{:S(2)}, u32[]{:S(2)}) collective-permute-start(f32[160,256]{1,0:T(8,128)S(1)} %get-tuple-element.41), channel_id=1, source_target_pairs={{0,0},{1,2},{2,1},{3,3},{4,4},{5,6},{6,5},{7,7},{8,8},{9,10},{10,9... | collective-permute-start | bytes 491528 | tf_op jit(solution)/shard_map/ppermute | solution.py:1030
  7.4 4.9 %collective-permute-start.4 = (f32[160,256]{1,0:T(8,128)S(1)}, f32[160,256]{1,0:T(8,128)S(1)}, u32[]{:S(2)}, u32[]{:S(2)}) collective-permute-start(f32[160,256]{1,0:T(8,128)S(1)} %get-tuple-element.42), channel_id=1, source_target_pairs={{0,1},{1,0},{2,3},{3,2},{4,5},{5,4},{6,7},{7,6},{8,9},{9,8},{10,11... | collective-permute-start | bytes 491528 | tf_op jit(solution)/shard_map/ppermute | solution.py:1030
  12.4 1.5 %shard_map.79.sums = f32[4,4,32,256]{3,2,1,0:T(8,128)S(1)} custom-call(f32[32,512]{1,0:T(8,128)S(1)} %get-tuple-element.37.table), custom_call_target="tpu_custom_call" | custom-call | tf_op jit(solution)/shard_map/pallas_call | solution.py:1085
  13.9 1.1 %shard_map.78 = (f32[19,2,32,256]{3,2,1,0:T(8,128)S(1)}, f32[19,2,32,256]{3,2,1,0:T(8,128)S(1)}, f32[2,32,256]{2,1,0:T(8,128)S(1)}) custom-call(f32[47,8,128]{2,1,0:T(8,128)S(1)} %shard_map.73.entries, f32[19,4,32,256]{3,2,1,0:T(8,128)S(1)} %copy-done), custom_call_target="tpu_custom_call" | custom-call | tf_op jit(solution)/shard_map/pallas_call | solution.py:1087
  15.0 1.8 %collective-permute-done.2.refs_1_ = f32[8,128]{1,0:T(8,128)S(1)} collective-permute-done((f32[8,128]{1,0:T(8,128)S(1)}, f32[8,128]{1,0:T(8,128)S(1)}, u32[]{:S(2)}, u32[]{:S(2)}) %collective-permute-start.2) | collective-permute-done | bytes 4128 | tf_op jit(solution)/shard_map/ppermute | solution.py:1018
  16.9 0.2 shard_map.77
  17.1 0.6 %shard_map.80 = (f32[4,1,40,256]{3,2,1,0:T(8,128)S(1)}, f32[176,256]{1,0:T(8,128)S(1)}) custom-call(f32[47,8,128]{2,1,0:T(8,128)S(1)} %shard_map.73.entries, f32[4,4,32,256]{3,2,1,0:T(8,128)S(1)} %shard_map.79.sums, f32[4,2,8,256]{3,2,1,0:T(8,128)S(1)} %get-tuple-element.48.outer_sums, f32[19,2,8,256]{3,2,1,0:T(8,128)S(1)} %get-tuple-element.43.outer, ...), custom_call_target="tpu_custom_call" | custom-call | tf_op jit(solution)/shard_map/pallas_call | solution.py:1115
  17.6 1.4 %collective-permute-start.5 = (f32[176,256]{1,0:T(8,128)S(1)}, f32[176,256]{1,0:T(8,128)S(1)}, u32[]{:S(2)}, u32[]{:S(2)}) collective-permute-start(f32[176,256]{1,0:T(8,128)S(1)} %get-tuple-element.56), channel_id=1, source_target_pairs={{0,28},{4,8},{8,4},{12,16},{16,12},{20,24},{24,20},{28,0},{1,29},{... | collective-permute-start | bytes 540680 | tf_op jit(solution)/shard_map/ppermute | solution.py:1030
  19.0 0.5 %shard_map.81 = (f32[4,1,40,256]{3,2,1,0:T(8,128)S(1)}, f32[176,256]{1,0:T(8,128)S(1)}) custom-call(f32[47,8,128]{2,1,0:T(8,128)S(1)} %shard_map.73.entries, f32[4,4,32,256]{3,2,1,0:T(8,128)S(1)} %shard_map.79.sums, f32[4,2,8,256]{3,2,1,0:T(8,128)S(1)} %get-tuple-element.48.outer_sums, f32[19,2,8,256]{3,2,1,0:T(8,128)S(1)} %get-tuple-element.43.outer, ...), custom_call_target="tpu_custom_call" | custom-call | tf_op jit(solution)/shard_map/pallas_call | solution.py:1115
  19.6 0.7 %shard_map.82.ends = f32[19,2,56,256]{3,2,1,0:T(8,128)S(1)} custom-call(f32[47,8,128]{2,1,0:T(8,128)S(1)} %shard_map.73.entries, f32[19,2,8,256]{3,2,1,0:T(8,128)S(1)} %get-tuple-element.43.outer, f32[11,2,8,256]{3,2,1,0:T(8,128)S(1)} %get-tuple-element.44.second, f32[19,2,32,256]{3,2,1,0:T(8,128)S(1)} %get-tuple-element.45.relaxed, ...), custom_call_target="tpu_custom_call" | custom-call | tf_op jit(solution)/shard_map/pallas_call | solution.py:1136
  20.4 1.5 %shard_map.84 = (f32[19,2,56,256]{3,2,1,0:T(8,128)S(1)}, f32[4,2,40,256]{3,2,1,0:T(8,128)S(1)}) custom-call(f32[47,8,128]{2,1,0:T(8,128)S(1)} %shard_map.73.entries, f32[4,4,32,256]{3,2,1,0:T(8,128)S(1)} %shard_map.79.sums, f32[4,2,8,256]{3,2,1,0:T(8,128)S(1)} %get-tuple-element.52.outer_sums, f32[19,2,8,256]{3,2,1,0:T(8,128)S(1)} %get-tuple-element.53.outer, ...), custom_call_target="tpu_custom_call" | custom-call | tf_op jit(solution)/shard_map/pallas_call | solution.py:1130
  21.9 1.5 %shard_map.86.refs_0_.middle = f32[19,2,56,256]{3,2,1,0:T(8,128)S(1)} custom-call(f32[47,8,128]{2,1,0:T(8,128)S(1)} %shard_map.73.entries, f32[19,2,56,256]{3,2,1,0:T(8,128)S(1)} %shard_map.82.ends, f32[19,2,56,256]{3,2,1,0:T(8,128)S(1)} %get-tuple-element.55.middle, f32[4,2,40,256]{3,2,1,0:T(8,128)S(1)} %get-tuple-element.58.solid), custom_call_target="tpu_custom_call" | custom-call | tf_op jit(solution)/shard_map/pallas_call | solution.py:1139
  23.4 1.7 %collective-permute-done.5.far.received = f32[176,256]{1,0:T(8,128)S(1)} collective-permute-done((f32[176,256]{1,0:T(8,128)S(1)}, f32[176,256]{1,0:T(8,128)S(1)}, u32[]{:S(2)}, u32[]{:S(2)}) %collective-permute-start.5) | collective-permute-done | bytes 180256 | tf_op jit(solution)/shard_map/ppermute | solution.py:1030
  25.0 0.5 %shard_map.87.refs_0_ = f32[160,256]{1,0:T(8,128)S(1)} custom-call(f32[47,8,128]{2,1,0:T(8,128)S(1)} %shard_map.73.entries, f32[19,2,56,256]{3,2,1,0:T(8,128)S(1)} %shard_map.82.ends, f32[19,2,56,256]{3,2,1,0:T(8,128)S(1)} %get-tuple-element.55.middle, f32[4,1,40,256]{3,2,1,0:T(8,128)S(1)} %get-tuple-element.50.refs_0_.solid_far.solid, ...), custom_call_target="tpu_custom_call" | custom-call | tf_op jit(solution)/shard_map/pallas_call | solution.py:1144
  25.6 0.9 %collective-permute-start.8 = (f32[160,256]{1,0:T(8,128)S(1)}, f32[160,256]{1,0:T(8,128)S(1)}, u32[]{:S(2)}, u32[]{:S(2)}) collective-permute-start(f32[160,256]{1,0:T(8,128)S(1)} %shard_map.87.refs_0_), channel_id=1, source_target_pairs={{0,28},{4,8},{8,4},{12,16},{16,12},{20,24},{24,20},{28,0},{1,29},{... | collective-permute-start | bytes 491528 | tf_op jit(solution)/shard_map/ppermute | solution.py:1030
  26.5 0.6 %shard_map.88 = f32[160,256]{1,0:T(8,128)S(1)} custom-call(f32[47,8,128]{2,1,0:T(8,128)S(1)} %shard_map.73.entries, f32[19,2,56,256]{3,2,1,0:T(8,128)S(1)} %shard_map.82.ends, f32[19,2,56,256]{3,2,1,0:T(8,128)S(1)} %get-tuple-element.55.middle, f32[4,1,40,256]{3,2,1,0:T(8,128)S(1)} %get-tuple-element.51.solid_near.solid, ...), custom_call_target="tpu_custom_call" | custom-call | tf_op jit(solution)/shard_map/pallas_call | solution.py:1144
  27.1 1.4 %shard_map.85.ends = f32[19,2,56,256]{3,2,1,0:T(8,128)S(1)} custom-call(f32[47,8,128]{2,1,0:T(8,128)S(1)} %shard_map.73.entries, f32[19,2,56,256]{3,2,1,0:T(8,128)S(1)} %shard_map.82.ends, f32[19,2,56,256]{3,2,1,0:T(8,128)S(1)} %get-tuple-element.55.middle, f32[4,1,40,256]{3,2,1,0:T(8,128)S(1)} %get-tuple-element.50.refs_0_.solid_far.solid, ...), custom_call_target="tpu_custom_call" | custom-call | tf_op jit(solution)/shard_map/pallas_call | solution.py:1156
  28.6 1.5 %shard_map.90.given = f32[19,4,32,256]{3,2,1,0:T(8,128)} custom-call(f32[19,2,56,256]{3,2,1,0:T(8,128)S(1)} %shard_map.85.ends, f32[19,2,56,256]{3,2,1,0:T(8,128)S(1)} %shard_map.86.refs_0_.middle), custom_call_target="tpu_custom_call" | custom-call | tf_op jit(solution)/shard_map/pallas_call | solution.py:1159
  30.1 2.1 %collective-permute-done.8.received = f32[160,256]{1,0:T(8,128)S(1)} collective-permute-done((f32[160,256]{1,0:T(8,128)S(1)}, f32[160,256]{1,0:T(8,128)S(1)}, u32[]{:S(2)}, u32[]{:S(2)}) %collective-permute-start.8) | collective-permute-done | bytes 163872 | tf_op jit(solution)/shard_map/ppermute | solution.py:1030
  32.2 0.8 %shard_map.91 = f32[19,4,32,256]{3,2,1,0:T(8,128)} custom-call(f32[19,2,56,256]{3,2,1,0:T(8,128)S(1)} %shard_map.85.ends, f32[160,256]{1,0:T(8,128)S(1)} %collective-permute-done.7.received, f32[5,32,256]{2,1,0:T(8,128)S(1)} %shard_map.89.far, f32[19,4,32,256]{3,2,1,0:T(8,128)} %shard_map.90.given), custom_call_target="tpu_custom_call", output_to_operand_aliasing={{}: (3, {})} | custom-call | tf_op jit(solution)/shard_map/pallas_call | solution.py:1169
  (17 shorter events, 0.3 us)
Async XLA Ops:
  0.0 5.2 %copy-start.1 = (f32[19]{0:T(128)S(1)}, f32[19]{0:T(128)}, u32[]{:S(2)}) copy-start(f32[19]{0:T(128)} %rates.1) | copy-start | bytes 232
  0.0 13.9 %copy-start = (f32[19,4,32,256]{3,2,1,0:T(8,128)S(1)}, f32[19,4,32,256]{3,2,1,0:T(8,128)}, u32[]{:S(2)}) copy-start(f32[19,4,32,256]{3,2,1,0:T(8,128)} %populations.5) | copy-start | bytes 7471108
  1.8 4.9 %collective-permute-start = (f32[8,128]{1,0:T(8,128)S(1)}, f32[8,128]{1,0:T(8,128)S(1)}, u32[]{:S(2)}, u32[]{:S(2)}) collective-permute-start(f32[8,128]{1,0:T(8,128)S(1)} %get-tuple-element.33), channel_id=1, source_target_pairs={{0,28},{4,8},{8,4},{12,16},{16,12},{20,24},{24,20},{28,0},{1,29},{... | collective-permute-start | bytes 12296 | tf_op jit(solution)/shard_map/ppermute | solution.py:1030
  5.2 1.6 %collective-permute-start.1 = (f32[8,128]{1,0:T(8,128)S(1)}, f32[8,128]{1,0:T(8,128)S(1)}, u32[]{:S(2)}, u32[]{:S(2)}) collective-permute-start(f32[8,128]{1,0:T(8,128)S(1)} %get-tuple-element.34), channel_id=1, source_target_pairs={{0,4},{4,0},{8,12},{12,8},{16,20},{20,16},{24,28},{28,24},{1,5},{5... | collective-permute-start | bytes 12296 | tf_op jit(solution)/shard_map/ppermute | solution.py:1030
  6.8 10.1 %collective-permute-start.3 = (f32[160,256]{1,0:T(8,128)S(1)}, f32[160,256]{1,0:T(8,128)S(1)}, u32[]{:S(2)}, u32[]{:S(2)}) collective-permute-start(f32[160,256]{1,0:T(8,128)S(1)} %get-tuple-element.41), channel_id=1, source_target_pairs={{0,0},{1,2},{2,1},{3,3},{4,4},{5,6},{6,5},{7,7},{8,8},{9,10},{10,9... | collective-permute-start | bytes 491528 | tf_op jit(solution)/shard_map/ppermute | solution.py:1030
  7.4 9.4 %collective-permute-start.4 = (f32[160,256]{1,0:T(8,128)S(1)}, f32[160,256]{1,0:T(8,128)S(1)}, u32[]{:S(2)}, u32[]{:S(2)}) collective-permute-start(f32[160,256]{1,0:T(8,128)S(1)} %get-tuple-element.42), channel_id=1, source_target_pairs={{0,1},{1,0},{2,3},{3,2},{4,5},{5,4},{6,7},{7,6},{8,9},{9,8},{10,11... | collective-permute-start | bytes 491528 | tf_op jit(solution)/shard_map/ppermute | solution.py:1030
  12.4 4.5 %collective-permute-start.2 = (f32[8,128]{1,0:T(8,128)S(1)}, f32[8,128]{1,0:T(8,128)S(1)}, u32[]{:S(2)}, u32[]{:S(2)}) collective-permute-start(f32[8,128]{1,0:T(8,128)S(1)} %get-tuple-element.40.refs_0_), channel_id=1, source_target_pairs={{0,2},{1,3},{2,0},{3,1},{4,6},{5,7},{6,4},{7,5},{8,10},{9,11},{10,... | collective-permute-start | bytes 12296 | tf_op jit(solution)/shard_map/ppermute | solution.py:1018
  17.6 7.4 %collective-permute-start.5 = (f32[176,256]{1,0:T(8,128)S(1)}, f32[176,256]{1,0:T(8,128)S(1)}, u32[]{:S(2)}, u32[]{:S(2)}) collective-permute-start(f32[176,256]{1,0:T(8,128)S(1)} %get-tuple-element.56), channel_id=1, source_target_pairs={{0,28},{4,8},{8,4},{12,16},{16,12},{20,24},{24,20},{28,0},{1,29},{... | collective-permute-start | bytes 540680 | tf_op jit(solution)/shard_map/ppermute | solution.py:1030
  19.6 6.9 %collective-permute-start.6 = (f32[176,256]{1,0:T(8,128)S(1)}, f32[176,256]{1,0:T(8,128)S(1)}, u32[]{:S(2)}, u32[]{:S(2)}) collective-permute-start(f32[176,256]{1,0:T(8,128)S(1)} %get-tuple-element.57), channel_id=1, source_target_pairs={{0,4},{4,0},{8,12},{12,8},{16,20},{20,16},{24,28},{28,24},{1,5},{5... | collective-permute-start | bytes 540680 | tf_op jit(solution)/shard_map/ppermute | solution.py:1030
  25.6 6.6 %collective-permute-start.8 = (f32[160,256]{1,0:T(8,128)S(1)}, f32[160,256]{1,0:T(8,128)S(1)}, u32[]{:S(2)}, u32[]{:S(2)}) collective-permute-start(f32[160,256]{1,0:T(8,128)S(1)} %shard_map.87.refs_0_), channel_id=1, source_target_pairs={{0,28},{4,8},{8,4},{12,16},{16,12},{20,24},{24,20},{28,0},{1,29},{... | collective-permute-start | bytes 491528 | tf_op jit(solution)/shard_map/ppermute | solution.py:1030
  27.1 5.1 %collective-permute-start.7 = (f32[160,256]{1,0:T(8,128)S(1)}, f32[160,256]{1,0:T(8,128)S(1)}, u32[]{:S(2)}, u32[]{:S(2)}) collective-permute-start(f32[160,256]{1,0:T(8,128)S(1)} %shard_map.88), channel_id=1, source_target_pairs={{0,4},{4,0},{8,12},{12,8},{16,20},{20,16},{24,28},{28,24},{1,5},{5... | collective-permute-start | bytes 491528 | tf_op jit(solution)/shard_map/ppermute | solution.py:1030

commit v7 on v6

--- a/solution.py
+++ b/solution.py
@@ -502,14 +502,13 @@
     )
 
 
-def merge_kernel(first, fold, own, far, near, one_in, two_in, column, one, two):
-    del one_in, two_in
+def merge_kernel(first, fold, own, far, near, one_in, column, one):
+    del one_in
     merged = own[...] + near[...] + far[...]
     column[...] = merged
     deep = 8 // fold
     for k in range(fold):
-        for target in (one, two):
-            target[first : first + deep, 128 * k : 128 * k + 128] = merged[deep * k : deep * k + deep]
+        one[first : first + deep, 128 * k : 128 * k + 128] = merged[deep * k : deep * k + deep]
 
 
 def relax_kernel(rates, entries):
@@ -530,7 +529,8 @@
                 density[p, rows, lanes] = d
 
 
-def stay_kernel(size_x, size_y, size_z, table, sums):
+def stay_kernel(size_x, size_y, size_z, table, after, sums):
+    del after
     a_x, a_y, a_z = cells_of(table[30:31, :].astype(I32), size_y, size_z)
     index = iota((size_x * size_y, 1), 0)
     rows_x = lax.div(index, jnp.int32(size_y))
@@ -553,9 +553,9 @@
 
 def outer_kernel(size_x, size_y, size_z, count, shifts, planes, *refs):
     if planes[0] == 0:
-        column, *rest = refs[: 1 + len(shifts)]
-        two, one, sums, outer, second, migrants = refs[1 + len(shifts) :]
-        arrivals(size_x, size_y, size_z, count, shifts, column, one, two, rest, migrants)
+        column, one, column_two, *rest = refs[: 3 + len(shifts)]
+        two, sums, outer, second, migrants = refs[3 + len(shifts) :]
+        arrivals(size_x, size_y, size_z, count, shifts, column, one, column_two, rest, migrants)
     else:
         two, one, sums, outer, second = refs
     blank = jnp.zeros((8, size_z), F32)
@@ -607,7 +607,7 @@
             [message[first : first + deep, 128 * k : 128 * k + 128] for k in range(fold)], axis=0
         )
 
-    parts = [column[...], gathered(one), gathered(two)] + [r[...] for r in rest]
+    parts = [column[...], gathered(one), two[...]] + [r[...] for r in rest]
     sources = [here, pair_source(here, 0, count), pair_source(here, 1, count)]
     sources += [lax.rem(here - shift + 2 * count, count) for shift in shifts]
     lane = iota((1, 128), 1)
@@ -1018,21 +1018,28 @@
     return lax.ppermute(value, axis, [(i, (i + steps) % count) for i in range(count)])
 
 
-def paired(value, axis, parity, wrap=False):
-    count = lax.axis_size(axis)
-    if wrap and count % 2:
+def paired_x(value, parity):
+    count = lax.axis_size("gx")
+    if count % 2:
         raise ValueError("odd ring")
+    pairs = [(i, (i + 1 if i % 2 == parity else i - 1) % count) for i in range(count)]
+    return lax.ppermute(value, "gx", pairs)
+
+
+def paired_y(value, parity):
+    count_x, count = lax.axis_size("gx"), lax.axis_size("gy")
     pairs = []
-    for i in range(count):
-        other = i + 1 if i % 2 == parity else i - 1
-        other = other % count if wrap else other
-        pairs.append((i, other if 0 <= other < count else i))
-    return lax.ppermute(value, axis, pairs)
+    for i in range(count_x):
+        for j in range(count):
+            other = j + 1 if j % 2 == parity else j - 1
+            to = i * count + other if 0 <= other < count else (i ^ 1) * count + j
+            pairs.append((i * count + j, to))
+    return lax.ppermute(value, ("gx", "gy"), pairs)
 
 
 def exchanged(near, far):
-    far = paired(far, "gx", 1, True)
-    return paired(near, "gx", 0, True), far
+    far = paired_x(far, 1)
+    return paired_x(near, 0), far
 
 
 def local(populations, relax_rates, velocity, velocity_change, fractions, anchor, destination):
@@ -1069,20 +1076,22 @@
         [VMEM] * 4,
         scratch=[pltpu.VMEM((19, 2 * size_x, size_z), F32)],
     )(bottom, top, table, entries)
-    column, one, two = call(
+    two = paired_y(two, 1)
+    column, one = call(
         part(merge_kernel, first, fold),
-        (shape(8, 128), message, message),
+        (shape(8, 128), message),
         8,
-        [VMEM] * 5,
-        aliases={3: 1, 4: 2},
-    )(own, far, near, one, two)
+        [VMEM] * 4,
+        aliases={3: 1},
+    )(own, far, near, one)
     shifts = []
     for shift in (2, -2):
         if shift % count > 1 and all((shift - other) % count for other in shifts):
             shifts.append(shift)
     rest = [around(column, "gy", shift) for shift in shifts]
-    one, two = paired(one, "gy", 0), paired(two, "gy", 1)
-    sums = call(part(stay_kernel, *sizes), shape(4, *sizes), 16, [VMEM])(table)
+    one, column_two = paired_y(one, 0), paired_y(column, 1)
+    unused = pl.BlockSpec(memory_space=pl.ANY)
+    sums = call(part(stay_kernel, *sizes), shape(4, *sizes), 16, [VMEM, unused])(table, two)
     plane_pair = shape(19, 2, size_y, size_z)
     parts = call(
         part(fluid_kernel, *sizes), (plane_pair, plane_pair, shape(2, size_y, size_z)), 16, [VMEM] * 2
@@ -1097,8 +1106,8 @@
         part(outer_kernel, *sizes, count, shifts, outside),
         outer_shapes(outside) + (shape(40, width),),
         8,
-        [VMEM] * (3 + len(shifts)),
-    )(column, *rest, two, one)
+        [VMEM] * (4 + len(shifts)),
+    )(column, one, column_two, *rest, two)
 
     def padded(planes):
         return shape(19, planes, size_y + 24, size_z)
@@ -1106,7 +1115,6 @@
     def solid_shape(planes):
         return shape(4, planes, size_y + 8, size_z)
 
-    unused = pl.BlockSpec(memory_space=pl.ANY)
     sent = pltpu.VMEM((5, 1, size_y + 24, size_z), F32)
     wide_face = shape((5 * size_y + 10 + 7) // 8 * 8, size_z)
     face = shape(5 * size_y, size_z)

time: 33.3 us -> 31.8 us (0.955)
  starting transfers between devices: 11.5 us -> 10.3 us
    ppermute x8 -> x9, starting transfers between devices: 11.5 us -> 8.81 us  [the longest x6 5.52 us: paired_x(): return lax.ppermute(value, 'gx', pairs)]
    ppermute x1, starting transfers between devices: 0.01 us -> 1.53 us  [around(): lax.ppermute(value, axis, [(i, (i + steps) % count) for i in range(count)])]
    ppermute x1, waiting for transfers between devices: 1.85 us -> 0.45 us  [around(): lax.ppermute(value, axis, [(i, (i + steps) % count) for i in range(count)])]
    ppermute x8 -> x9, waiting for transfers between devices: 3.73 us -> 4.84 us  [the longest x6 4.8 us: paired_x(): return lax.ppermute(value, 'gx', pairs)]
  transfers between devices with their start and end apart: 9 -> 10, of which waited for: 3 -> 3; matrix products, arithmetic and copies ran while one was open for 0% -> 0% of each run, Pallas kernels for 37% -> 39%
where the time goes in v7:
time: 31.8 us; the launch traced here: 31.7 us
  Pallas kernels  15.8 us (50%)
  starting transfers between devices  10.3 us (32%)
  waiting for transfers between devices  5.28 us (17%)
    ppermute x6, starting transfers between devices, paired_x(): return lax.ppermute(value, 'gx', pairs)  5.52 us
    ppermute x6, waiting for transfers between devices, paired_x(): return lax.ppermute(value, 'gx', pairs)  4.8 us
    ppermute x3, starting transfers between devices, paired_y(): return lax.ppermute(value, ('gx', 'gy'), pairs)  3.29 us
    pallas_call x1, Pallas kernels, local(): call(pack_kernel, (shape(32, rows), packed, packed, packed, band, band),...  1.77 us
    ppermute x1, starting transfers between devices, around(): lax.ppermute(value, axis, [(i, (i + steps) % count) for i in range(count)])  1.53 us
    pallas_call x1, Pallas kernels, local(): call(part(last_kernel, *sizes, count), shape(19, *sizes), 16, [VMEM] * 2,...  1.5 us
    pallas_call x1, Pallas kernels, local(): call(part(stay_kernel, *sizes), shape(4, *sizes), 16, [VMEM, unused])  1.5 us
    pallas_call x1, Pallas kernels, local(): call(part(second_kernel, *sizes, count), padded(len(inside)), 16, [VMEM]...  1.49 us
  transfers between devices with their start and end apart: 10, of which 3 were waited for; matrix products, arithmetic and copies ran while one was open for 0% of the time, Pallas kernels for 39%

profile of v7, /device:TPU:0, one launch (start us, length us, event | category | flops | bytes accessed | tf_op | source)
XLA Modules:
  0.0 31.7 jit_solution(14439666052981140586)
XLA Ops:
  0.0 1.8 %shard_map.74 = (f32[32,512]{1,0:T(8,128)S(1)}, f32[8,128]{1,0:T(8,128)S(1)}, f32[8,128]{1,0:T(8,128)S(1)}, f32[8,128]{1,0:T(8,128)S(1)}, f32[19,4,8,256]{3,2,1,0:T(8,128)S(1)}, /*index=5*/f32[19,4,8,256]{3,2,1,0:T(8,128)S(1)}) custom-call(f32[3,512]{1,0:T(4,128)} %velocity_in.1, f32[3,512]{1,0:T(4,128)} %change_in.1, f32[27,512]{1,0:T(8,128)} %fractions_in.1, ...), custom_call_target="tpu_custom_call" | custom-call | tf_op jit(solution)/shard_map/pallas_call | solution.py:1053
  1.8 3.4 %collective-permute-start = (f32[8,128]{1,0:T(8,128)S(1)}, f32[8,128]{1,0:T(8,128)S(1)}, u32[]{:S(2)}, u32[]{:S(2)}) collective-permute-start(f32[8,128]{1,0:T(8,128)S(1)} %get-tuple-element.32), channel_id=1, source_target_pairs={{0,28},{4,8},{8,4},{12,16},{16,12},{20,24},{24,20},{28,0},{1,29},{... | collective-permute-start | bytes 12296 | tf_op jit(solution)/shard_map/ppermute | solution.py:1026
  5.2 0.6 %shard_map.73.entries = f32[47,8,128]{2,1,0:T(8,128)S(1)} custom-call(f32[19]{0:T(128)S(1)} %copy-done.1), custom_call_target="tpu_custom_call" | custom-call | tf_op jit(solution)/shard_map/pallas_call | solution.py:1071
  5.8 0.9 %shard_map.75 = (f32[160,256]{1,0:T(8,128)S(1)}, f32[160,256]{1,0:T(8,128)S(1)}) custom-call(f32[19,4,8,256]{3,2,1,0:T(8,128)S(1)} %get-tuple-element.34.bottom, f32[19,4,8,256]{3,2,1,0:T(8,128)S(1)} %get-tuple-element.35.top, f32[32,512]{1,0:T(8,128)S(1)} %get-tuple-element.36.table, f32[47,8,128]{2,1,0:T(8,128)S(1)} %shard_map.73.entries), custom_call_target="tpu_custom_call" | custom-call | tf_op jit(solution)/shard_map/pallas_call | solution.py:1072
  6.7 0.6 %collective-permute-start.5 = (f32[160,256]{1,0:T(8,128)S(1)}, f32[160,256]{1,0:T(8,128)S(1)}, u32[]{:S(2)}, u32[]{:S(2)}) collective-permute-start(f32[160,256]{1,0:T(8,128)S(1)} %get-tuple-element.40), channel_id=1, source_target_pairs={{0,4},{1,2},{2,1},{3,7},{4,0},{5,6},{6,5},{7,3},{8,12},{9,10},{10,... | collective-permute-start | bytes 491528 | tf_op jit(solution)/shard_map/ppermute | solution.py:1037
  7.3 2.7 %collective-permute-start.2 = (f32[160,256]{1,0:T(8,128)S(1)}, f32[160,256]{1,0:T(8,128)S(1)}, u32[]{:S(2)}, u32[]{:S(2)}) collective-permute-start(f32[160,256]{1,0:T(8,128)S(1)} %get-tuple-element.39), channel_id=1, source_target_pairs={{0,1},{1,0},{2,3},{3,2},{4,5},{5,4},{6,7},{7,6},{8,9},{9,8},{10,11... | collective-permute-start | bytes 491528 | tf_op jit(solution)/shard_map/ppermute | solution.py:1037
  10.0 1.5 %collective-permute-start.4 = (f32[8,128]{1,0:T(8,128)S(1)}, f32[8,128]{1,0:T(8,128)S(1)}, u32[]{:S(2)}, u32[]{:S(2)}) collective-permute-start(f32[8,128]{1,0:T(8,128)S(1)} %get-tuple-element.38.refs_0_), channel_id=1, source_target_pairs={{0,2},{1,3},{2,0},{3,1},{4,6},{5,7},{6,4},{7,5},{8,10},{9,11},{10,... | collective-permute-start | bytes 12296 | tf_op jit(solution)/shard_map/ppermute | solution.py:1018
  11.6 1.1 %shard_map.78 = (f32[19,2,32,256]{3,2,1,0:T(8,128)S(1)}, f32[19,2,32,256]{3,2,1,0:T(8,128)S(1)}, f32[2,32,256]{2,1,0:T(8,128)S(1)}) custom-call(f32[47,8,128]{2,1,0:T(8,128)S(1)} %shard_map.73.entries, f32[19,4,32,256]{3,2,1,0:T(8,128)S(1)} %copy-done), custom_call_target="tpu_custom_call" | custom-call | tf_op jit(solution)/shard_map/pallas_call | solution.py:1096
  12.7 1.5 %shard_map.79.sums = f32[4,4,32,256]{3,2,1,0:T(8,128)S(1)} custom-call(f32[32,512]{1,0:T(8,128)S(1)} %get-tuple-element.36.table, f32[160,256]{1,0:T(8,128)S(1)} %collective-permute-done.5.refs_4_.after.refs_0_), custom_call_target="tpu_custom_call" | custom-call | tf_op jit(solution)/shard_map/pallas_call | solution.py:1094
  14.2 0.4 %collective-permute-done.4.refs_3_ = f32[8,128]{1,0:T(8,128)S(1)} collective-permute-done((f32[8,128]{1,0:T(8,128)S(1)}, f32[8,128]{1,0:T(8,128)S(1)}, u32[]{:S(2)}, u32[]{:S(2)}) %collective-permute-start.4) | collective-permute-done | bytes 4128 | tf_op jit(solution)/shard_map/ppermute | solution.py:1018
  14.9 0.6 %shard_map.80 = (f32[4,1,40,256]{3,2,1,0:T(8,128)S(1)}, f32[176,256]{1,0:T(8,128)S(1)}) custom-call(f32[47,8,128]{2,1,0:T(8,128)S(1)} %shard_map.73.entries, f32[4,4,32,256]{3,2,1,0:T(8,128)S(1)} %shard_map.79.sums, f32[4,2,8,256]{3,2,1,0:T(8,128)S(1)} %get-tuple-element.46.outer_sums, f32[19,2,8,256]{3,2,1,0:T(8,128)S(1)} %get-tuple-element.41.outer, ...), custom_call_target="tpu_custom_call" | custom-call | tf_op jit(solution)/shard_map/pallas_call | solution.py:1123
  15.4 1.2 %collective-permute-start.6 = (f32[176,256]{1,0:T(8,128)S(1)}, f32[176,256]{1,0:T(8,128)S(1)}, u32[]{:S(2)}, u32[]{:S(2)}) collective-permute-start(f32[176,256]{1,0:T(8,128)S(1)} %get-tuple-element.54), channel_id=1, source_target_pairs={{0,28},{4,8},{8,4},{12,16},{16,12},{20,24},{24,20},{28,0},{1,29},{... | collective-permute-start | bytes 540680 | tf_op jit(solution)/shard_map/ppermute | solution.py:1026
  16.6 0.5 %shard_map.81 = (f32[4,1,40,256]{3,2,1,0:T(8,128)S(1)}, f32[176,256]{1,0:T(8,128)S(1)}) custom-call(f32[47,8,128]{2,1,0:T(8,128)S(1)} %shard_map.73.entries, f32[4,4,32,256]{3,2,1,0:T(8,128)S(1)} %shard_map.79.sums, f32[4,2,8,256]{3,2,1,0:T(8,128)S(1)} %get-tuple-element.46.outer_sums, f32[19,2,8,256]{3,2,1,0:T(8,128)S(1)} %get-tuple-element.41.outer, ...), custom_call_target="tpu_custom_call" | custom-call | tf_op jit(solution)/shard_map/pallas_call | solution.py:1123
  17.3 0.6 %shard_map.82.ends = f32[19,2,56,256]{3,2,1,0:T(8,128)S(1)} custom-call(f32[47,8,128]{2,1,0:T(8,128)S(1)} %shard_map.73.entries, f32[19,2,8,256]{3,2,1,0:T(8,128)S(1)} %get-tuple-element.41.outer, f32[11,2,8,256]{3,2,1,0:T(8,128)S(1)} %get-tuple-element.42.second, f32[19,2,32,256]{3,2,1,0:T(8,128)S(1)} %get-tuple-element.43.relaxed, ...), custom_call_target="tpu_custom_call" | custom-call | tf_op jit(solution)/shard_map/pallas_call | solution.py:1144
  18.1 1.5 %shard_map.84 = (f32[19,2,56,256]{3,2,1,0:T(8,128)S(1)}, f32[4,2,40,256]{3,2,1,0:T(8,128)S(1)}) custom-call(f32[47,8,128]{2,1,0:T(8,128)S(1)} %shard_map.73.entries, f32[4,4,32,256]{3,2,1,0:T(8,128)S(1)} %shard_map.79.sums, f32[4,2,8,256]{3,2,1,0:T(8,128)S(1)} %get-tuple-element.50.outer_sums, f32[19,2,8,256]{3,2,1,0:T(8,128)S(1)} %get-tuple-element.51.outer, ...), custom_call_target="tpu_custom_call" | custom-call | tf_op jit(solution)/shard_map/pallas_call | solution.py:1138
  19.5 1.5 %shard_map.86.refs_0_.middle = f32[19,2,56,256]{3,2,1,0:T(8,128)S(1)} custom-call(f32[47,8,128]{2,1,0:T(8,128)S(1)} %shard_map.73.entries, f32[19,2,56,256]{3,2,1,0:T(8,128)S(1)} %shard_map.82.ends, f32[19,2,56,256]{3,2,1,0:T(8,128)S(1)} %get-tuple-element.53.middle, f32[4,2,40,256]{3,2,1,0:T(8,128)S(1)} %get-tuple-element.56.solid), custom_call_target="tpu_custom_call" | custom-call | tf_op jit(solution)/shard_map/pallas_call | solution.py:1147
  21.0 2.1 %collective-permute-done.6.far.received = f32[176,256]{1,0:T(8,128)S(1)} collective-permute-done((f32[176,256]{1,0:T(8,128)S(1)}, f32[176,256]{1,0:T(8,128)S(1)}, u32[]{:S(2)}, u32[]{:S(2)}) %collective-permute-start.6) | collective-permute-done | bytes 180256 | tf_op jit(solution)/shard_map/ppermute | solution.py:1026
  23.1 0.5 %shard_map.87.refs_0_ = f32[160,256]{1,0:T(8,128)S(1)} custom-call(f32[47,8,128]{2,1,0:T(8,128)S(1)} %shard_map.73.entries, f32[19,2,56,256]{3,2,1,0:T(8,128)S(1)} %shard_map.82.ends, f32[19,2,56,256]{3,2,1,0:T(8,128)S(1)} %get-tuple-element.53.middle, f32[4,1,40,256]{3,2,1,0:T(8,128)S(1)} %get-tuple-element.48.refs_0_.solid_far.solid, ...), custom_call_target="tpu_custom_call" | custom-call | tf_op jit(solution)/shard_map/pallas_call | solution.py:1152
  23.6 0.8 %collective-permute-start.9 = (f32[160,256]{1,0:T(8,128)S(1)}, f32[160,256]{1,0:T(8,128)S(1)}, u32[]{:S(2)}, u32[]{:S(2)}) collective-permute-start(f32[160,256]{1,0:T(8,128)S(1)} %shard_map.87.refs_0_), channel_id=1, source_target_pairs={{0,28},{4,8},{8,4},{12,16},{16,12},{20,24},{24,20},{28,0},{1,29},{... | collective-permute-start | bytes 491528 | tf_op jit(solution)/shard_map/ppermute | solution.py:1026
  24.4 0.6 %shard_map.88 = f32[160,256]{1,0:T(8,128)S(1)} custom-call(f32[47,8,128]{2,1,0:T(8,128)S(1)} %shard_map.73.entries, f32[19,2,56,256]{3,2,1,0:T(8,128)S(1)} %shard_map.82.ends, f32[19,2,56,256]{3,2,1,0:T(8,128)S(1)} %get-tuple-element.53.middle, f32[4,1,40,256]{3,2,1,0:T(8,128)S(1)} %get-tuple-element.49.solid_near.solid, ...), custom_call_target="tpu_custom_call" | custom-call | tf_op jit(solution)/shard_map/pallas_call | solution.py:1152
  25.0 1.4 %shard_map.85.ends = f32[19,2,56,256]{3,2,1,0:T(8,128)S(1)} custom-call(f32[47,8,128]{2,1,0:T(8,128)S(1)} %shard_map.73.entries, f32[19,2,56,256]{3,2,1,0:T(8,128)S(1)} %shard_map.82.ends, f32[19,2,56,256]{3,2,1,0:T(8,128)S(1)} %get-tuple-element.53.middle, f32[4,1,40,256]{3,2,1,0:T(8,128)S(1)} %get-tuple-element.48.refs_0_.solid_far.solid, ...), custom_call_target="tpu_custom_call" | custom-call | tf_op jit(solution)/shard_map/pallas_call | solution.py:1164
  26.5 1.5 %shard_map.90.given = f32[19,4,32,256]{3,2,1,0:T(8,128)} custom-call(f32[19,2,56,256]{3,2,1,0:T(8,128)S(1)} %shard_map.85.ends, f32[19,2,56,256]{3,2,1,0:T(8,128)S(1)} %shard_map.86.refs_0_.middle), custom_call_target="tpu_custom_call" | custom-call | tf_op jit(solution)/shard_map/pallas_call | solution.py:1167
  28.0 2.7 %collective-permute-done.9.received = f32[160,256]{1,0:T(8,128)S(1)} collective-permute-done((f32[160,256]{1,0:T(8,128)S(1)}, f32[160,256]{1,0:T(8,128)S(1)}, u32[]{:S(2)}, u32[]{:S(2)}) %collective-permute-start.9) | collective-permute-done | bytes 163872 | tf_op jit(solution)/shard_map/ppermute | solution.py:1026
  30.7 0.8 %shard_map.91 = f32[19,4,32,256]{3,2,1,0:T(8,128)} custom-call(f32[19,2,56,256]{3,2,1,0:T(8,128)S(1)} %shard_map.85.ends, f32[160,256]{1,0:T(8,128)S(1)} %collective-permute-done.8.received, f32[5,32,256]{2,1,0:T(8,128)S(1)} %shard_map.89.far, f32[19,4,32,256]{3,2,1,0:T(8,128)} %shard_map.90.given), custom_call_target="tpu_custom_call", output_to_operand_aliasing={{}: (3, {})} | custom-call | tf_op jit(solution)/shard_map/pallas_call | solution.py:1177
  (19 shorter events, 0.6 us)
Async XLA Ops:
  0.0 5.2 %copy-start.1 = (f32[19]{0:T(128)S(1)}, f32[19]{0:T(128)}, u32[]{:S(2)}) copy-start(f32[19]{0:T(128)} %rates.1) | copy-start | bytes 232
  0.0 11.6 %copy-start = (f32[19,4,32,256]{3,2,1,0:T(8,128)S(1)}, f32[19,4,32,256]{3,2,1,0:T(8,128)}, u32[]{:S(2)}) copy-start(f32[19,4,32,256]{3,2,1,0:T(8,128)} %populations.5) | copy-start | bytes 7471108
  1.8 5.5 %collective-permute-start = (f32[8,128]{1,0:T(8,128)S(1)}, f32[8,128]{1,0:T(8,128)S(1)}, u32[]{:S(2)}, u32[]{:S(2)}) collective-permute-start(f32[8,128]{1,0:T(8,128)S(1)} %get-tuple-element.32), channel_id=1, source_target_pairs={{0,28},{4,8},{8,4},{12,16},{16,12},{20,24},{24,20},{28,0},{1,29},{... | collective-permute-start | bytes 12296 | tf_op jit(solution)/shard_map/ppermute | solution.py:1026
  5.2 2.1 %collective-permute-start.1 = (f32[8,128]{1,0:T(8,128)S(1)}, f32[8,128]{1,0:T(8,128)S(1)}, u32[]{:S(2)}, u32[]{:S(2)}) collective-permute-start(f32[8,128]{1,0:T(8,128)S(1)} %get-tuple-element.33), channel_id=1, source_target_pairs={{0,4},{4,0},{8,12},{12,8},{16,20},{20,16},{24,28},{28,24},{1,5},{5... | collective-permute-start | bytes 12296 | tf_op jit(solution)/shard_map/ppermute | solution.py:1026
  6.7 6.0 %collective-permute-start.5 = (f32[160,256]{1,0:T(8,128)S(1)}, f32[160,256]{1,0:T(8,128)S(1)}, u32[]{:S(2)}, u32[]{:S(2)}) collective-permute-start(f32[160,256]{1,0:T(8,128)S(1)} %get-tuple-element.40), channel_id=1, source_target_pairs={{0,4},{1,2},{2,1},{3,7},{4,0},{5,6},{6,5},{7,3},{8,12},{9,10},{10,... | collective-permute-start | bytes 491528 | tf_op jit(solution)/shard_map/ppermute | solution.py:1037
  7.3 7.4 %collective-permute-start.2 = (f32[160,256]{1,0:T(8,128)S(1)}, f32[160,256]{1,0:T(8,128)S(1)}, u32[]{:S(2)}, u32[]{:S(2)}) collective-permute-start(f32[160,256]{1,0:T(8,128)S(1)} %get-tuple-element.39), channel_id=1, source_target_pairs={{0,1},{1,0},{2,3},{3,2},{4,5},{5,4},{6,7},{7,6},{8,9},{9,8},{10,11... | collective-permute-start | bytes 491528 | tf_op jit(solution)/shard_map/ppermute | solution.py:1037
  10.0 4.6 %collective-permute-start.4 = (f32[8,128]{1,0:T(8,128)S(1)}, f32[8,128]{1,0:T(8,128)S(1)}, u32[]{:S(2)}, u32[]{:S(2)}) collective-permute-start(f32[8,128]{1,0:T(8,128)S(1)} %get-tuple-element.38.refs_0_), channel_id=1, source_target_pairs={{0,2},{1,3},{2,0},{3,1},{4,6},{5,7},{6,4},{7,5},{8,10},{9,11},{10,... | collective-permute-start | bytes 12296 | tf_op jit(solution)/shard_map/ppermute | solution.py:1018
  11.6 3.1 %collective-permute-start.3 = (f32[8,128]{1,0:T(8,128)S(1)}, f32[8,128]{1,0:T(8,128)S(1)}, u32[]{:S(2)}, u32[]{:S(2)}) collective-permute-start(f32[8,128]{1,0:T(8,128)S(1)} %get-tuple-element.38.refs_0_), channel_id=1, source_target_pairs={{0,4},{1,2},{2,1},{3,7},{4,0},{5,6},{6,5},{7,3},{8,12},{9,10},{10,... | collective-permute-start | bytes 12296 | tf_op jit(solution)/shard_map/ppermute | solution.py:1037
  15.4 7.6 %collective-permute-start.6 = (f32[176,256]{1,0:T(8,128)S(1)}, f32[176,256]{1,0:T(8,128)S(1)}, u32[]{:S(2)}, u32[]{:S(2)}) collective-permute-start(f32[176,256]{1,0:T(8,128)S(1)} %get-tuple-element.54), channel_id=1, source_target_pairs={{0,28},{4,8},{8,4},{12,16},{16,12},{20,24},{24,20},{28,0},{1,29},{... | collective-permute-start | bytes 540680 | tf_op jit(solution)/shard_map/ppermute | solution.py:1026
  17.1 7.2 %collective-permute-start.7 = (f32[176,256]{1,0:T(8,128)S(1)}, f32[176,256]{1,0:T(8,128)S(1)}, u32[]{:S(2)}, u32[]{:S(2)}) collective-permute-start(f32[176,256]{1,0:T(8,128)S(1)} %get-tuple-element.55), channel_id=1, source_target_pairs={{0,4},{4,0},{8,12},{12,8},{16,20},{20,16},{24,28},{28,24},{1,5},{5... | collective-permute-start | bytes 540680 | tf_op jit(solution)/shard_map/ppermute | solution.py:1026
  23.6 7.1 %collective-permute-start.9 = (f32[160,256]{1,0:T(8,128)S(1)}, f32[160,256]{1,0:T(8,128)S(1)}, u32[]{:S(2)}, u32[]{:S(2)}) collective-permute-start(f32[160,256]{1,0:T(8,128)S(1)} %shard_map.87.refs_0_), channel_id=1, source_target_pairs={{0,28},{4,8},{8,4},{12,16},{16,12},{20,24},{24,20},{28,0},{1,29},{... | collective-permute-start | bytes 491528 | tf_op jit(solution)/shard_map/ppermute | solution.py:1026
  24.9 5.8 %collective-permute-start.8 = (f32[160,256]{1,0:T(8,128)S(1)}, f32[160,256]{1,0:T(8,128)S(1)}, u32[]{:S(2)}, u32[]{:S(2)}) collective-permute-start(f32[160,256]{1,0:T(8,128)S(1)} %shard_map.88), channel_id=1, source_target_pairs={{0,4},{4,0},{8,12},{12,8},{16,20},{20,16},{24,28},{28,24},{1,5},{5... | collective-permute-start | bytes 491528 | tf_op jit(solution)/shard_map/ppermute | solution.py:1026

commit v8 on v7

--- a/solution.py
+++ b/solution.py
@@ -529,13 +529,14 @@
                 density[p, rows, lanes] = d
 
 
-def stay_kernel(size_x, size_y, size_z, table, after, sums):
+def stay_kernel(size_x, size_y, size_z, planes, table, after, sums):
     del after
     a_x, a_y, a_z = cells_of(table[30:31, :].astype(I32), size_y, size_z)
-    index = iota((size_x * size_y, 1), 0)
-    rows_x = lax.div(index, jnp.int32(size_y))
+    index = iota((len(planes) * size_y, 1), 0)
+    number = lax.div(index, jnp.int32(size_y))
+    rows_x = number * (size_x - 1) if planes[0] == 0 else number + planes[0]
     totals = deposited(
-        [(rows_x, index - rows_x * size_y)],
+        [(rows_x, index - number * size_y)],
         table[0:27, :],
         table[27:30, :],
         a_x,
@@ -544,11 +545,11 @@
         size_z,
         8 * size_y,
     )
-    cells = size_x * size_y
+    cells = len(planes) * size_y
     for c in range(4):
-        for x in range(size_x):
-            at = c * cells + x * size_y
-            sums[c, x, :, :] = totals[at : at + size_y]
+        for p in range(len(planes)):
+            at = c * cells + p * size_y
+            sums[c, p, :, :] = totals[at : at + size_y]
 
 
 def outer_kernel(size_x, size_y, size_z, count, shifts, planes, *refs):
@@ -668,7 +669,7 @@
         parts = []
         for c in range(4):
             at = c * cells + p * wide
-            solid_sum = jnp.concatenate([sums[c, x, :, :], outer_sums[c, first + p, :, :]], axis=0)
+            solid_sum = jnp.concatenate([sums[c, first + p, :, :], outer_sums[c, first + p, :, :]], axis=0)
             parts.append(totals[at : at + wide] + solid_sum)
         scale = 1.0 / (parts[0] + 1e-06)
         solid[0, p, :, :] = jnp.minimum(parts[0], 1.0)
@@ -1091,14 +1092,22 @@
     rest = [around(column, "gy", shift) for shift in shifts]
     one, column_two = paired_y(one, 0), paired_y(column, 1)
     unused = pl.BlockSpec(memory_space=pl.ANY)
-    sums = call(part(stay_kernel, *sizes), shape(4, *sizes), 16, [VMEM, unused])(table, two)
+    outside, inside = (0, size_x - 1), tuple(range(1, size_x - 1))
+
+    def staying(planes, after):
+        return call(
+            part(stay_kernel, *sizes, planes),
+            shape(4, len(planes), size_y, size_z),
+            16,
+            [VMEM, unused],
+        )(table, after)
+
+    sums = staying(outside, two)
     plane_pair = shape(19, 2, size_y, size_z)
     parts = call(
         part(fluid_kernel, *sizes), (plane_pair, plane_pair, shape(2, size_y, size_z)), 16, [VMEM] * 2
     )(entries, populations)
     width = -(-(3 + len(shifts)) * LANES // 128) * 128
-    outside, inside = (0, size_x - 1), tuple(range(1, size_x - 1))
-
     def outer_shapes(planes):
         return tuple(shape(k, len(planes), 8, size_z) for k in (4, 19, 11))
 
@@ -1140,7 +1149,7 @@
         (padded(len(inside)), solid_shape(len(inside))),
         16,
         [VMEM] * 7,
-    )(entries, sums, *inner, migrants, populations)
+    )(entries, staying(inside, solid_near), *inner, migrants, populations)
     ends = call(part(ends_kernel, *sizes), padded(2), 16, [VMEM] * 8)(
         entries, outer, second, *parts, solid_far, solid_near
     )

time: 31.8 us -> 31.1 us (0.978)
  waiting for transfers between devices: 5.28 us -> 3.95 us
    ppermute x6, waiting for transfers between devices: 4.8 us -> 2.88 us  [paired_x(): return lax.ppermute(value, 'gx', pairs)]
    ppermute x1, waiting for transfers between devices: 0.45 us -> 1.03 us  [around(): lax.ppermute(value, axis, [(i, (i + steps) % count) for i in range(count)])]
    pallas_call x1 -> x2, Pallas kernels: 1.5 us -> 1.83 us  [staying(): call(part(stay_kernel, *sizes, planes), shape(4, len(planes), size_y, siz...]
  transfers between devices with their start and end apart: 10 -> 10, of which waited for: 3 -> 3; matrix products, arithmetic and copies ran while one was open for 0% -> 0% of each run, Pallas kernels for 39% -> 41%
where the time goes in v8:
time: 31.1 us; the launch traced here: 31 us
  Pallas kernels  16.1 us (52%)
  starting transfers between devices  10.6 us (34%)
  waiting for transfers between devices  3.95 us (13%)
  between operations  0.32 us (1%)
    ppermute x6, starting transfers between devices, paired_x(): return lax.ppermute(value, 'gx', pairs)  5.77 us
    ppermute x3, starting transfers between devices, paired_y(): return lax.ppermute(value, ('gx', 'gy'), pairs)  3.29 us
    ppermute x6, waiting for transfers between devices, paired_x(): return lax.ppermute(value, 'gx', pairs)  2.88 us
    pallas_call x2, Pallas kernels, staying(): call(part(stay_kernel, *sizes, planes), shape(4, len(planes), size_y, siz...  1.83 us
    pallas_call x1, Pallas kernels, local(): call(pack_kernel, (shape(32, rows), packed, packed, packed, band, band),...  1.77 us
    ppermute x1, starting transfers between devices, around(): lax.ppermute(value, axis, [(i, (i + steps) % count) for i in range(count)])  1.53 us
    pallas_call x1, Pallas kernels, local(): call(part(last_kernel, *sizes, count), shape(19, *sizes), 16, [VMEM] * 2,...  1.5 us
    pallas_call x1, Pallas kernels, local(): call(part(second_kernel, *sizes, count), padded(len(inside)), 16, [VMEM]...  1.49 us
  transfers between devices with their start and end apart: 10, of which 3 were waited for; matrix products, arithmetic and copies ran while one was open for 0% of the time, Pallas kernels for 41%

profile of v8, /device:TPU:0, one launch (start us, length us, event | category | flops | bytes accessed | tf_op | source)
XLA Modules:
  0.0 31.0 jit_solution(5572060327354380266)
XLA Ops:
  0.0 1.8 %shard_map.74 = (f32[32,512]{1,0:T(8,128)S(1)}, f32[8,128]{1,0:T(8,128)S(1)}, f32[8,128]{1,0:T(8,128)S(1)}, f32[8,128]{1,0:T(8,128)S(1)}, f32[19,4,8,256]{3,2,1,0:T(8,128)S(1)}, /*index=5*/f32[19,4,8,256]{3,2,1,0:T(8,128)S(1)}) custom-call(f32[3,512]{1,0:T(4,128)} %velocity_in.1, f32[3,512]{1,0:T(4,128)} %change_in.1, f32[27,512]{1,0:T(8,128)} %fractions_in.1, ...), custom_call_target="tpu_custom_call" | custom-call | tf_op jit(solution)/shard_map/pallas_call | solution.py:1054
  1.8 3.4 %collective-permute-start = (f32[8,128]{1,0:T(8,128)S(1)}, f32[8,128]{1,0:T(8,128)S(1)}, u32[]{:S(2)}, u32[]{:S(2)}) collective-permute-start(f32[8,128]{1,0:T(8,128)S(1)} %get-tuple-element.32), channel_id=1, source_target_pairs={{0,28},{4,8},{8,4},{12,16},{16,12},{20,24},{24,20},{28,0},{1,29},{... | collective-permute-start | bytes 12296 | tf_op jit(solution)/shard_map/ppermute | solution.py:1027
  5.2 0.6 %shard_map.73.entries = f32[47,8,128]{2,1,0:T(8,128)S(1)} custom-call(f32[19]{0:T(128)S(1)} %copy-done.1), custom_call_target="tpu_custom_call" | custom-call | tf_op jit(solution)/shard_map/pallas_call | solution.py:1072
  5.8 0.9 %shard_map.75 = (f32[160,256]{1,0:T(8,128)S(1)}, f32[160,256]{1,0:T(8,128)S(1)}) custom-call(f32[19,4,8,256]{3,2,1,0:T(8,128)S(1)} %get-tuple-element.34.bottom, f32[19,4,8,256]{3,2,1,0:T(8,128)S(1)} %get-tuple-element.35.top, f32[32,512]{1,0:T(8,128)S(1)} %get-tuple-element.36.table, f32[47,8,128]{2,1,0:T(8,128)S(1)} %shard_map.73.entries), custom_call_target="tpu_custom_call" | custom-call | tf_op jit(solution)/shard_map/pallas_call | solution.py:1073
  6.7 0.6 %collective-permute-start.5 = (f32[160,256]{1,0:T(8,128)S(1)}, f32[160,256]{1,0:T(8,128)S(1)}, u32[]{:S(2)}, u32[]{:S(2)}) collective-permute-start(f32[160,256]{1,0:T(8,128)S(1)} %get-tuple-element.40), channel_id=1, source_target_pairs={{0,4},{1,2},{2,1},{3,7},{4,0},{5,6},{6,5},{7,3},{8,12},{9,10},{10,... | collective-permute-start | bytes 491528 | tf_op jit(solution)/shard_map/ppermute | solution.py:1038
  7.3 2.7 %collective-permute-start.2 = (f32[160,256]{1,0:T(8,128)S(1)}, f32[160,256]{1,0:T(8,128)S(1)}, u32[]{:S(2)}, u32[]{:S(2)}) collective-permute-start(f32[160,256]{1,0:T(8,128)S(1)} %get-tuple-element.39), channel_id=1, source_target_pairs={{0,1},{1,0},{2,3},{3,2},{4,5},{5,4},{6,7},{7,6},{8,9},{9,8},{10,11... | collective-permute-start | bytes 491528 | tf_op jit(solution)/shard_map/ppermute | solution.py:1038
  10.0 1.5 %collective-permute-start.4 = (f32[8,128]{1,0:T(8,128)S(1)}, f32[8,128]{1,0:T(8,128)S(1)}, u32[]{:S(2)}, u32[]{:S(2)}) collective-permute-start(f32[8,128]{1,0:T(8,128)S(1)} %get-tuple-element.38.refs_0_), channel_id=1, source_target_pairs={{0,2},{1,3},{2,0},{3,1},{4,6},{5,7},{6,4},{7,5},{8,10},{9,11},{10,... | collective-permute-start | bytes 12296 | tf_op jit(solution)/shard_map/ppermute | solution.py:1019
  11.6 1.1 %shard_map.78 = (f32[19,2,32,256]{3,2,1,0:T(8,128)S(1)}, f32[19,2,32,256]{3,2,1,0:T(8,128)S(1)}, f32[2,32,256]{2,1,0:T(8,128)S(1)}) custom-call(f32[47,8,128]{2,1,0:T(8,128)S(1)} %shard_map.73.entries, f32[19,4,32,256]{3,2,1,0:T(8,128)S(1)} %copy-done), custom_call_target="tpu_custom_call" | custom-call | tf_op jit(solution)/shard_map/pallas_call | solution.py:1107
  12.7 0.9 %shard_map.79.sums = f32[4,2,32,256]{3,2,1,0:T(8,128)S(1)} custom-call(f32[32,512]{1,0:T(8,128)S(1)} %get-tuple-element.36.table, f32[160,256]{1,0:T(8,128)S(1)} %collective-permute-done.5.refs_4_.after.refs_0_), custom_call_target="tpu_custom_call" | custom-call | tf_op jit(solution)/shard_map/pallas_call | solution.py:1098
  13.6 1.0 %collective-permute-done.4.refs_3_ = f32[8,128]{1,0:T(8,128)S(1)} collective-permute-done((f32[8,128]{1,0:T(8,128)S(1)}, f32[8,128]{1,0:T(8,128)S(1)}, u32[]{:S(2)}, u32[]{:S(2)}) %collective-permute-start.4) | collective-permute-done | bytes 4128 | tf_op jit(solution)/shard_map/ppermute | solution.py:1019
  14.9 0.6 %shard_map.80 = (f32[4,1,40,256]{3,2,1,0:T(8,128)S(1)}, f32[176,256]{1,0:T(8,128)S(1)}) custom-call(f32[47,8,128]{2,1,0:T(8,128)S(1)} %shard_map.73.entries, f32[4,2,32,256]{3,2,1,0:T(8,128)S(1)} %shard_map.79.sums, f32[4,2,8,256]{3,2,1,0:T(8,128)S(1)} %get-tuple-element.46.outer_sums, f32[19,2,8,256]{3,2,1,0:T(8,128)S(1)} %get-tuple-element.41.outer, ...), custom_call_target="tpu_custom_call" | custom-call | tf_op jit(solution)/shard_map/pallas_call | solution.py:1132
  15.4 0.6 %collective-permute-start.6 = (f32[176,256]{1,0:T(8,128)S(1)}, f32[176,256]{1,0:T(8,128)S(1)}, u32[]{:S(2)}, u32[]{:S(2)}) collective-permute-start(f32[176,256]{1,0:T(8,128)S(1)} %get-tuple-element.54), channel_id=1, source_target_pairs={{0,28},{4,8},{8,4},{12,16},{16,12},{20,24},{24,20},{28,0},{1,29},{... | collective-permute-start | bytes 540680 | tf_op jit(solution)/shard_map/ppermute | solution.py:1027
  16.6 0.7 %collective-permute-start.7 = (f32[176,256]{1,0:T(8,128)S(1)}, f32[176,256]{1,0:T(8,128)S(1)}, u32[]{:S(2)}, u32[]{:S(2)}) collective-permute-start(f32[176,256]{1,0:T(8,128)S(1)} %get-tuple-element.55), channel_id=1, source_target_pairs={{0,4},{4,0},{8,12},{12,8},{16,20},{20,16},{24,28},{28,24},{1,5},{5... | collective-permute-start | bytes 540680 | tf_op jit(solution)/shard_map/ppermute | solution.py:1027
  17.3 0.6 %shard_map.82.ends = f32[19,2,56,256]{3,2,1,0:T(8,128)S(1)} custom-call(f32[47,8,128]{2,1,0:T(8,128)S(1)} %shard_map.73.entries, f32[19,2,8,256]{3,2,1,0:T(8,128)S(1)} %get-tuple-element.41.outer, f32[11,2,8,256]{3,2,1,0:T(8,128)S(1)} %get-tuple-element.42.second, f32[19,2,32,256]{3,2,1,0:T(8,128)S(1)} %get-tuple-element.43.relaxed, ...), custom_call_target="tpu_custom_call" | custom-call | tf_op jit(solution)/shard_map/pallas_call | solution.py:1153
  17.9 0.9 %shard_map.83.sums = f32[4,2,32,256]{3,2,1,0:T(8,128)S(1)} custom-call(f32[32,512]{1,0:T(8,128)S(1)} %get-tuple-element.36.table, f32[4,1,40,256]{3,2,1,0:T(8,128)S(1)} %get-tuple-element.49.solid_near.after.solid), custom_call_target="tpu_custom_call" | custom-call | tf_op jit(solution)/shard_map/pallas_call | solution.py:1098
  19.0 1.5 %shard_map.85 = (f32[19,2,56,256]{3,2,1,0:T(8,128)S(1)}, f32[4,2,40,256]{3,2,1,0:T(8,128)S(1)}) custom-call(f32[47,8,128]{2,1,0:T(8,128)S(1)} %shard_map.73.entries, f32[4,2,32,256]{3,2,1,0:T(8,128)S(1)} %shard_map.83.sums, f32[4,2,8,256]{3,2,1,0:T(8,128)S(1)} %get-tuple-element.50.outer_sums, f32[19,2,8,256]{3,2,1,0:T(8,128)S(1)} %get-tuple-element.51.outer, ...), custom_call_target="tpu_custom_call" | custom-call | tf_op jit(solution)/shard_map/pallas_call | solution.py:1147
  20.5 1.5 %shard_map.87.refs_0_.middle = f32[19,2,56,256]{3,2,1,0:T(8,128)S(1)} custom-call(f32[47,8,128]{2,1,0:T(8,128)S(1)} %shard_map.73.entries, f32[19,2,56,256]{3,2,1,0:T(8,128)S(1)} %shard_map.82.ends, f32[19,2,56,256]{3,2,1,0:T(8,128)S(1)} %get-tuple-element.53.middle, f32[4,2,40,256]{3,2,1,0:T(8,128)S(1)} %get-tuple-element.56.solid), custom_call_target="tpu_custom_call" | custom-call | tf_op jit(solution)/shard_map/pallas_call | solution.py:1156
  22.0 0.9 %collective-permute-done.6.far.received = f32[176,256]{1,0:T(8,128)S(1)} collective-permute-done((f32[176,256]{1,0:T(8,128)S(1)}, f32[176,256]{1,0:T(8,128)S(1)}, u32[]{:S(2)}, u32[]{:S(2)}) %collective-permute-start.6) | collective-permute-done | bytes 180256 | tf_op jit(solution)/shard_map/ppermute | solution.py:1027
  23.4 1.0 %collective-permute-start.9 = (f32[160,256]{1,0:T(8,128)S(1)}, f32[160,256]{1,0:T(8,128)S(1)}, u32[]{:S(2)}, u32[]{:S(2)}) collective-permute-start(f32[160,256]{1,0:T(8,128)S(1)} %shard_map.88.refs_0_), channel_id=1, source_target_pairs={{0,28},{4,8},{8,4},{12,16},{16,12},{20,24},{24,20},{28,0},{1,29},{... | collective-permute-start | bytes 491528 | tf_op jit(solution)/shard_map/ppermute | solution.py:1027
  24.4 0.6 %shard_map.89 = f32[160,256]{1,0:T(8,128)S(1)} custom-call(f32[47,8,128]{2,1,0:T(8,128)S(1)} %shard_map.73.entries, f32[19,2,56,256]{3,2,1,0:T(8,128)S(1)} %shard_map.82.ends, f32[19,2,56,256]{3,2,1,0:T(8,128)S(1)} %get-tuple-element.53.middle, f32[4,1,40,256]{3,2,1,0:T(8,128)S(1)} %get-tuple-element.49.solid_near.after.solid, ...), custom_call_target="tpu_custom_call" | custom-call | tf_op jit(solution)/shard_map/pallas_call | solution.py:1161
  25.0 1.4 %shard_map.86.ends = f32[19,2,56,256]{3,2,1,0:T(8,128)S(1)} custom-call(f32[47,8,128]{2,1,0:T(8,128)S(1)} %shard_map.73.entries, f32[19,2,56,256]{3,2,1,0:T(8,128)S(1)} %shard_map.82.ends, f32[19,2,56,256]{3,2,1,0:T(8,128)S(1)} %get-tuple-element.53.middle, f32[4,1,40,256]{3,2,1,0:T(8,128)S(1)} %get-tuple-element.48.refs_0_.solid_far.solid, ...), custom_call_target="tpu_custom_call" | custom-call | tf_op jit(solution)/shard_map/pallas_call | solution.py:1173
  26.5 1.5 %shard_map.91.given = f32[19,4,32,256]{3,2,1,0:T(8,128)} custom-call(f32[19,2,56,256]{3,2,1,0:T(8,128)S(1)} %shard_map.86.ends, f32[19,2,56,256]{3,2,1,0:T(8,128)S(1)} %shard_map.87.refs_0_.middle), custom_call_target="tpu_custom_call" | custom-call | tf_op jit(solution)/shard_map/pallas_call | solution.py:1176
  28.0 2.0 %collective-permute-done.9.received = f32[160,256]{1,0:T(8,128)S(1)} collective-permute-done((f32[160,256]{1,0:T(8,128)S(1)}, f32[160,256]{1,0:T(8,128)S(1)}, u32[]{:S(2)}, u32[]{:S(2)}) %collective-permute-start.9) | collective-permute-done | bytes 163872 | tf_op jit(solution)/shard_map/ppermute | solution.py:1027
  30.0 0.8 %shard_map.92 = f32[19,4,32,256]{3,2,1,0:T(8,128)} custom-call(f32[19,2,56,256]{3,2,1,0:T(8,128)S(1)} %shard_map.86.ends, f32[160,256]{1,0:T(8,128)S(1)} %collective-permute-done.8.received, f32[5,32,256]{2,1,0:T(8,128)S(1)} %shard_map.90.far, f32[19,4,32,256]{3,2,1,0:T(8,128)} %shard_map.91.given), custom_call_target="tpu_custom_call", output_to_operand_aliasing={{}: (3, {})} | custom-call | tf_op jit(solution)/shard_map/pallas_call | solution.py:1186
  (20 shorter events, 1.5 us)
Async XLA Ops:
  0.0 5.2 %copy-start.1 = (f32[19]{0:T(128)S(1)}, f32[19]{0:T(128)}, u32[]{:S(2)}) copy-start(f32[19]{0:T(128)} %rates.1) | copy-start | bytes 232
  0.0 11.6 %copy-start = (f32[19,4,32,256]{3,2,1,0:T(8,128)S(1)}, f32[19,4,32,256]{3,2,1,0:T(8,128)}, u32[]{:S(2)}) copy-start(f32[19,4,32,256]{3,2,1,0:T(8,128)} %populations.5) | copy-start | bytes 7471108
  1.8 5.5 %collective-permute-start = (f32[8,128]{1,0:T(8,128)S(1)}, f32[8,128]{1,0:T(8,128)S(1)}, u32[]{:S(2)}, u32[]{:S(2)}) collective-permute-start(f32[8,128]{1,0:T(8,128)S(1)} %get-tuple-element.32), channel_id=1, source_target_pairs={{0,28},{4,8},{8,4},{12,16},{16,12},{20,24},{24,20},{28,0},{1,29},{... | collective-permute-start | bytes 12296 | tf_op jit(solution)/shard_map/ppermute | solution.py:1027
  5.2 2.1 %collective-permute-start.1 = (f32[8,128]{1,0:T(8,128)S(1)}, f32[8,128]{1,0:T(8,128)S(1)}, u32[]{:S(2)}, u32[]{:S(2)}) collective-permute-start(f32[8,128]{1,0:T(8,128)S(1)} %get-tuple-element.33), channel_id=1, source_target_pairs={{0,4},{4,0},{8,12},{12,8},{16,20},{20,16},{24,28},{28,24},{1,5},{5... | collective-permute-start | bytes 12296 | tf_op jit(solution)/shard_map/ppermute | solution.py:1027
  6.7 6.0 %collective-permute-start.5 = (f32[160,256]{1,0:T(8,128)S(1)}, f32[160,256]{1,0:T(8,128)S(1)}, u32[]{:S(2)}, u32[]{:S(2)}) collective-permute-start(f32[160,256]{1,0:T(8,128)S(1)} %get-tuple-element.40), channel_id=1, source_target_pairs={{0,4},{1,2},{2,1},{3,7},{4,0},{5,6},{6,5},{7,3},{8,12},{9,10},{10,... | collective-permute-start | bytes 491528 | tf_op jit(solution)/shard_map/ppermute | solution.py:1038
  7.3 7.4 %collective-permute-start.2 = (f32[160,256]{1,0:T(8,128)S(1)}, f32[160,256]{1,0:T(8,128)S(1)}, u32[]{:S(2)}, u32[]{:S(2)}) collective-permute-start(f32[160,256]{1,0:T(8,128)S(1)} %get-tuple-element.39), channel_id=1, source_target_pairs={{0,1},{1,0},{2,3},{3,2},{4,5},{5,4},{6,7},{7,6},{8,9},{9,8},{10,11... | collective-permute-start | bytes 491528 | tf_op jit(solution)/shard_map/ppermute | solution.py:1038
  10.0 4.6 %collective-permute-start.4 = (f32[8,128]{1,0:T(8,128)S(1)}, f32[8,128]{1,0:T(8,128)S(1)}, u32[]{:S(2)}, u32[]{:S(2)}) collective-permute-start(f32[8,128]{1,0:T(8,128)S(1)} %get-tuple-element.38.refs_0_), channel_id=1, source_target_pairs={{0,2},{1,3},{2,0},{3,1},{4,6},{5,7},{6,4},{7,5},{8,10},{9,11},{10,... | collective-permute-start | bytes 12296 | tf_op jit(solution)/shard_map/ppermute | solution.py:1019
  11.6 3.1 %collective-permute-start.3 = (f32[8,128]{1,0:T(8,128)S(1)}, f32[8,128]{1,0:T(8,128)S(1)}, u32[]{:S(2)}, u32[]{:S(2)}) collective-permute-start(f32[8,128]{1,0:T(8,128)S(1)} %get-tuple-element.38.refs_0_), channel_id=1, source_target_pairs={{0,4},{1,2},{2,1},{3,7},{4,0},{5,6},{6,5},{7,3},{8,12},{9,10},{10,... | collective-permute-start | bytes 12296 | tf_op jit(solution)/shard_map/ppermute | solution.py:1038
  15.4 7.4 %collective-permute-start.6 = (f32[176,256]{1,0:T(8,128)S(1)}, f32[176,256]{1,0:T(8,128)S(1)}, u32[]{:S(2)}, u32[]{:S(2)}) collective-permute-start(f32[176,256]{1,0:T(8,128)S(1)} %get-tuple-element.54), channel_id=1, source_target_pairs={{0,28},{4,8},{8,4},{12,16},{16,12},{20,24},{24,20},{28,0},{1,29},{... | collective-permute-start | bytes 540680 | tf_op jit(solution)/shard_map/ppermute | solution.py:1027
  16.6 7.8 %collective-permute-start.7 = (f32[176,256]{1,0:T(8,128)S(1)}, f32[176,256]{1,0:T(8,128)S(1)}, u32[]{:S(2)}, u32[]{:S(2)}) collective-permute-start(f32[176,256]{1,0:T(8,128)S(1)} %get-tuple-element.55), channel_id=1, source_target_pairs={{0,4},{4,0},{8,12},{12,8},{16,20},{20,16},{24,28},{28,24},{1,5},{5... | collective-permute-start | bytes 540680 | tf_op jit(solution)/shard_map/ppermute | solution.py:1027
  23.4 6.6 %collective-permute-start.9 = (f32[160,256]{1,0:T(8,128)S(1)}, f32[160,256]{1,0:T(8,128)S(1)}, u32[]{:S(2)}, u32[]{:S(2)}) collective-permute-start(f32[160,256]{1,0:T(8,128)S(1)} %shard_map.88.refs_0_), channel_id=1, source_target_pairs={{0,28},{4,8},{8,4},{12,16},{16,12},{20,24},{24,20},{28,0},{1,29},{... | collective-permute-start | bytes 491528 | tf_op jit(solution)/shard_map/ppermute | solution.py:1027
  24.9 5.0 %collective-permute-start.8 = (f32[160,256]{1,0:T(8,128)S(1)}, f32[160,256]{1,0:T(8,128)S(1)}, u32[]{:S(2)}, u32[]{:S(2)}) collective-permute-start(f32[160,256]{1,0:T(8,128)S(1)} %shard_map.89), channel_id=1, source_target_pairs={{0,4},{4,0},{8,12},{12,8},{16,20},{20,16},{24,28},{28,24},{1,5},{5... | collective-permute-start | bytes 491528 | tf_op jit(solution)/shard_map/ppermute | solution.py:1027

commit v9 on v8

--- a/solution.py
+++ b/solution.py
@@ -127,16 +127,12 @@
 
 
 def relax_rows(rates, target):
-    values = [rates[k] for k in range(19)]
+    values = [jnp.broadcast_to(rates[0:1, k : k + 1], (8, 128)) for k in range(19)]
     at = 0
     for block in RELAX:
         for row in block:
             for terms in row:
-                total = None
-                for k, factor in terms:
-                    part = values[k] * np.float32(factor)
-                    total = part if total is None else total + part
-                target[at] = jnp.full((8, 128), total, F32)
+                target[at] = sum(values[k] * np.float32(factor) for k, factor in terms)
                 at += 1
 
 
@@ -1069,7 +1065,7 @@
     first = edge_rows(size_x)[-1]
     fold = size_z // 128
     message = shape(-(-(first + 8 // fold) // 8) * 8, size_z)
-    entries = call(relax_kernel, shape(ENTRIES, 8, 128), 8, [SMEM])(relax_rates)
+    entries = call(relax_kernel, shape(ENTRIES, 8, 128), 8, [VMEM])(relax_rates[None, :])
     one, two = call(
         part(edge_kernel, *sizes),
         (message, message),

time: 31.1 us -> 31.4 us (level)
  waiting for transfers between devices: 3.95 us -> 4.68 us
  Pallas kernels: 16.1 us -> 15.6 us
    ppermute x6, waiting for transfers between devices: 2.88 us -> 3.99 us  [paired_x(): return lax.ppermute(value, 'gx', pairs)]
    pallas_call x1, Pallas kernels: 0.58 us -> 0.1 us  [local(): call(relax_kernel, shape(ENTRIES, 8, 128), 8, [VMEM])(relax_rates[None, :])]
    ppermute x1, starting transfers between devices: 1.53 us -> 1.93 us  [around(): lax.ppermute(value, axis, [(i, (i + steps) % count) for i in range(count)])]
    ppermute x6, starting transfers between devices: 5.77 us -> 5.4 us  [paired_x(): return lax.ppermute(value, 'gx', pairs)]
    ppermute x1, waiting for transfers between devices: 1.03 us -> 0.67 us  [around(): lax.ppermute(value, axis, [(i, (i + steps) % count) for i in range(count)])]
  transfers between devices with their start and end apart: 10 -> 10, of which waited for: 3 -> 3; matrix products, arithmetic and copies ran while one was open for 0% -> 0% of each run, Pallas kernels for 41% -> 39%
where the time goes in v9:
time: 31.4 us; the launch traced here: 31.2 us
  Pallas kernels  15.6 us (50%)
  starting transfers between devices  10.6 us (34%)
  waiting for transfers between devices  4.68 us (15%)
  between operations  0.32 us (1%)
    ppermute x6, starting transfers between devices, paired_x(): return lax.ppermute(value, 'gx', pairs)  5.4 us
    ppermute x6, waiting for transfers between devices, paired_x(): return lax.ppermute(value, 'gx', pairs)  3.99 us
    ppermute x3, starting transfers between devices, paired_y(): return lax.ppermute(value, ('gx', 'gy'), pairs)  3.29 us
    ppermute x1, starting transfers between devices, around(): lax.ppermute(value, axis, [(i, (i + steps) % count) for i in range(count)])  1.93 us
    pallas_call x2, Pallas kernels, staying(): call(part(stay_kernel, *sizes, planes), shape(4, len(planes), size_y, siz...  1.83 us
    pallas_call x1, Pallas kernels, local(): call(pack_kernel, (shape(32, rows), packed, packed, packed, band, band),...  1.77 us
    pallas_call x1, Pallas kernels, local(): call(part(last_kernel, *sizes, count), shape(19, *sizes), 16, [VMEM] * 2,...  1.5 us
    pallas_call x1, Pallas kernels, local(): call(part(second_kernel, *sizes, count), padded(len(inside)), 16, [VMEM]...  1.49 us
  transfers between devices with their start and end apart: 10, of which 3 were waited for; matrix products, arithmetic and copies ran while one was open for 0% of the time, Pallas kernels for 39%

profile of v9, /device:TPU:0, one launch (start us, length us, event | category | flops | bytes accessed | tf_op | source)
XLA Modules:
  0.0 31.2 jit_solution(10771436226428464855)
XLA Ops:
  0.0 1.8 %shard_map.74 = (f32[32,512]{1,0:T(8,128)S(1)}, f32[8,128]{1,0:T(8,128)S(1)}, f32[8,128]{1,0:T(8,128)S(1)}, f32[8,128]{1,0:T(8,128)S(1)}, f32[19,4,8,256]{3,2,1,0:T(8,128)S(1)}, /*index=5*/f32[19,4,8,256]{3,2,1,0:T(8,128)S(1)}) custom-call(f32[3,512]{1,0:T(4,128)} %velocity_in.1, f32[3,512]{1,0:T(4,128)} %change_in.1, f32[27,512]{1,0:T(8,128)} %fractions_in.1, ...), custom_call_target="tpu_custom_call" | custom-call | tf_op jit(solution)/shard_map/pallas_call | solution.py:1050
  1.8 3.4 %collective-permute-start = (f32[8,128]{1,0:T(8,128)S(1)}, f32[8,128]{1,0:T(8,128)S(1)}, u32[]{:S(2)}, u32[]{:S(2)}) collective-permute-start(f32[8,128]{1,0:T(8,128)S(1)} %get-tuple-element.32), channel_id=1, source_target_pairs={{0,28},{4,8},{8,4},{12,16},{16,12},{20,24},{24,20},{28,0},{1,29},{... | collective-permute-start | bytes 12296 | tf_op jit(solution)/shard_map/ppermute | solution.py:1023
  5.3 0.9 %shard_map.75 = (f32[160,256]{1,0:T(8,128)S(1)}, f32[160,256]{1,0:T(8,128)S(1)}) custom-call(f32[19,4,8,256]{3,2,1,0:T(8,128)S(1)} %get-tuple-element.34.bottom, f32[19,4,8,256]{3,2,1,0:T(8,128)S(1)} %get-tuple-element.35.top, f32[32,512]{1,0:T(8,128)S(1)} %get-tuple-element.36.table, f32[47,8,128]{2,1,0:T(8,128)S(1)} %shard_map.73.entries), custom_call_target="tpu_custom_call" | custom-call | tf_op jit(solution)/shard_map/pallas_call | solution.py:1069
  6.2 0.6 %collective-permute-start.5 = (f32[160,256]{1,0:T(8,128)S(1)}, f32[160,256]{1,0:T(8,128)S(1)}, u32[]{:S(2)}, u32[]{:S(2)}) collective-permute-start(f32[160,256]{1,0:T(8,128)S(1)} %get-tuple-element.40), channel_id=1, source_target_pairs={{0,4},{1,2},{2,1},{3,7},{4,0},{5,6},{6,5},{7,3},{8,12},{9,10},{10,... | collective-permute-start | bytes 491528 | tf_op jit(solution)/shard_map/ppermute | solution.py:1034
  6.8 2.7 %collective-permute-start.2 = (f32[160,256]{1,0:T(8,128)S(1)}, f32[160,256]{1,0:T(8,128)S(1)}, u32[]{:S(2)}, u32[]{:S(2)}) collective-permute-start(f32[160,256]{1,0:T(8,128)S(1)} %get-tuple-element.39), channel_id=1, source_target_pairs={{0,1},{1,0},{2,3},{3,2},{4,5},{5,4},{6,7},{7,6},{8,9},{9,8},{10,11... | collective-permute-start | bytes 491528 | tf_op jit(solution)/shard_map/ppermute | solution.py:1034
  9.5 1.9 %collective-permute-start.4 = (f32[8,128]{1,0:T(8,128)S(1)}, f32[8,128]{1,0:T(8,128)S(1)}, u32[]{:S(2)}, u32[]{:S(2)}) collective-permute-start(f32[8,128]{1,0:T(8,128)S(1)} %get-tuple-element.38.refs_0_), channel_id=1, source_target_pairs={{0,2},{1,3},{2,0},{3,1},{4,6},{5,7},{6,4},{7,5},{8,10},{9,11},{10,... | collective-permute-start | bytes 12296 | tf_op jit(solution)/shard_map/ppermute | solution.py:1015
  11.5 1.1 %shard_map.78 = (f32[19,2,32,256]{3,2,1,0:T(8,128)S(1)}, f32[19,2,32,256]{3,2,1,0:T(8,128)S(1)}, f32[2,32,256]{2,1,0:T(8,128)S(1)}) custom-call(f32[47,8,128]{2,1,0:T(8,128)S(1)} %shard_map.73.entries, f32[19,4,32,256]{3,2,1,0:T(8,128)S(1)} %copy-done), custom_call_target="tpu_custom_call" | custom-call | tf_op jit(solution)/shard_map/pallas_call | solution.py:1103
  12.6 0.9 %shard_map.79.sums = f32[4,2,32,256]{3,2,1,0:T(8,128)S(1)} custom-call(f32[32,512]{1,0:T(8,128)S(1)} %get-tuple-element.36.table, f32[160,256]{1,0:T(8,128)S(1)} %collective-permute-done.5.refs_4_.after.refs_0_), custom_call_target="tpu_custom_call" | custom-call | tf_op jit(solution)/shard_map/pallas_call | solution.py:1094
  13.5 0.7 %collective-permute-done.4.refs_3_ = f32[8,128]{1,0:T(8,128)S(1)} collective-permute-done((f32[8,128]{1,0:T(8,128)S(1)}, f32[8,128]{1,0:T(8,128)S(1)}, u32[]{:S(2)}, u32[]{:S(2)}) %collective-permute-start.4) | collective-permute-done | bytes 4128 | tf_op jit(solution)/shard_map/ppermute | solution.py:1015
  14.4 0.6 %shard_map.80 = (f32[4,1,40,256]{3,2,1,0:T(8,128)S(1)}, f32[176,256]{1,0:T(8,128)S(1)}) custom-call(f32[47,8,128]{2,1,0:T(8,128)S(1)} %shard_map.73.entries, f32[4,2,32,256]{3,2,1,0:T(8,128)S(1)} %shard_map.79.sums, f32[4,2,8,256]{3,2,1,0:T(8,128)S(1)} %get-tuple-element.46.outer_sums, f32[19,2,8,256]{3,2,1,0:T(8,128)S(1)} %get-tuple-element.41.outer, ...), custom_call_target="tpu_custom_call" | custom-call | tf_op jit(solution)/shard_map/pallas_call | solution.py:1128
  15.0 1.1 %collective-permute-start.6 = (f32[176,256]{1,0:T(8,128)S(1)}, f32[176,256]{1,0:T(8,128)S(1)}, u32[]{:S(2)}, u32[]{:S(2)}) collective-permute-start(f32[176,256]{1,0:T(8,128)S(1)} %get-tuple-element.54), channel_id=1, source_target_pairs={{0,28},{4,8},{8,4},{12,16},{16,12},{20,24},{24,20},{28,0},{1,29},{... | collective-permute-start | bytes 540680 | tf_op jit(solution)/shard_map/ppermute | solution.py:1023
  16.0 0.5 %shard_map.81 = (f32[4,1,40,256]{3,2,1,0:T(8,128)S(1)}, f32[176,256]{1,0:T(8,128)S(1)}) custom-call(f32[47,8,128]{2,1,0:T(8,128)S(1)} %shard_map.73.entries, f32[4,2,32,256]{3,2,1,0:T(8,128)S(1)} %shard_map.79.sums, f32[4,2,8,256]{3,2,1,0:T(8,128)S(1)} %get-tuple-element.46.outer_sums, f32[19,2,8,256]{3,2,1,0:T(8,128)S(1)} %get-tuple-element.41.outer, ...), custom_call_target="tpu_custom_call" | custom-call | tf_op jit(solution)/shard_map/pallas_call | solution.py:1128
  16.8 0.6 %shard_map.82.ends = f32[19,2,56,256]{3,2,1,0:T(8,128)S(1)} custom-call(f32[47,8,128]{2,1,0:T(8,128)S(1)} %shard_map.73.entries, f32[19,2,8,256]{3,2,1,0:T(8,128)S(1)} %get-tuple-element.41.outer, f32[11,2,8,256]{3,2,1,0:T(8,128)S(1)} %get-tuple-element.42.second, f32[19,2,32,256]{3,2,1,0:T(8,128)S(1)} %get-tuple-element.43.relaxed, ...), custom_call_target="tpu_custom_call" | custom-call | tf_op jit(solution)/shard_map/pallas_call | solution.py:1149
  17.4 0.9 %shard_map.83.sums = f32[4,2,32,256]{3,2,1,0:T(8,128)S(1)} custom-call(f32[32,512]{1,0:T(8,128)S(1)} %get-tuple-element.36.table, f32[4,1,40,256]{3,2,1,0:T(8,128)S(1)} %get-tuple-element.49.solid_near.after.solid), custom_call_target="tpu_custom_call" | custom-call | tf_op jit(solution)/shard_map/pallas_call | solution.py:1094
  18.5 1.5 %shard_map.85 = (f32[19,2,56,256]{3,2,1,0:T(8,128)S(1)}, f32[4,2,40,256]{3,2,1,0:T(8,128)S(1)}) custom-call(f32[47,8,128]{2,1,0:T(8,128)S(1)} %shard_map.73.entries, f32[4,2,32,256]{3,2,1,0:T(8,128)S(1)} %shard_map.83.sums, f32[4,2,8,256]{3,2,1,0:T(8,128)S(1)} %get-tuple-element.50.outer_sums, f32[19,2,8,256]{3,2,1,0:T(8,128)S(1)} %get-tuple-element.51.outer, ...), custom_call_target="tpu_custom_call" | custom-call | tf_op jit(solution)/shard_map/pallas_call | solution.py:1143
  20.0 1.5 %shard_map.87.refs_0_.middle = f32[19,2,56,256]{3,2,1,0:T(8,128)S(1)} custom-call(f32[47,8,128]{2,1,0:T(8,128)S(1)} %shard_map.73.entries, f32[19,2,56,256]{3,2,1,0:T(8,128)S(1)} %shard_map.82.ends, f32[19,2,56,256]{3,2,1,0:T(8,128)S(1)} %get-tuple-element.53.middle, f32[4,2,40,256]{3,2,1,0:T(8,128)S(1)} %get-tuple-element.56.solid), custom_call_target="tpu_custom_call" | custom-call | tf_op jit(solution)/shard_map/pallas_call | solution.py:1152
  21.5 1.2 %collective-permute-done.6.far.received = f32[176,256]{1,0:T(8,128)S(1)} collective-permute-done((f32[176,256]{1,0:T(8,128)S(1)}, f32[176,256]{1,0:T(8,128)S(1)}, u32[]{:S(2)}, u32[]{:S(2)}) %collective-permute-start.6) | collective-permute-done | bytes 180256 | tf_op jit(solution)/shard_map/ppermute | solution.py:1023
  22.7 0.5 %shard_map.88.refs_0_ = f32[160,256]{1,0:T(8,128)S(1)} custom-call(f32[47,8,128]{2,1,0:T(8,128)S(1)} %shard_map.73.entries, f32[19,2,56,256]{3,2,1,0:T(8,128)S(1)} %shard_map.82.ends, f32[19,2,56,256]{3,2,1,0:T(8,128)S(1)} %get-tuple-element.53.middle, f32[4,1,40,256]{3,2,1,0:T(8,128)S(1)} %get-tuple-element.48.refs_0_.solid_far.solid, ...), custom_call_target="tpu_custom_call" | custom-call | tf_op jit(solution)/shard_map/pallas_call | solution.py:1157
  23.2 0.6 %collective-permute-start.9 = (f32[160,256]{1,0:T(8,128)S(1)}, f32[160,256]{1,0:T(8,128)S(1)}, u32[]{:S(2)}, u32[]{:S(2)}) collective-permute-start(f32[160,256]{1,0:T(8,128)S(1)} %shard_map.88.refs_0_), channel_id=1, source_target_pairs={{0,28},{4,8},{8,4},{12,16},{16,12},{20,24},{24,20},{28,0},{1,29},{... | collective-permute-start | bytes 491528 | tf_op jit(solution)/shard_map/ppermute | solution.py:1023
  23.9 0.6 %shard_map.89 = f32[160,256]{1,0:T(8,128)S(1)} custom-call(f32[47,8,128]{2,1,0:T(8,128)S(1)} %shard_map.73.entries, f32[19,2,56,256]{3,2,1,0:T(8,128)S(1)} %shard_map.82.ends, f32[19,2,56,256]{3,2,1,0:T(8,128)S(1)} %get-tuple-element.53.middle, f32[4,1,40,256]{3,2,1,0:T(8,128)S(1)} %get-tuple-element.49.solid_near.after.solid, ...), custom_call_target="tpu_custom_call" | custom-call | tf_op jit(solution)/shard_map/pallas_call | solution.py:1157
  24.5 1.4 %shard_map.86.ends = f32[19,2,56,256]{3,2,1,0:T(8,128)S(1)} custom-call(f32[47,8,128]{2,1,0:T(8,128)S(1)} %shard_map.73.entries, f32[19,2,56,256]{3,2,1,0:T(8,128)S(1)} %shard_map.82.ends, f32[19,2,56,256]{3,2,1,0:T(8,128)S(1)} %get-tuple-element.53.middle, f32[4,1,40,256]{3,2,1,0:T(8,128)S(1)} %get-tuple-element.48.refs_0_.solid_far.solid, ...), custom_call_target="tpu_custom_call" | custom-call | tf_op jit(solution)/shard_map/pallas_call | solution.py:1169
  26.0 1.5 %shard_map.91.given = f32[19,4,32,256]{3,2,1,0:T(8,128)} custom-call(f32[19,2,56,256]{3,2,1,0:T(8,128)S(1)} %shard_map.86.ends, f32[19,2,56,256]{3,2,1,0:T(8,128)S(1)} %shard_map.87.refs_0_.middle), custom_call_target="tpu_custom_call" | custom-call | tf_op jit(solution)/shard_map/pallas_call | solution.py:1172
  27.5 2.7 %collective-permute-done.9.received = f32[160,256]{1,0:T(8,128)S(1)} collective-permute-done((f32[160,256]{1,0:T(8,128)S(1)}, f32[160,256]{1,0:T(8,128)S(1)}, u32[]{:S(2)}, u32[]{:S(2)}) %collective-permute-start.9) | collective-permute-done | bytes 163872 | tf_op jit(solution)/shard_map/ppermute | solution.py:1023
  30.2 0.8 %shard_map.92 = f32[19,4,32,256]{3,2,1,0:T(8,128)} custom-call(f32[19,2,56,256]{3,2,1,0:T(8,128)S(1)} %shard_map.86.ends, f32[160,256]{1,0:T(8,128)S(1)} %collective-permute-done.8.received, f32[5,32,256]{2,1,0:T(8,128)S(1)} %shard_map.90.far, f32[19,4,32,256]{3,2,1,0:T(8,128)} %shard_map.91.given), custom_call_target="tpu_custom_call", output_to_operand_aliasing={{}: (3, {})} | custom-call | tf_op jit(solution)/shard_map/pallas_call | solution.py:1182
  (20 shorter events, 0.7 us)
Async XLA Ops:
  0.0 5.2 %copy-start.1 = (f32[19]{0:T(128)S(1)}, f32[19]{0:T(128)}, u32[]{:S(2)}) copy-start(f32[19]{0:T(128)} %param.8) | copy-start | bytes 232
  0.0 11.5 %copy-start = (f32[19,4,32,256]{3,2,1,0:T(8,128)S(1)}, f32[19,4,32,256]{3,2,1,0:T(8,128)}, u32[]{:S(2)}) copy-start(f32[19,4,32,256]{3,2,1,0:T(8,128)} %populations.5) | copy-start | bytes 7471108
  1.8 5.0 %collective-permute-start = (f32[8,128]{1,0:T(8,128)S(1)}, f32[8,128]{1,0:T(8,128)S(1)}, u32[]{:S(2)}, u32[]{:S(2)}) collective-permute-start(f32[8,128]{1,0:T(8,128)S(1)} %get-tuple-element.32), channel_id=1, source_target_pairs={{0,28},{4,8},{8,4},{12,16},{16,12},{20,24},{24,20},{28,0},{1,29},{... | collective-permute-start | bytes 12296 | tf_op jit(solution)/shard_map/ppermute | solution.py:1023
  5.2 1.6 %collective-permute-start.1 = (f32[8,128]{1,0:T(8,128)S(1)}, f32[8,128]{1,0:T(8,128)S(1)}, u32[]{:S(2)}, u32[]{:S(2)}) collective-permute-start(f32[8,128]{1,0:T(8,128)S(1)} %get-tuple-element.33), channel_id=1, source_target_pairs={{0,4},{4,0},{8,12},{12,8},{16,20},{20,16},{24,28},{28,24},{1,5},{5... | collective-permute-start | bytes 12296 | tf_op jit(solution)/shard_map/ppermute | solution.py:1023
  6.2 6.4 %collective-permute-start.5 = (f32[160,256]{1,0:T(8,128)S(1)}, f32[160,256]{1,0:T(8,128)S(1)}, u32[]{:S(2)}, u32[]{:S(2)}) collective-permute-start(f32[160,256]{1,0:T(8,128)S(1)} %get-tuple-element.40), channel_id=1, source_target_pairs={{0,4},{1,2},{2,1},{3,7},{4,0},{5,6},{6,5},{7,3},{8,12},{9,10},{10,... | collective-permute-start | bytes 491528 | tf_op jit(solution)/shard_map/ppermute | solution.py:1034
  6.8 7.4 %collective-permute-start.2 = (f32[160,256]{1,0:T(8,128)S(1)}, f32[160,256]{1,0:T(8,128)S(1)}, u32[]{:S(2)}, u32[]{:S(2)}) collective-permute-start(f32[160,256]{1,0:T(8,128)S(1)} %get-tuple-element.39), channel_id=1, source_target_pairs={{0,1},{1,0},{2,3},{3,2},{4,5},{5,4},{6,7},{7,6},{8,9},{9,8},{10,11... | collective-permute-start | bytes 491528 | tf_op jit(solution)/shard_map/ppermute | solution.py:1034
  9.5 4.7 %collective-permute-start.4 = (f32[8,128]{1,0:T(8,128)S(1)}, f32[8,128]{1,0:T(8,128)S(1)}, u32[]{:S(2)}, u32[]{:S(2)}) collective-permute-start(f32[8,128]{1,0:T(8,128)S(1)} %get-tuple-element.38.refs_0_), channel_id=1, source_target_pairs={{0,2},{1,3},{2,0},{3,1},{4,6},{5,7},{6,4},{7,5},{8,10},{9,11},{10,... | collective-permute-start | bytes 12296 | tf_op jit(solution)/shard_map/ppermute | solution.py:1015
  11.5 2.8 %collective-permute-start.3 = (f32[8,128]{1,0:T(8,128)S(1)}, f32[8,128]{1,0:T(8,128)S(1)}, u32[]{:S(2)}, u32[]{:S(2)}) collective-permute-start(f32[8,128]{1,0:T(8,128)S(1)} %get-tuple-element.38.refs_0_), channel_id=1, source_target_pairs={{0,4},{1,2},{2,1},{3,7},{4,0},{5,6},{6,5},{7,3},{8,12},{9,10},{10,... | collective-permute-start | bytes 12296 | tf_op jit(solution)/shard_map/ppermute | solution.py:1034
  15.0 7.7 %collective-permute-start.6 = (f32[176,256]{1,0:T(8,128)S(1)}, f32[176,256]{1,0:T(8,128)S(1)}, u32[]{:S(2)}, u32[]{:S(2)}) collective-permute-start(f32[176,256]{1,0:T(8,128)S(1)} %get-tuple-element.54), channel_id=1, source_target_pairs={{0,28},{4,8},{8,4},{12,16},{16,12},{20,24},{24,20},{28,0},{1,29},{... | collective-permute-start | bytes 540680 | tf_op jit(solution)/shard_map/ppermute | solution.py:1023
  16.6 7.3 %collective-permute-start.7 = (f32[176,256]{1,0:T(8,128)S(1)}, f32[176,256]{1,0:T(8,128)S(1)}, u32[]{:S(2)}, u32[]{:S(2)}) collective-permute-start(f32[176,256]{1,0:T(8,128)S(1)} %get-tuple-element.55), channel_id=1, source_target_pairs={{0,4},{4,0},{8,12},{12,8},{16,20},{20,16},{24,28},{28,24},{1,5},{5... | collective-permute-start | bytes 540680 | tf_op jit(solution)/shard_map/ppermute | solution.py:1023
  23.2 7.0 %collective-permute-start.9 = (f32[160,256]{1,0:T(8,128)S(1)}, f32[160,256]{1,0:T(8,128)S(1)}, u32[]{:S(2)}, u32[]{:S(2)}) collective-permute-start(f32[160,256]{1,0:T(8,128)S(1)} %shard_map.88.refs_0_), channel_id=1, source_target_pairs={{0,28},{4,8},{8,4},{12,16},{16,12},{20,24},{24,20},{28,0},{1,29},{... | collective-permute-start | bytes 491528 | tf_op jit(solution)/shard_map/ppermute | solution.py:1023
  24.5 5.8 %collective-permute-start.8 = (f32[160,256]{1,0:T(8,128)S(1)}, f32[160,256]{1,0:T(8,128)S(1)}, u32[]{:S(2)}, u32[]{:S(2)}) collective-permute-start(f32[160,256]{1,0:T(8,128)S(1)} %shard_map.89), channel_id=1, source_target_pairs={{0,4},{4,0},{8,12},{12,8},{16,20},{20,16},{24,28},{28,24},{1,5},{5... | collective-permute-start | bytes 491528 | tf_op jit(solution)/shard_map/ppermute | solution.py:1023

commit v10 on v8

--- a/solution.py
+++ b/solution.py
@@ -350,7 +350,8 @@
         rows = jnp.concatenate([w for block in weights for w in block], axis=0)
         high, low = halves(rows)
         hot = jnp.where(rows_z == a_z + (off_z - 1), 1.0, 0.0).astype(BF16)
-        part = dot_t(high, hot) + dot_t(low, hot)
+        both = dot_t(jnp.concatenate([high, low], axis=0), hot)
+        part = both[: rows.shape[0]] + both[rows.shape[0] :]
         totals = part if totals is None else totals + part
     return totals
 
@@ -419,14 +420,16 @@
     leaving = (dest < 9) & (dest != 4)
     slot = jnp.sum(hot * (begin + rank - 1.0), axis=0, keepdims=True)
     slot = jnp.where(leaving, slot, -1.0).astype(I32)
-    chosen = jnp.where(iota((128, rows), 0) == slot, 1.0, 0.0).astype(BF16)
+    chosen = jnp.where(iota((LANES, rows), 0) == slot, 1.0, 0.0).astype(BF16)
+    chosen = jnp.concatenate([chosen, jnp.zeros((128 - LANES, rows), BF16)], axis=0)
     new_velocity = velocity[...] + change[...]
     payload = jnp.concatenate(
         [fractions[...], new_velocity, anchor[...].astype(F32), jnp.zeros((1, rows), F32)], axis=0
     )
     high = payload.astype(BF16)
     middle, low = halves(payload - high.astype(F32))
-    packed = dot_t(high, chosen) + dot_t(middle, chosen) + dot_t(low, chosen)
+    pieces = dot_t(jnp.concatenate([high, middle, low], axis=0), chosen)
+    packed = pieces[0:32] + pieces[32:64] + pieces[64:96]
     packed = folded(packed)
     lane = lax.rem(iota((8, 128), 1), jnp.int32(LANES))
     own[...] = jnp.where(lane < 2 * CAP, packed, 0.0)

time: 31.1 us -> 31 us (level)
  Pallas kernels: 16.1 us -> 15.5 us
  waiting for transfers between devices: 3.95 us -> 4.39 us
    ppermute x6, waiting for transfers between devices: 2.88 us -> 3.34 us  [paired_x(): return lax.ppermute(value, 'gx', pairs)]
  transfers between devices with their start and end apart: 10 -> 10, of which waited for: 3 -> 3; matrix products, arithmetic and copies ran while one was open for 0% -> 0% of each run, Pallas kernels for 41% -> 40%
where the time goes in v10:
time: 31 us; the launch traced here: 30.8 us
  Pallas kernels  15.5 us (50%)
  starting transfers between devices  10.6 us (34%)
  waiting for transfers between devices  4.39 us (14%)
  between operations  0.32 us (1%)
    ppermute x6, starting transfers between devices, paired_x(): return lax.ppermute(value, 'gx', pairs)  5.62 us
    ppermute x6, waiting for transfers between devices, paired_x(): return lax.ppermute(value, 'gx', pairs)  3.34 us
    ppermute x3, starting transfers between devices, paired_y(): return lax.ppermute(value, ('gx', 'gy'), pairs)  3.29 us
    ppermute x1, starting transfers between devices, around(): lax.ppermute(value, axis, [(i, (i + steps) % count) for i in range(count)])  1.69 us
    pallas_call x1, Pallas kernels, local(): call(pack_kernel, (shape(32, rows), packed, packed, packed, band, band),...  1.69 us
    pallas_call x2, Pallas kernels, staying(): call(part(stay_kernel, *sizes, planes), shape(4, len(planes), size_y, siz...  1.56 us
    pallas_call x1, Pallas kernels, local(): call(part(last_kernel, *sizes, count), shape(19, *sizes), 16, [VMEM] * 2,...  1.5 us
    pallas_call x1, Pallas kernels, local(): call(part(middle_kernel, *sizes, inside), (padded(len(inside)), solid_sha...  1.5 us
  transfers between devices with their start and end apart: 10, of which 3 were waited for; matrix products, arithmetic and copies ran while one was open for 0% of the time, Pallas kernels for 40%

profile of v10, /device:TPU:0, one launch (start us, length us, event | category | flops | bytes accessed | tf_op | source)
XLA Modules:
  0.0 30.8 jit_solution(12221295557664619942)
XLA Ops:
  0.0 1.7 %shard_map.74 = (f32[32,512]{1,0:T(8,128)S(1)}, f32[8,128]{1,0:T(8,128)S(1)}, f32[8,128]{1,0:T(8,128)S(1)}, f32[8,128]{1,0:T(8,128)S(1)}, f32[19,4,8,256]{3,2,1,0:T(8,128)S(1)}, /*index=5*/f32[19,4,8,256]{3,2,1,0:T(8,128)S(1)}) custom-call(f32[3,512]{1,0:T(4,128)} %velocity_in.1, f32[3,512]{1,0:T(4,128)} %change_in.1, f32[27,512]{1,0:T(8,128)} %fractions_in.1, ...), custom_call_target="tpu_custom_call" | custom-call | tf_op jit(solution)/shard_map/pallas_call | solution.py:1057
  1.7 3.4 %collective-permute-start = (f32[8,128]{1,0:T(8,128)S(1)}, f32[8,128]{1,0:T(8,128)S(1)}, u32[]{:S(2)}, u32[]{:S(2)}) collective-permute-start(f32[8,128]{1,0:T(8,128)S(1)} %get-tuple-element.32), channel_id=1, source_target_pairs={{0,28},{4,8},{8,4},{12,16},{16,12},{20,24},{24,20},{28,0},{1,29},{... | collective-permute-start | bytes 12296 | tf_op jit(solution)/shard_map/ppermute | solution.py:1030
  5.1 0.6 %shard_map.73.entries = f32[47,8,128]{2,1,0:T(8,128)S(1)} custom-call(f32[19]{0:T(128)S(1)} %copy-done.1), custom_call_target="tpu_custom_call" | custom-call | tf_op jit(solution)/shard_map/pallas_call | solution.py:1075
  5.7 0.7 %shard_map.75 = (f32[160,256]{1,0:T(8,128)S(1)}, f32[160,256]{1,0:T(8,128)S(1)}) custom-call(f32[19,4,8,256]{3,2,1,0:T(8,128)S(1)} %get-tuple-element.34.bottom, f32[19,4,8,256]{3,2,1,0:T(8,128)S(1)} %get-tuple-element.35.top, f32[32,512]{1,0:T(8,128)S(1)} %get-tuple-element.36.table, f32[47,8,128]{2,1,0:T(8,128)S(1)} %shard_map.73.entries), custom_call_target="tpu_custom_call" | custom-call | tf_op jit(solution)/shard_map/pallas_call | solution.py:1076
  6.4 0.6 %collective-permute-start.5 = (f32[160,256]{1,0:T(8,128)S(1)}, f32[160,256]{1,0:T(8,128)S(1)}, u32[]{:S(2)}, u32[]{:S(2)}) collective-permute-start(f32[160,256]{1,0:T(8,128)S(1)} %get-tuple-element.40), channel_id=1, source_target_pairs={{0,4},{1,2},{2,1},{3,7},{4,0},{5,6},{6,5},{7,3},{8,12},{9,10},{10,... | collective-permute-start | bytes 491528 | tf_op jit(solution)/shard_map/ppermute | solution.py:1041
  7.0 2.7 %collective-permute-start.2 = (f32[160,256]{1,0:T(8,128)S(1)}, f32[160,256]{1,0:T(8,128)S(1)}, u32[]{:S(2)}, u32[]{:S(2)}) collective-permute-start(f32[160,256]{1,0:T(8,128)S(1)} %get-tuple-element.39), channel_id=1, source_target_pairs={{0,1},{1,0},{2,3},{3,2},{4,5},{5,4},{6,7},{7,6},{8,9},{9,8},{10,11... | collective-permute-start | bytes 491528 | tf_op jit(solution)/shard_map/ppermute | solution.py:1041
  9.7 1.7 %collective-permute-start.4 = (f32[8,128]{1,0:T(8,128)S(1)}, f32[8,128]{1,0:T(8,128)S(1)}, u32[]{:S(2)}, u32[]{:S(2)}) collective-permute-start(f32[8,128]{1,0:T(8,128)S(1)} %get-tuple-element.38.refs_0_), channel_id=1, source_target_pairs={{0,2},{1,3},{2,0},{3,1},{4,6},{5,7},{6,4},{7,5},{8,10},{9,11},{10,... | collective-permute-start | bytes 12296 | tf_op jit(solution)/shard_map/ppermute | solution.py:1022
  11.4 1.1 %shard_map.78 = (f32[19,2,32,256]{3,2,1,0:T(8,128)S(1)}, f32[19,2,32,256]{3,2,1,0:T(8,128)S(1)}, f32[2,32,256]{2,1,0:T(8,128)S(1)}) custom-call(f32[47,8,128]{2,1,0:T(8,128)S(1)} %shard_map.73.entries, f32[19,4,32,256]{3,2,1,0:T(8,128)S(1)} %copy-done), custom_call_target="tpu_custom_call" | custom-call | tf_op jit(solution)/shard_map/pallas_call | solution.py:1110
  12.5 0.8 %shard_map.79.sums = f32[4,2,32,256]{3,2,1,0:T(8,128)S(1)} custom-call(f32[32,512]{1,0:T(8,128)S(1)} %get-tuple-element.36.table, f32[160,256]{1,0:T(8,128)S(1)} %collective-permute-done.5.refs_4_.after.refs_0_), custom_call_target="tpu_custom_call" | custom-call | tf_op jit(solution)/shard_map/pallas_call | solution.py:1101
  13.3 1.0 %collective-permute-done.4.refs_3_ = f32[8,128]{1,0:T(8,128)S(1)} collective-permute-done((f32[8,128]{1,0:T(8,128)S(1)}, f32[8,128]{1,0:T(8,128)S(1)}, u32[]{:S(2)}, u32[]{:S(2)}) %collective-permute-start.4) | collective-permute-done | bytes 4128 | tf_op jit(solution)/shard_map/ppermute | solution.py:1022
  14.5 0.6 %shard_map.80 = (f32[4,1,40,256]{3,2,1,0:T(8,128)S(1)}, f32[176,256]{1,0:T(8,128)S(1)}) custom-call(f32[47,8,128]{2,1,0:T(8,128)S(1)} %shard_map.73.entries, f32[4,2,32,256]{3,2,1,0:T(8,128)S(1)} %shard_map.79.sums, f32[4,2,8,256]{3,2,1,0:T(8,128)S(1)} %get-tuple-element.46.outer_sums, f32[19,2,8,256]{3,2,1,0:T(8,128)S(1)} %get-tuple-element.41.outer, ...), custom_call_target="tpu_custom_call" | custom-call | tf_op jit(solution)/shard_map/pallas_call | solution.py:1135
  15.1 0.8 %collective-permute-start.6 = (f32[176,256]{1,0:T(8,128)S(1)}, f32[176,256]{1,0:T(8,128)S(1)}, u32[]{:S(2)}, u32[]{:S(2)}) collective-permute-start(f32[176,256]{1,0:T(8,128)S(1)} %get-tuple-element.54), channel_id=1, source_target_pairs={{0,28},{4,8},{8,4},{12,16},{16,12},{20,24},{24,20},{28,0},{1,29},{... | collective-permute-start | bytes 540680 | tf_op jit(solution)/shard_map/ppermute | solution.py:1030
  15.9 0.5 %shard_map.81 = (f32[4,1,40,256]{3,2,1,0:T(8,128)S(1)}, f32[176,256]{1,0:T(8,128)S(1)}) custom-call(f32[47,8,128]{2,1,0:T(8,128)S(1)} %shard_map.73.entries, f32[4,2,32,256]{3,2,1,0:T(8,128)S(1)} %shard_map.79.sums, f32[4,2,8,256]{3,2,1,0:T(8,128)S(1)} %get-tuple-element.46.outer_sums, f32[19,2,8,256]{3,2,1,0:T(8,128)S(1)} %get-tuple-element.41.outer, ...), custom_call_target="tpu_custom_call" | custom-call | tf_op jit(solution)/shard_map/pallas_call | solution.py:1135
  16.9 0.6 %shard_map.82.ends = f32[19,2,56,256]{3,2,1,0:T(8,128)S(1)} custom-call(f32[47,8,128]{2,1,0:T(8,128)S(1)} %shard_map.73.entries, f32[19,2,8,256]{3,2,1,0:T(8,128)S(1)} %get-tuple-element.41.outer, f32[11,2,8,256]{3,2,1,0:T(8,128)S(1)} %get-tuple-element.42.second, f32[19,2,32,256]{3,2,1,0:T(8,128)S(1)} %get-tuple-element.43.relaxed, ...), custom_call_target="tpu_custom_call" | custom-call | tf_op jit(solution)/shard_map/pallas_call | solution.py:1156
  17.6 0.8 %shard_map.83.sums = f32[4,2,32,256]{3,2,1,0:T(8,128)S(1)} custom-call(f32[32,512]{1,0:T(8,128)S(1)} %get-tuple-element.36.table, f32[4,1,40,256]{3,2,1,0:T(8,128)S(1)} %get-tuple-element.49.solid_near.after.solid), custom_call_target="tpu_custom_call" | custom-call | tf_op jit(solution)/shard_map/pallas_call | solution.py:1101
  18.5 1.5 %shard_map.85 = (f32[19,2,56,256]{3,2,1,0:T(8,128)S(1)}, f32[4,2,40,256]{3,2,1,0:T(8,128)S(1)}) custom-call(f32[47,8,128]{2,1,0:T(8,128)S(1)} %shard_map.73.entries, f32[4,2,32,256]{3,2,1,0:T(8,128)S(1)} %shard_map.83.sums, f32[4,2,8,256]{3,2,1,0:T(8,128)S(1)} %get-tuple-element.50.outer_sums, f32[19,2,8,256]{3,2,1,0:T(8,128)S(1)} %get-tuple-element.51.outer, ...), custom_call_target="tpu_custom_call" | custom-call | tf_op jit(solution)/shard_map/pallas_call | solution.py:1150
  20.0 1.5 %shard_map.87.refs_0_.middle = f32[19,2,56,256]{3,2,1,0:T(8,128)S(1)} custom-call(f32[47,8,128]{2,1,0:T(8,128)S(1)} %shard_map.73.entries, f32[19,2,56,256]{3,2,1,0:T(8,128)S(1)} %shard_map.82.ends, f32[19,2,56,256]{3,2,1,0:T(8,128)S(1)} %get-tuple-element.53.middle, f32[4,2,40,256]{3,2,1,0:T(8,128)S(1)} %get-tuple-element.56.solid), custom_call_target="tpu_custom_call" | custom-call | tf_op jit(solution)/shard_map/pallas_call | solution.py:1159
  21.5 1.1 %collective-permute-done.6.far.received = f32[176,256]{1,0:T(8,128)S(1)} collective-permute-done((f32[176,256]{1,0:T(8,128)S(1)}, f32[176,256]{1,0:T(8,128)S(1)}, u32[]{:S(2)}, u32[]{:S(2)}) %collective-permute-start.6) | collective-permute-done | bytes 180256 | tf_op jit(solution)/shard_map/ppermute | solution.py:1030
  23.2 0.9 %collective-permute-start.9 = (f32[160,256]{1,0:T(8,128)S(1)}, f32[160,256]{1,0:T(8,128)S(1)}, u32[]{:S(2)}, u32[]{:S(2)}) collective-permute-start(f32[160,256]{1,0:T(8,128)S(1)} %shard_map.88.refs_0_), channel_id=1, source_target_pairs={{0,28},{4,8},{8,4},{12,16},{16,12},{20,24},{24,20},{28,0},{1,29},{... | collective-permute-start | bytes 491528 | tf_op jit(solution)/shard_map/ppermute | solution.py:1030
  24.0 0.6 %shard_map.89 = f32[160,256]{1,0:T(8,128)S(1)} custom-call(f32[47,8,128]{2,1,0:T(8,128)S(1)} %shard_map.73.entries, f32[19,2,56,256]{3,2,1,0:T(8,128)S(1)} %shard_map.82.ends, f32[19,2,56,256]{3,2,1,0:T(8,128)S(1)} %get-tuple-element.53.middle, f32[4,1,40,256]{3,2,1,0:T(8,128)S(1)} %get-tuple-element.49.solid_near.after.solid, ...), custom_call_target="tpu_custom_call" | custom-call | tf_op jit(solution)/shard_map/pallas_call | solution.py:1164
  24.7 1.4 %shard_map.86.ends = f32[19,2,56,256]{3,2,1,0:T(8,128)S(1)} custom-call(f32[47,8,128]{2,1,0:T(8,128)S(1)} %shard_map.73.entries, f32[19,2,56,256]{3,2,1,0:T(8,128)S(1)} %shard_map.82.ends, f32[19,2,56,256]{3,2,1,0:T(8,128)S(1)} %get-tuple-element.53.middle, f32[4,1,40,256]{3,2,1,0:T(8,128)S(1)} %get-tuple-element.48.refs_0_.solid_far.solid, ...), custom_call_target="tpu_custom_call" | custom-call | tf_op jit(solution)/shard_map/pallas_call | solution.py:1176
  26.1 1.5 %shard_map.91.given = f32[19,4,32,256]{3,2,1,0:T(8,128)} custom-call(f32[19,2,56,256]{3,2,1,0:T(8,128)S(1)} %shard_map.86.ends, f32[19,2,56,256]{3,2,1,0:T(8,128)S(1)} %shard_map.87.refs_0_.middle), custom_call_target="tpu_custom_call" | custom-call | tf_op jit(solution)/shard_map/pallas_call | solution.py:1179
  27.6 2.2 %collective-permute-done.9.received = f32[160,256]{1,0:T(8,128)S(1)} collective-permute-done((f32[160,256]{1,0:T(8,128)S(1)}, f32[160,256]{1,0:T(8,128)S(1)}, u32[]{:S(2)}, u32[]{:S(2)}) %collective-permute-start.9) | collective-permute-done | bytes 163872 | tf_op jit(solution)/shard_map/ppermute | solution.py:1030
  29.8 0.8 %shard_map.92 = f32[19,4,32,256]{3,2,1,0:T(8,128)} custom-call(f32[19,2,56,256]{3,2,1,0:T(8,128)S(1)} %shard_map.86.ends, f32[160,256]{1,0:T(8,128)S(1)} %collective-permute-done.8.received, f32[5,32,256]{2,1,0:T(8,128)S(1)} %shard_map.90.far, f32[19,4,32,256]{3,2,1,0:T(8,128)} %shard_map.91.given), custom_call_target="tpu_custom_call", output_to_operand_aliasing={{}: (3, {})} | custom-call | tf_op jit(solution)/shard_map/pallas_call | solution.py:1189
  (20 shorter events, 1.5 us)
Async XLA Ops:
  0.0 5.1 %copy-start.1 = (f32[19]{0:T(128)S(1)}, f32[19]{0:T(128)}, u32[]{:S(2)}) copy-start(f32[19]{0:T(128)} %rates.1) | copy-start | bytes 232
  0.0 11.4 %copy-start = (f32[19,4,32,256]{3,2,1,0:T(8,128)S(1)}, f32[19,4,32,256]{3,2,1,0:T(8,128)}, u32[]{:S(2)}) copy-start(f32[19,4,32,256]{3,2,1,0:T(8,128)} %populations.5) | copy-start | bytes 7471108
  1.7 5.3 %collective-permute-start = (f32[8,128]{1,0:T(8,128)S(1)}, f32[8,128]{1,0:T(8,128)S(1)}, u32[]{:S(2)}, u32[]{:S(2)}) collective-permute-start(f32[8,128]{1,0:T(8,128)S(1)} %get-tuple-element.32), channel_id=1, source_target_pairs={{0,28},{4,8},{8,4},{12,16},{16,12},{20,24},{24,20},{28,0},{1,29},{... | collective-permute-start | bytes 12296 | tf_op jit(solution)/shard_map/ppermute | solution.py:1030
  5.1 1.9 %collective-permute-start.1 = (f32[8,128]{1,0:T(8,128)S(1)}, f32[8,128]{1,0:T(8,128)S(1)}, u32[]{:S(2)}, u32[]{:S(2)}) collective-permute-start(f32[8,128]{1,0:T(8,128)S(1)} %get-tuple-element.33), channel_id=1, source_target_pairs={{0,4},{4,0},{8,12},{12,8},{16,20},{20,16},{24,28},{28,24},{1,5},{5... | collective-permute-start | bytes 12296 | tf_op jit(solution)/shard_map/ppermute | solution.py:1030
  6.4 6.1 %collective-permute-start.5 = (f32[160,256]{1,0:T(8,128)S(1)}, f32[160,256]{1,0:T(8,128)S(1)}, u32[]{:S(2)}, u32[]{:S(2)}) collective-permute-start(f32[160,256]{1,0:T(8,128)S(1)} %get-tuple-element.40), channel_id=1, source_target_pairs={{0,4},{1,2},{2,1},{3,7},{4,0},{5,6},{6,5},{7,3},{8,12},{9,10},{10,... | collective-permute-start | bytes 491528 | tf_op jit(solution)/shard_map/ppermute | solution.py:1041
  7.0 7.4 %collective-permute-start.2 = (f32[160,256]{1,0:T(8,128)S(1)}, f32[160,256]{1,0:T(8,128)S(1)}, u32[]{:S(2)}, u32[]{:S(2)}) collective-permute-start(f32[160,256]{1,0:T(8,128)S(1)} %get-tuple-element.39), channel_id=1, source_target_pairs={{0,1},{1,0},{2,3},{3,2},{4,5},{5,4},{6,7},{7,6},{8,9},{9,8},{10,11... | collective-permute-start | bytes 491528 | tf_op jit(solution)/shard_map/ppermute | solution.py:1041
  9.7 4.6 %collective-permute-start.4 = (f32[8,128]{1,0:T(8,128)S(1)}, f32[8,128]{1,0:T(8,128)S(1)}, u32[]{:S(2)}, u32[]{:S(2)}) collective-permute-start(f32[8,128]{1,0:T(8,128)S(1)} %get-tuple-element.38.refs_0_), channel_id=1, source_target_pairs={{0,2},{1,3},{2,0},{3,1},{4,6},{5,7},{6,4},{7,5},{8,10},{9,11},{10,... | collective-permute-start | bytes 12296 | tf_op jit(solution)/shard_map/ppermute | solution.py:1022
  11.4 2.9 %collective-permute-start.3 = (f32[8,128]{1,0:T(8,128)S(1)}, f32[8,128]{1,0:T(8,128)S(1)}, u32[]{:S(2)}, u32[]{:S(2)}) collective-permute-start(f32[8,128]{1,0:T(8,128)S(1)} %get-tuple-element.38.refs_0_), channel_id=1, source_target_pairs={{0,4},{1,2},{2,1},{3,7},{4,0},{5,6},{6,5},{7,3},{8,12},{9,10},{10,... | collective-permute-start | bytes 12296 | tf_op jit(solution)/shard_map/ppermute | solution.py:1041
  15.1 7.5 %collective-permute-start.6 = (f32[176,256]{1,0:T(8,128)S(1)}, f32[176,256]{1,0:T(8,128)S(1)}, u32[]{:S(2)}, u32[]{:S(2)}) collective-permute-start(f32[176,256]{1,0:T(8,128)S(1)} %get-tuple-element.54), channel_id=1, source_target_pairs={{0,28},{4,8},{8,4},{12,16},{16,12},{20,24},{24,20},{28,0},{1,29},{... | collective-permute-start | bytes 540680 | tf_op jit(solution)/shard_map/ppermute | solution.py:1030
  16.4 7.6 %collective-permute-start.7 = (f32[176,256]{1,0:T(8,128)S(1)}, f32[176,256]{1,0:T(8,128)S(1)}, u32[]{:S(2)}, u32[]{:S(2)}) collective-permute-start(f32[176,256]{1,0:T(8,128)S(1)} %get-tuple-element.55), channel_id=1, source_target_pairs={{0,4},{4,0},{8,12},{12,8},{16,20},{20,16},{24,28},{28,24},{1,5},{5... | collective-permute-start | bytes 540680 | tf_op jit(solution)/shard_map/ppermute | solution.py:1030
  23.2 6.6 %collective-permute-start.9 = (f32[160,256]{1,0:T(8,128)S(1)}, f32[160,256]{1,0:T(8,128)S(1)}, u32[]{:S(2)}, u32[]{:S(2)}) collective-permute-start(f32[160,256]{1,0:T(8,128)S(1)} %shard_map.88.refs_0_), channel_id=1, source_target_pairs={{0,28},{4,8},{8,4},{12,16},{16,12},{20,24},{24,20},{28,0},{1,29},{... | collective-permute-start | bytes 491528 | tf_op jit(solution)/shard_map/ppermute | solution.py:1030
  24.6 5.2 %collective-permute-start.8 = (f32[160,256]{1,0:T(8,128)S(1)}, f32[160,256]{1,0:T(8,128)S(1)}, u32[]{:S(2)}, u32[]{:S(2)}) collective-permute-start(f32[160,256]{1,0:T(8,128)S(1)} %shard_map.89), channel_id=1, source_target_pairs={{0,4},{4,0},{8,12},{12,8},{16,20},{20,16},{24,28},{28,24},{1,5},{5... | collective-permute-start | bytes 491528 | tf_op jit(solution)/shard_map/ppermute | solution.py:1030
